TPU v7x, 32 devices: a whole 2x2x4 slice. The times are simulated.
32 devices in a mesh: dp: 16 (over z, y, x), tensor: 2 (over core).
Axes of the slice: x: 2, y: 2, z: 4, core: 2. Of those that a mesh axis runs over, the one named last changes fastest.
Arguments:
- inputs: bfloat16 [64, 1024, 512], P('dp', 'tensor'), may hold values from -6 to 6
- initial_state: float32 [64, 1024], P('dp', 'tensor'), may hold values from -6 to 6
- first_gain: float32 [512], replicated, may hold values from 0.1 to 1.9
- causal_filter: float32 [4, 512], replicated, may hold values from -3 to 3
- mixer_weight: bfloat16 [512, 2, 1024], P(None, None, 'tensor'), may hold values from -0.25 to 0.25
- gate_bias: float32 [1024], P('tensor'), may hold values from -6 to 2
- readout_weight: bfloat16 [1024, 512], P('tensor'), may hold values from -0.1875 to 0.1875
- second_gain: float32 [512], replicated, may hold values from 0.1 to 1.9
- up_weight: bfloat16 [512, 2048], P(None, 'tensor'), may hold values from -0.25 to 0.25
- up_bias: float32 [2048], P('tensor'), may hold values from -3 to 3
- down_weight: bfloat16 [2048, 512], P('tensor'), may hold values from -0.1875 to 0.1875
- cotangent: bfloat16 [64, 1024, 512], P('dp', 'tensor'), may hold values from -6 to 6
Outputs:
- block_output: bfloat16 [64, 1024, 512], P('dp', 'tensor')
- input_gradient: bfloat16 [64, 1024, 512], P('dp', 'tensor')
- state_gradient: float32 [64, 1024], P('dp', 'tensor')
- first_gain_gradient: float32 [512], replicated
- filter_gradient: float32 [4, 512], replicated
- mixer_gradient: float32 [512, 2, 1024], P(None, None, 'tensor')
- gate_bias_gradient: float32 [1024], P('tensor')
- readout_gradient: float32 [1024, 512], P('tensor')
- second_gain_gradient: float32 [512], replicated
- up_weight_gradient: float32 [512, 2048], P(None, 'tensor')
- up_bias_gradient: float32 [2048], P('tensor')
- down_weight_gradient: float32 [2048, 512], P('tensor')
All inputs are finite; a program needn't handle non-finite values.
Results may differ from a plain program's by a relative error of at most 0.0075.
Values may be sent and summed in bfloat16 or wider, within the bound.
No kernel may reach another device: no remote copies, remote signals or barrier semaphores. Data moves between devices by JAX's collectives and lax.ppermute only.
A program may use at most 256 MiB of HBM per device.

v0:
```python
import functools
import math

import jax
import jax.numpy as jnp
from jax import lax
from jax.experimental import pallas as pl
from jax.experimental.pallas import tpu as pltpu
from jax.sharding import PartitionSpec as P

epsilon = 1e-06
low = jnp.bfloat16
wide = jnp.float32
root = math.sqrt(2.0 / math.pi)
cubic = 0.044715
MIB = 1 << 20


def mm(left, right):
    return lax.dot_general(left, right, (((1,), (0,)), ((), ())), preferred_element_type=wide)


def mm_nt(left, right):
    return lax.dot_general(left, right, (((1,), (1,)), ((), ())), preferred_element_type=wide)


def mm_tn(left, right):
    return lax.dot_general(left, right, (((0,), (0,)), ((), ())), preferred_element_type=wide)


def params(mib, grid):
    return pltpu.CompilerParams(
        vmem_limit_bytes=mib * MIB, dimension_semantics=("arbitrary",) * grid
    )


def cost(macs, moved, curves=0):
    return pl.CostEstimate(flops=2 * macs, bytes_accessed=moved, transcendentals=curves)


def whole(array):
    rank = array.ndim
    return pl.BlockSpec(array.shape, lambda *_: (0,) * rank, pipeline_mode=pl.Buffered(1))


def stream_order(rows, inverse):
    at = lax.broadcasted_iota(jnp.int32, (rows, rows), 1 if inverse else 0)
    source = lax.broadcasted_iota(jnp.int32, (rows, rows), 0 if inverse else 1)
    moved = jnp.bitwise_and(at, 7) * (rows // 8) + lax.shift_right_logical(at, 3)
    return jnp.where(source == moved, 1.0, 0.0).astype(low)


def forward_kernel(
    core, own, got, gain, taps, mixer_own, mixer_other, bias_own, bias_other, start_own, start_other,
    read_own, read_other,
    gain_two, filtered_out, decay_out, differ_out, cand_out, state_out, middle_out, normed_out,
    order, back_order, streams, rim, tail, gates, cands, carry,
):
    half_chunks = pl.num_programs(1) // 2
    step = pl.program_id(1)
    rows = own.shape[1]
    width = own.shape[2]
    count = rows // 8
    tap_count = taps.shape[0]
    edge = 8 * (tap_count - 1)
    channels = read_own.shape[0]
    mine = step // half_chunks == core[0]

    @pl.when((step == 0) & (pl.program_id(0) == 0))
    def _():
        order[...] = stream_order(rows, False)
        back_order[...] = stream_order(rows, True)

    x = mm(order[...], jnp.where(mine, own[0], got[0]))
    streams[...] = x
    scale = lax.rsqrt(jnp.mean(x * x, axis=-1, keepdims=True) + epsilon)
    normed = x * scale * gain[...]

    @pl.when(step == 0)
    def _():
        tail[...] = jnp.zeros_like(tail)
        for at, start in enumerate((start_own, start_other)):
            carry[:, at * channels : (at + 1) * channels] = jnp.broadcast_to(start[0], (8, channels))

    rim[edge:, :] = normed
    first = lax.broadcasted_iota(jnp.int32, (8, width), 0) == 0
    for at in range(0, edge, 8):
        ends = normed[rows - edge + at : rows - edge + at + 8, :]
        rim[at : at + 8, :] = jnp.where(
            first, pltpu.roll(tail[at : at + 8, :], 1, 0), pltpu.roll(ends, 1, 0)
        )
        tail[at : at + 8, :] = ends
    total = taps[0:1, :] * rim[0:rows, :]
    for tap in range(1, tap_count):
        total = total + taps[tap : tap + 1, :] * rim[8 * tap : 8 * tap + rows, :]
    filtered = total.astype(low)
    filtered_out[...] = filtered
    for at, (weight, bias) in enumerate(((mixer_own, bias_own), (mixer_other, bias_other))):
        lanes = slice(at * channels, (at + 1) * channels)
        gates[:, lanes] = mm(filtered, weight[:, :channels]) + bias[...]
        cands[:, lanes] = mm(filtered, weight[:, channels:])

    group = min(2 * channels, 1024)
    place = lax.broadcasted_iota(jnp.int32, (8, group), 0)
    for lane in range(0, 2 * channels, group):
        lanes = slice(lane, lane + group)

        def open_gates(index, state):
            factor, offset = state
            base = pl.multiple_of(index * 16, 16)
            kept = []
            for sub in (0, 8):
                c = cands[pl.ds(base + sub, 8), lanes]
                decay = jax.nn.sigmoid(-gates[pl.ds(base + sub, 8), lanes])
                soft = jnp.maximum(c, jnp.log(1.0 + jnp.exp(jnp.minimum(c, 60.0))))
                decay_out[pl.ds(base + sub, 8), lanes] = decay
                gates[pl.ds(base + sub, 8), lanes] = soft
                factor = factor * decay
                offset = soft + decay * (offset - soft)
                kept.append(c)
            cand_out[pl.ds(base, 16), lanes] = jnp.concatenate(kept, axis=0).astype(low)
            return factor, offset

        factor, offset = lax.fori_loop(
            0,
            count // 2,
            open_gates,
            (jnp.ones((8, group), wide), jnp.zeros((8, group), wide)),
            unroll=True,
        )
        for hop in (1, 2, 4):
            inside = place >= hop
            offset = factor * jnp.where(inside, pltpu.roll(offset, hop, 0), 0.0) + offset
            factor = factor * jnp.where(inside, pltpu.roll(factor, hop, 0), 1.0)
        entered = carry[:, lanes]
        leaving = factor * entered + offset
        carry[:, lanes] = jnp.broadcast_to(leaving[7:8, :], leaving.shape)
        entered = jnp.where(place >= 1, pltpu.roll(leaving, 1, 0), entered)

        def run_states(index, state):
            base = pl.multiple_of(index * 16, 16)
            held, differ = [], []
            for sub in (0, 8):
                soft = gates[pl.ds(base + sub, 8), lanes]
                differ.append(soft - state)
                state = soft - decay_out[pl.ds(base + sub, 8), lanes] * differ[-1]
                held.append(state)
            differ_out[pl.ds(base, 16), lanes] = jnp.concatenate(differ, axis=0).astype(low)
            state_out[pl.ds(base, 16), lanes] = jnp.concatenate(held, axis=0).astype(low)
            return state

        lax.fori_loop(0, count // 2, run_states, entered, unroll=True)

    mixed = mm(state_out[:, :channels], read_own[...]) + mm(
        state_out[:, channels:], read_other[...]
    )
    middle = streams[...] + mixed
    middle_out[...] = middle
    scale_two = lax.rsqrt(jnp.mean(middle * middle, axis=-1, keepdims=True) + epsilon)
    normed_out[...] = (middle * scale_two * gain_two[...]).astype(low)


def halves_specs(chunk, width, windows, halves):
    return (
        pl.BlockSpec(
            (1, chunk, width), lambda w, t, core: (windows * core[0] + w, t % halves, 0)
        ),
        pl.BlockSpec((1, chunk, width), lambda w, t, core: (w, t % halves, 0)),
    )


def forward(core, inputs, got, gain, taps, mixers, biases, starts, reads, gain_two):
    windows, half, width = got.shape
    channels = reads[0].shape[0]
    chunk = math.gcd(half, 512)
    halves = half // chunk
    steps = 2 * halves
    rows = 2 * half * windows
    row = lambda lanes: pl.BlockSpec((chunk, lanes), lambda w, t, core: (w * steps + t, 0))
    out = lambda lanes, dtype: jax.ShapeDtypeStruct((rows, lanes), dtype)
    return pl.pallas_call(
        forward_kernel,
        grid_spec=pltpu.PrefetchScalarGridSpec(
            num_scalar_prefetch=1,
            grid=(windows, steps),
            in_specs=[
                *halves_specs(chunk, width, windows, halves),
                whole(gain),
                whole(taps),
                whole(mixers[0]),
                whole(mixers[1]),
                whole(biases[0]),
                whole(biases[1]),
                *[
                    pl.BlockSpec((1, 1, channels), lambda w, t, core: (windows * core[0] + w, 0, 0))
                    for _ in starts
                ],
                whole(reads[0]),
                whole(reads[1]),
                whole(gain_two),
            ],
            out_specs=[
                row(width),
                row(2 * channels),
                row(2 * channels),
                row(2 * channels),
                row(2 * channels),
                row(width),
                row(width),
                pl.BlockSpec((chunk, chunk), lambda w, t, core: (0, 0)),
                pl.BlockSpec((chunk, chunk), lambda w, t, core: (0, 0)),
            ],
            scratch_shapes=[
                pltpu.VMEM((chunk, width), wide),
                pltpu.VMEM((chunk + 8 * (taps.shape[0] - 1), width), wide),
                pltpu.VMEM((8 * (taps.shape[0] - 1), width), wide),
                pltpu.VMEM((chunk, 2 * channels), wide),
                pltpu.VMEM((chunk, 2 * channels), wide),
                pltpu.VMEM((8, 2 * channels), wide),
            ],
        ),
        out_shape=[
            out(width, low),
            out(2 * channels, wide),
            out(2 * channels, low),
            out(2 * channels, low),
            out(2 * channels, low),
            out(width, wide),
            out(width, low),
            jax.ShapeDtypeStruct((chunk, chunk), low),
            jax.ShapeDtypeStruct((chunk, chunk), low),
        ],
        compiler_params=params(60, 2),
        cost_estimate=cost(rows * width * channels * 6, rows * channels * 24, rows * channels * 8),
        name="forward_mixer",
    )(core, inputs, got, gain, taps, *mixers, *biases, *starts, *reads, gain_two)


def feed(core, cotangent, got, order, tangent, normed, up, bias, down, dtype):
    windows, half, width = got.shape
    units = up.shape[1]
    rows = normed.shape[0]
    chunk = order.shape[0]
    block = min(units, 512)
    fresh = tangent is None

    def kernel(core, *refs):
        if fresh:
            own, came, order_in, *refs, tangent_in = refs
        else:
            tangent_in, *refs = refs
        normed_in, up_in, bias_in, down_in, active_out, back_out, bias_out, grad_out = refs

        if fresh:

            @pl.when(pl.program_id(0) == 0)
            def _():
                for window in range(windows):
                    for side in range(2):
                        mine = core[0] == side
                        for at in range(0, half, chunk):
                            rows_at = slice(at, at + chunk)
                            to = (2 * window + side) * half + at
                            tangent_in[to : to + chunk, :] = mm(
                                order_in[...],
                                jnp.where(mine, own[window, rows_at, :], came[window, rows_at, :]),
                            ).astype(low)

        sums = [jnp.zeros((8, block), wide), 0.0, 0.0]
        for at in range(0, rows, chunk):
            rows_at = slice(at, at + chunk)
            v = mm(normed_in[rows_at, :], up_in[...]) + bias_in[...]
            back = mm_nt(tangent_in[rows_at, :], down_in[...])
            square = v * v
            s = jax.nn.sigmoid(v * (2.0 * root + (2.0 * root * cubic) * square))
            active = v * s
            slope = s + (active * (1.0 - s)) * (2.0 * root + (6.0 * root * cubic) * square)
            back = back * slope
            for row in range(0, chunk, 8):
                sums[0] = sums[0] + back[row : row + 8, :]
            active_low, back_low = active.astype(low), back.astype(low)
            active_out[rows_at, :] = active_low
            back_out[rows_at, :] = back_low
            sums[1] = sums[1] + mm_tn(tangent_in[rows_at, :], active_low)
            sums[2] = sums[2] + mm_tn(normed_in[rows_at, :], back_low)
        bias_out[...] = sums[0]
        grad_out[0:width, :] = sums[1].astype(dtype)
        grad_out[width:, :] = sums[2].astype(dtype)

    lanes = lambda count: pl.BlockSpec((count, block), lambda j, core: (0, j))
    in_specs = [whole(normed), lanes(width), lanes(1), pl.BlockSpec((block, width), lambda j, core: (j, 0))]
    arrays = [normed, up, bias, down]
    out_specs = [lanes(rows), lanes(rows), lanes(8), lanes(2 * width)]
    out_shape = [
        jax.ShapeDtypeStruct((rows, units), low),
        jax.ShapeDtypeStruct((rows, units), low),
        jax.ShapeDtypeStruct((8, units), wide),
        jax.ShapeDtypeStruct((2 * width, units), dtype),
    ]
    if fresh:
        in_specs = [
            pl.BlockSpec((windows, half, width), lambda j, core: (core[0], 0, 0)),
            whole(got),
            whole(order),
        ] + in_specs
        arrays = [cotangent, got, order] + arrays
        out_specs.append(pl.BlockSpec((rows, width), lambda j, core: (0, 0)))
        out_shape.append(jax.ShapeDtypeStruct((rows, width), low))
    else:
        in_specs.insert(0, whole(tangent))
        arrays.insert(0, tangent)
    return pl.pallas_call(
        kernel,
        grid_spec=pltpu.PrefetchScalarGridSpec(
            num_scalar_prefetch=1, grid=(units // block,), in_specs=in_specs, out_specs=out_specs
        ),
        out_shape=out_shape,
        compiler_params=params(60, 1),
        cost_estimate=cost(rows * width * units * 4, rows * units * 4, rows * units),
        name="feed_forward",
    )(core, *arrays)


def norm_kernel(
    tangent, back_own, back_other, middle_in, up_own, up_other, gain_two, middle_out, mixed_out, gain_out
):
    @pl.when(pl.program_id(0) == 0)
    def _():
        gain_out[...] = jnp.zeros_like(gain_out)

    rows = tangent.shape[0]
    part = math.gcd(rows, 256)
    for begin in range(0, rows, part):
        at = slice(begin, begin + part)
        back = mm_nt(back_own[at, :], up_own[...]) + mm_nt(back_other[at, :], up_other[...])
        middle = middle_in[at, :]
        scale = lax.rsqrt(jnp.mean(middle * middle, axis=-1, keepdims=True) + epsilon)
        gain_out[...] += jnp.sum(back * (middle * scale), axis=0, keepdims=True)
        weighted = gain_two[...] * back
        inner = jnp.mean(weighted * middle, axis=-1, keepdims=True)
        back_middle = (
            tangent[at, :].astype(wide) + scale * weighted - middle * (scale * scale * scale * inner)
        )
        middle_out[at, :] = back_middle
        mixed_out[at, :] = back_middle.astype(low)


def norm_back(tangent, backs, middle, ups, gain_two):
    rows, width = tangent.shape
    units = ups[0].shape[1]
    chunk = math.gcd(rows, 512)
    row = lambda lanes: pl.BlockSpec((chunk, lanes), lambda t: (t, 0))
    return pl.pallas_call(
        norm_kernel,
        grid=(rows // chunk,),
        in_specs=[
            row(width),
            row(units),
            row(units),
            row(width),
            whole(ups[0]),
            whole(ups[1]),
            whole(gain_two),
        ],
        out_specs=[row(width), row(width), pl.BlockSpec((1, width), lambda t: (0, 0))],
        out_shape=[
            jax.ShapeDtypeStruct((rows, width), wide),
            jax.ShapeDtypeStruct((rows, width), low),
            jax.ShapeDtypeStruct((1, width), wide),
        ],
        compiler_params=params(60, 1),
        cost_estimate=cost(rows * width * 2 * units, rows * (units * 4 + width * 16)),
        name="norm_back",
    )(tangent, *backs, middle, *ups, gain_two)


def scan_kernel(
    windows, chunk, mixed, filtered, read, decay_in, differ_in, cand_in, state_in,
    gate_out, cand_out, state_out, bias_out, grad_out, states,
):
    rows, width = mixed.shape
    group = read.shape[0]
    count = chunk // 16
    chunks = rows // chunk
    each = chunks // windows
    place = lax.broadcasted_iota(jnp.int32, (8, group), 0)
    states[...] = mm_nt(mixed[...], read[...])
    factors = [jnp.ones((8, group), wide)] * chunks
    offsets = [jnp.zeros((8, group), wide)] * chunks
    for index in range(2 * count - 1, -1, -1):
        for at in range(chunks):
            here = slice(at * chunk + 8 * index, at * chunk + 8 * index + 8)
            decay = decay_in[here, :]
            factors[at] = factors[at] * decay
            offsets[at] = decay * (offsets[at] + states[here, :])
    later = [None] * chunks
    for window in range(windows):
        entered = jnp.zeros((8, group), wide)
        for at in range(window * each + each - 1, window * each - 1, -1):
            factor, offset = factors[at], offsets[at]
            for hop in (1, 2, 4):
                inside = place < 8 - hop
                offset = factor * jnp.where(inside, pltpu.roll(offset, 8 - hop, 0), 0.0) + offset
                factor = factor * jnp.where(inside, pltpu.roll(factor, 8 - hop, 0), 1.0)
            leaving = factor * entered + offset
            later[at] = jnp.where(place < 7, pltpu.roll(leaving, 7, 0), entered)
            entered = jnp.broadcast_to(leaving[0:1, :], leaving.shape)
        state_out[window] = entered[0:1, :]
    bias = [jnp.zeros((8, group), wide)] * chunks
    for index in range(count - 1, -1, -1):
        for at in range(chunks):
            base = at * chunk + 16 * index
            both = slice(base, base + 16)
            differ = differ_in[both, :].astype(wide)
            chosen = jax.nn.sigmoid(cand_in[both, :].astype(wide))
            gate, cand = [None] * 2, [None] * 2
            for half in (1, 0):
                near = slice(8 * half, 8 * half + 8)
                here = slice(base + 8 * half, base + 8 * half + 8)
                decay = decay_in[here, :]
                carried = states[here, :] + later[at]
                later[at] = decay * carried
                opened = carried - later[at]
                gate[half] = decay * opened * differ[near]
                cand[half] = opened * chosen[near]
                bias[at] = bias[at] + gate[half]
            gate_out[both, :] = jnp.concatenate(gate, axis=0).astype(low)
            cand_out[both, :] = jnp.concatenate(cand, axis=0).astype(low)
    bias_out[...] = sum(bias[1:], bias[0])
    grad_out[2 * width :, :] = mm_tn(mixed[...], state_in[...]).astype(grad_out.dtype)
    grad_out[0:width, :] = mm_tn(filtered[...], gate_out[...]).astype(grad_out.dtype)
    grad_out[width : 2 * width, :] = mm_tn(filtered[...], cand_out[...]).astype(grad_out.dtype)


def scan_back(windows, chunk, side, mixed, filtered, read, decay, differ, cand, states, dtype):
    rows, width = mixed.shape
    channels = read.shape[0]
    block = min(channels, 256)
    count = channels // block
    lanes = lambda size: pl.BlockSpec((size, block), lambda j: (0, j))
    half = pl.BlockSpec((rows, block), lambda j: (0, side * count + j))
    out = jax.ShapeDtypeStruct((rows, channels), low)
    return pl.pallas_call(
        functools.partial(scan_kernel, windows, chunk),
        grid=(count,),
        in_specs=[
            whole(mixed),
            whole(filtered),
            pl.BlockSpec((block, width), lambda j: (j, 0)),
            half,
            half,
            half,
            half,
        ],
        out_specs=[
            lanes(rows),
            lanes(rows),
            pl.BlockSpec((windows, 1, block), lambda j: (0, 0, j)),
            lanes(8),
            lanes(3 * width),
        ],
        out_shape=[
            out,
            out,
            jax.ShapeDtypeStruct((windows, 1, channels), wide),
            jax.ShapeDtypeStruct((8, channels), wide),
            jax.ShapeDtypeStruct((3 * width, channels), dtype),
        ],
        scratch_shapes=[pltpu.VMEM((rows, block), wide)],
        compiler_params=params(60, 1),
        cost_estimate=cost(rows * width * 4 * channels, rows * channels * 14, rows * channels),
        name="scan_back",
    )(mixed, filtered, read, decay, differ, cand, states)


def entry_kernel(
    core, own, got, order, back_order, gate_own, cand_own, gate_other, cand_other, middle_in, mixer_own,
    mixer_other, gain, taps, mine_out, sent_out, gain_out, taps_out, rim, head,
):
    step = pl.program_id(1)
    steps = pl.num_programs(1)
    half_chunks = steps // 2
    position = steps - 1 - step
    rows, width = own.shape[1:]
    tap_count = taps.shape[0]
    edge = 8 * (tap_count - 1)
    channels = gate_own.shape[1]

    @pl.when((step == 0) & (pl.program_id(0) == 0))
    def _():
        gain_out[...] = jnp.zeros_like(gain_out)
        taps_out[...] = jnp.zeros_like(taps_out)

    @pl.when(step == 0)
    def _():
        head[...] = jnp.zeros_like(head)

    rim[0:rows, :] = (
        mm_nt(gate_own[...], mixer_own[:, :channels])
        + mm_nt(cand_own[...], mixer_own[:, channels:])
        + mm_nt(gate_other[...], mixer_other[:, :channels])
        + mm_nt(cand_other[...], mixer_other[:, channels:])
    )
    last = lax.broadcasted_iota(jnp.int32, (8, width), 0) == 7
    for at in range(0, edge, 8):
        begins = rim[at : at + 8, :]
        rim[rows + at : rows + at + 8, :] = jnp.where(
            last, pltpu.roll(head[at : at + 8, :], 7, 0), pltpu.roll(begins, 7, 0)
        )
        head[at : at + 8, :] = begins
    x = mm(order[...], jnp.where(position // half_chunks == core[0], own[0], got[0]))
    scale = lax.rsqrt(jnp.mean(x * x, axis=-1, keepdims=True) + epsilon)
    unit = x * scale
    normed = unit * gain[...]
    back = jnp.zeros((rows, width), wide)
    for tap in range(tap_count):
        begin = 8 * (tap_count - 1 - tap)
        ahead = rim[begin : begin + rows, :]
        back = back + taps[tap : tap + 1, :] * ahead
        taps_out[tap : tap + 1, :] += jnp.sum(ahead * normed, axis=0, keepdims=True)
    gain_out[...] += jnp.sum(back * unit, axis=0, keepdims=True)
    weighted = gain[...] * back
    inner = jnp.mean(weighted * x, axis=-1, keepdims=True)
    gradient = middle_in[...] + scale * weighted - x * (scale * scale * scale * inner)
    gradient = mm(back_order[...], gradient.astype(low)).astype(low)
    give(gradient, position, half_chunks, core, mine_out, sent_out)


def give(values, position, half_chunks, core, mine_out, sent_out):
    rows = values.shape[0]
    at = pl.ds(pl.multiple_of(position % half_chunks * rows, rows), rows)
    mine = position // half_chunks == core[0]

    @pl.when(mine)
    def _():
        mine_out[0, at, :] = values

    @pl.when(jnp.logical_not(mine))
    def _():
        sent_out[0, at, :] = values


def side_specs(windows, half, width):
    block = (1, half, width)
    return (
        [
            pl.BlockSpec(block, lambda w, t, core: (windows * core[0] + w, 0, 0)),
            pl.BlockSpec(block, lambda w, t, core: (w, 0, 0)),
        ],
        [
            jax.ShapeDtypeStruct((2 * windows, half, width), low),
            jax.ShapeDtypeStruct((windows, half, width), low),
        ],
    )


def entry(core, inputs, got, orders, projects, back_middle, mixers, gain, taps):
    windows, half, width = got.shape
    chunk = math.gcd(half, 512)
    halves = half // chunk
    steps = 2 * halves
    rows = 2 * half * windows
    row = lambda lanes: pl.BlockSpec(
        (chunk, lanes), lambda w, t, core: (w * steps + steps - 1 - t, 0)
    )
    specs, shapes = side_specs(windows, half, width)
    return pl.pallas_call(
        entry_kernel,
        grid_spec=pltpu.PrefetchScalarGridSpec(
            num_scalar_prefetch=1,
            grid=(windows, steps),
            in_specs=[
                pl.BlockSpec(
                    (1, chunk, width),
                    lambda w, t, core: (windows * core[0] + w, (steps - 1 - t) % halves, 0),
                ),
                pl.BlockSpec((1, chunk, width), lambda w, t, core: (w, (steps - 1 - t) % halves, 0)),
                whole(orders[0]),
                whole(orders[1]),
                *[row(array.shape[1]) for array in projects],
                row(width),
                whole(mixers[0]),
                whole(mixers[1]),
                whole(gain),
                whole(taps),
            ],
            out_specs=[
                *specs,
                pl.BlockSpec((1, width), lambda w, t, core: (0, 0)),
                pl.BlockSpec(taps.shape, lambda w, t, core: (0, 0)),
            ],
            scratch_shapes=[
                pltpu.VMEM((chunk + 8 * (taps.shape[0] - 1), width), wide),
                pltpu.VMEM((8 * (taps.shape[0] - 1), width), wide),
            ],
        ),
        out_shape=[
            *shapes,
            jax.ShapeDtypeStruct((1, width), wide),
            jax.ShapeDtypeStruct(taps.shape, wide),
        ],
        compiler_params=params(60, 2),
        cost_estimate=cost(
            rows * width * 2 * mixers[0].shape[1], rows * mixers[0].shape[1] * 6
        ),
        name="input_gradient",
    )(core, inputs, got, *orders, *projects, back_middle, *mixers, gain, taps)


def leave_kernel(
    core, back_order, active_own, active_other, middle, down_own, down_other, mine_out, sent_out
):
    total = middle[...] + mm(active_own[...], down_own[...]) + mm(active_other[...], down_other[...])
    total = mm(back_order[...], total.astype(low)).astype(low)
    give(total, pl.program_id(1), pl.num_programs(1) // 2, core, mine_out, sent_out)


def leave(windows, core, back_order, actives, middle, downs):
    rows, width = middle.shape
    length = rows // windows
    chunk = back_order.shape[0]
    steps = length // chunk
    row = lambda lanes: pl.BlockSpec((chunk, lanes), lambda w, t, core: (w * steps + t, 0))
    specs, shapes = side_specs(windows, length // 2, width)
    return pl.pallas_call(
        leave_kernel,
        grid_spec=pltpu.PrefetchScalarGridSpec(
            num_scalar_prefetch=1,
            grid=(windows, steps),
            in_specs=[
                whole(back_order),
                row(actives[0].shape[1]),
                row(actives[1].shape[1]),
                row(width),
                whole(downs[0]),
                whole(downs[1]),
            ],
            out_specs=specs,
        ),
        out_shape=shapes,
        compiler_params=params(60, 2),
        cost_estimate=cost(rows * width * 2 * downs[0].shape[0], rows * downs[0].shape[0] * 6),
        name="block_output",
    )(core, back_order, *actives, middle, *downs)


def pack_kernel(width, *refs):
    gains, taps, gain_two, gate_own, gate_other, up_own, up_other, mine_out, sent_out = refs
    for out, gate, up in ((mine_out, gate_own, up_own), (sent_out, gate_other, up_other)):
        out[...] = jnp.zeros_like(out)
        row = 0
        for part in (
            gains[...],
            taps[...],
            gain_two[...],
            jnp.sum(gate[...], axis=0, keepdims=True),
            jnp.sum(up[...], axis=0, keepdims=True),
        ):
            for lane in range(0, part.shape[1], width):
                out[row : row + part.shape[0], 0 : min(width, part.shape[1])] = part[:, lane : lane + width]
                row += part.shape[0]


def pack(width, gains, taps, *rest):
    arrays = [gains, taps, *rest]
    count = taps.shape[0] + 3 + -(-rest[-1].shape[1] // width)
    out = jax.ShapeDtypeStruct((-(-count // 8) * 8, width), wide)
    return pl.pallas_call(
        functools.partial(pack_kernel, width),
        out_shape=[out, out],
        compiler_params=params(60, 0),
        name="pack_short",
    )(*arrays)


def finish_feed_kernel(bit, piece, got, down_out, up_out):
    lead = bit[0] == 0
    a, b = piece[...].astype(wide), got[...].astype(wide)
    down_out[...] = jnp.where(lead, a, b).T
    up_out[...] = jnp.where(lead, b, a)


def finish_feed(bit, piece, got):
    width, units = piece.shape
    block = min(units, 512)
    half = pl.BlockSpec((width, block), lambda j, bit: (0, j))
    return pl.pallas_call(
        finish_feed_kernel,
        grid_spec=pltpu.PrefetchScalarGridSpec(
            num_scalar_prefetch=1,
            grid=(units // block,),
            in_specs=[half, half],
            out_specs=[pl.BlockSpec((block, width), lambda j, bit: (j, 0)), half],
        ),
        out_shape=[
            jax.ShapeDtypeStruct((units, width), wide),
            jax.ShapeDtypeStruct((width, units), wide),
        ],
        compiler_params=params(60, 1),
        name="finish_feed",
    )(bit, piece, got)


def finish_mixer_kernel(bit, piece, got, mixer_out, read_out):
    lead = bit[0] == 0
    width = mixer_out.shape[0]
    cut = piece.shape[0]
    a, b = piece[...].astype(wide), got[...].astype(wide)
    a, b = jnp.where(lead, a, b), jnp.where(lead, b, a)
    mixer_out[:, 0, :] = a[:width]
    mixer_out[0 : cut - width, 1, :] = a[width:]
    mixer_out[cut - width :, 1, :] = b[: 2 * width - cut]
    read_out[...] = b[2 * width - cut :].T


def finish_mixer(bit, piece, got):
    cut, channels = piece.shape
    width = 2 * cut // 3
    return pl.pallas_call(
        finish_mixer_kernel,
        grid_spec=pltpu.PrefetchScalarGridSpec(
            num_scalar_prefetch=1,
            grid=(1,),
            in_specs=[whole(piece), whole(got)],
            out_specs=[
                pl.BlockSpec((width, 2, channels), lambda j, bit: (0, 0, 0)),
                pl.BlockSpec((channels, width), lambda j, bit: (0, 0)),
            ],
        ),
        out_shape=[
            jax.ShapeDtypeStruct((width, 2, channels), wide),
            jax.ShapeDtypeStruct((channels, width), wide),
        ],
        compiler_params=params(60, 1),
        name="finish_mixer",
    )(bit, piece, got)


def partner(array):
    return lax.ppermute(array, "tensor", [(0, 1), (1, 0)])


def hold(*values):
    return lax.optimization_barrier(values)


class DpSum:
    def __init__(self, *terms):
        self.terms = terms
        self.piece = None
        count = lax.axis_size("dp").bit_length() - 1
        first = list(range(count))
        if count >= 2:
            groups = [((0,), (1,)), ((1,), (0,))] + [
                (tuple(first[at : at + 2]),) * 2 for at in range(2, count, 2)
            ]
        else:
            groups = [((bit,), (bit,)) for bit in first]
        self.todo = [(False, group) for group in groups] + [(True, group) for group in groups[::-1]]

    def place(self, group):
        index, core = lax.axis_index("dp"), lax.axis_index("tensor")
        return [
            jnp.where(core == 0, (index >> low_bit) & 1, (index >> high_bit) & 1)
            for low_bit, high_bit in zip(*group)
        ]

    def exchange(self, array, group, mask):
        sizes = (lax.axis_size("dp"), lax.axis_size("tensor"))
        flips = [
            sum(1 << bit for at, bit in enumerate(bits) if mask >> at & 1) for bits in group
        ]
        route = [
            (d * sizes[1] + c, (d ^ flips[c]) * sizes[1] + c)
            for d in range(sizes[0])
            for c in range(sizes[1])
        ]
        return lax.ppermute(array, ("dp", "tensor"), route)

    def prepare(self):
        join, group = self.todo[0]
        if join:
            if self.piece is None:
                self.piece = sum(term.astype(wide) for term in self.terms).astype(low)
            self.sends = [self.piece]
            return
        bits = self.place(group)
        self.spot = sum(bit << at for at, bit in enumerate(bits))
        count = 1 << len(bits)
        self.sends = [self.share(self.spot ^ mask, count).astype(low) for mask in range(1, count)]

    def share(self, spot, count):
        size = self.terms[0].shape[0] // count
        cuts = [lax.dynamic_slice_in_dim(term, spot * size, size) for term in self.terms]
        return sum(cut.astype(wide) for cut in cuts)

    def start(self):
        join, group = self.todo[0]
        count = 1 << len(group[0])
        sends = self.sends * (count - 1) if join else self.sends
        self.got = [
            self.exchange(array, group, mask) for array, mask in zip(sends, range(1, count))
        ]

    def finish(self):
        join, group = self.todo.pop(0)
        if not join:
            self.terms = [self.share(self.spot, 1 << len(group[0])), *self.got]
            return
        parts = [self.piece] + self.got
        for bit in self.place(group):
            parts = [
                jnp.where(
                    bit == 0,
                    jnp.concatenate([parts[at], parts[at + 1]]),
                    jnp.concatenate([parts[at + 1], parts[at]]),
                )
                for at in range(0, len(parts), 2)
            ]
        self.piece = parts[0]


    def begin(self, piece):
        self.sends = [piece]
        self.start()
        return self.got[0]

    def last(self):
        _, group = self.todo[0]
        (bit,) = self.place(group)
        return bit.reshape(1).astype(jnp.int32), self.piece, self.got[0]


class DpSmall(DpSum):
    def __init__(self, total):
        super().__init__(total)
        self.todo = [(join, (group[0], group[0])) for join, group in self.todo if not join]

    def prepare(self):
        self.sends = [self.terms[0]] * ((1 << len(self.todo[0][1][0])) - 1)

    def finish(self):
        _, group = self.todo.pop(0)
        parts = [self.terms[0], *self.got]
        while len(parts) > 1:
            parts = [parts[at] + parts[at + 1] for at in range(0, len(parts), 2)]
        self.terms = parts


def beside(chains, work, *leads, loose=()):
    chains = [chain for chain in chains if chain.todo]
    begun = [*chains, *(chain for chain in loose if chain.todo)]
    for chain in begun:
        chain.prepare()
    held = hold(*leads, *(send for chain in begun for send in chain.sends))
    leads, sends = held[: len(leads)], list(held[len(leads) :])
    for chain in begun:
        chain.sends, sends = sends[: len(chain.sends)], sends[len(chain.sends) :]
        chain.start()
    results = work(*leads)
    held = hold(*results, *(got for chain in chains for got in chain.got))
    results, gots = held[: len(results)], list(held[len(results) :])
    for chain in chains:
        chain.got, gots = gots[: len(chain.got)], gots[len(chain.got) :]
        chain.finish()
    return results


def local(
    inputs,
    initial_state,
    first_gain,
    causal_filter,
    mixer_weight,
    gate_bias,
    readout_weight,
    second_gain,
    up_weight,
    up_bias,
    down_weight,
    cotangent,
):
    sides = lax.axis_size("tensor")
    windows = inputs.shape[0] // sides
    half, width = inputs.shape[1:]
    channels = gate_bias.shape[0]
    units = up_bias.shape[0]
    core = lax.axis_index("tensor")
    core_at = core.reshape(1).astype(jnp.int32)

    def other_windows(array):
        return lax.dynamic_slice_in_dim(array, (1 - core) * windows, windows)

    mixer = mixer_weight.reshape(width, 2 * channels)
    mixers = (mixer, partner(mixer))
    got_inputs = partner(other_windows(inputs))
    reads = (readout_weight, partner(readout_weight))
    biases = (gate_bias[None], partner(gate_bias)[None])
    starts = (initial_state[:, None], partner(initial_state)[:, None])
    got_cotangent = partner(other_windows(cotangent))
    ups = (up_weight, partner(up_weight))
    up_biases = (up_bias[None], partner(up_bias)[None])
    downs = (down_weight, partner(down_weight))
    gain, gain_two = first_gain[None], second_gain[None]

    filtered, decay, differ, cand, states, middle, normed, *orders = forward(
        core_at, inputs, got_inputs, gain, causal_filter, mixers, biases, starts, reads, gain_two
    )
    chunk = orders[0].shape[0]
    active_other, back_other, bias_other, feed_other, tangent = feed(
        core_at, cotangent, got_cotangent, orders[0], None, normed, ups[1], up_biases[1], downs[1], low
    )
    tangent, feed_other = hold(tangent, feed_other)
    feed_got = partner(feed_other)
    active_own, back_own, bias_own, feed_own = feed(
        core_at, cotangent, got_cotangent, orders[0], tangent, normed, ups[0], up_biases[0], downs[0], wide
    )
    actives = [active_own, active_other]
    feed_own, feed_got = hold(feed_own, feed_got)
    feed_sum = DpSum(feed_own, feed_got)
    up_bias_own, up_bias_other = bias_own, bias_other

    def scan(side, lead, dtype):
        return scan_back(
            windows, chunk, side, lead, filtered, reads[side], decay, differ, cand, states, dtype
        )

    back_middle, mixed, gain_two_grad = beside(
        [feed_sum],
        lambda lead: norm_back(tangent, [lead, back_other], middle, ups, gain_two),
        back_own,
    )
    gate_other, cand_other, state_other, bias_other, mixer_other = beside(
        [feed_sum], lambda lead: scan(1, lead, low), mixed
    )
    mixed, mixer_other = hold(mixed, mixer_other)
    mixer_got = partner(mixer_other)
    gate_own, cand_own, state_own, bias_own, mixer_own = beside(
        [feed_sum], lambda lead: scan(0, lead, wide), mixed
    )
    mixer_own, mixer_got = hold(mixer_own, mixer_got)
    mixer_sum = DpSum(mixer_own, mixer_got)
    def put_back(whole_rows, got):
        return lax.dynamic_update_slice_in_dim(whole_rows, got, (1 - core) * windows, 0)

    grad_mine, grad_sent, gain_grad, taps_grad = beside(
        [feed_sum, mixer_sum],
        lambda lead: entry(
            core_at, inputs, got_inputs, orders, [lead, cand_own, gate_other, cand_other],
            back_middle, mixers, gain, causal_filter,
        ),
        gate_own,
    )
    def turn(gain_grad, taps_grad, state_other, grad_sent):
        short, sent = pack(
            width, gain_grad, taps_grad, gain_two_grad, bias_own, bias_other, up_bias_own, up_bias_other
        )
        return short + partner(sent), partner(state_other), partner(grad_sent)

    short, state_got, grad_got = beside(
        [mixer_sum], turn, gain_grad, taps_grad, state_other[:, 0], grad_sent
    )
    short_sum = DpSmall(short)
    out_mine, out_sent = beside(
        [feed_sum, mixer_sum, short_sum],
        lambda lead: leave(windows, core_at, orders[1], [lead, active_other], middle, downs),
        active_own,
    )

    def exits(grad_mine, grad_got, state_own, state_got, out_sent):
        state_gradient = jnp.where(
            core == 0,
            jnp.concatenate([state_own, state_got]),
            jnp.concatenate([state_got, state_own]),
        )
        return put_back(grad_mine, grad_got), state_gradient, partner(out_sent)

    input_gradient, state_gradient, out_got = beside(
        [mixer_sum, short_sum], exits, grad_mine, grad_got, state_own[:, 0], state_got, out_sent,
        loose=[feed_sum],
    )
    while len(mixer_sum.todo) > 1 or short_sum.todo:
        beside([mixer_sum, short_sum], lambda: ())

    def feed_results(mine, got, *gots):
        feed_sum.got = list(gots)
        while len(feed_sum.todo) > 1:
            feed_sum.finish()
            feed_sum.prepare()
            feed_sum.start()
        return put_back(mine, got), *finish_feed(*feed_sum.last())

    block_output, down_sum, up_sum, mixer_last = beside(
        [],
        lambda *leads: (*feed_results(*leads[:-1]), mixer_sum.begin(leads[-1])),
        out_mine,
        out_got,
        *feed_sum.got,
        mixer_sum.piece,
    )
    mixer_sum.got = [mixer_last]
    mixer_grad, read_grad = finish_mixer(*mixer_sum.last())
    short_sum = short_sum.terms[0]
    taps = causal_filter.shape[0]
    end = taps + 3 + units // width
    return (
        block_output,
        input_gradient,
        state_gradient,
        short_sum[0],
        short_sum[1 : 1 + taps],
        mixer_grad,
        short_sum[taps + 2, :channels],
        read_grad,
        short_sum[taps + 1],
        up_sum,
        short_sum[taps + 3 : end].reshape(units),
        down_sum,
    )


def solution(mesh):
    return jax.shard_map(
        local,
        mesh=mesh,
        in_specs=(
            P("dp", "tensor", None),
            P("dp", "tensor"),
            P(),
            P(),
            P(None, None, "tensor"),
            P("tensor"),
            P("tensor", None),
            P(),
            P(None, "tensor"),
            P("tensor"),
            P("tensor", None),
            P("dp", "tensor", None),
        ),
        out_specs=(
            P("dp", "tensor", None),
            P("dp", "tensor", None),
            P("dp", "tensor"),
            P(),
            P(),
            P(None, None, "tensor"),
            P("tensor"),
            P("tensor", None),
            P(),
            P(None, "tensor"),
            P("tensor"),
            P("tensor", None),
        ),
        check_vma=False,
    )
```

profile of v0, /device:TPU:0, one launch (start us, length us, event | category | flops | bytes accessed | tf_op | source)
XLA Modules:
  0.0 213.2 jit_solution(3002454196772485030)
XLA Ops:
  0.7 1.4 constant_dynamic-slice_fusion.1
  2.2 0.5 collective-permute-start
  3.1 0.5 collective-permute-start.4
  3.6 0.4 collective-permute-start.2
  4.0 1.0 constant_dynamic-slice_fusion
  5.1 2.2 %collective-permute-done.2 = f32[512]{0:T(512)S(1)} collective-permute-done((f32[512]{0:T(512)S(1)}, f32[512]{0:T(512)S(1)}, u32[]{:S(2)}, u32[]{:S(2)}) %collective-permute-start.2) | collective-permute-done | bytes 2080 | tf_op jit(solution)/shard_map/ppermute | solution.py:740
  8.1 0.6 broadcast_in_dim.27.start_own
  8.7 0.6 broadcast_in_dim.28.start_other
  9.6 0.7 copy-done.8
  10.3 1.0 copy-done.9
  11.3 19.7 %forward_mixer.1 = (bf16[2048,512]{1,0:T(8,128)(2,1)}, f32[2048,1024]{1,0:T(8,128)}, bf16[2048,1024]{1,0:T(8,128)(2,1)}, bf16[2048,1024]{1,0:T(8,128)(2,1)}, bf1...) custom-call(s32[1]{0:T(128)} %bitcast.core, ...), custom_call_target="tpu_custom_call" | custom-call | flops 6442450944 | bytes 25165824 | tf_op jit(solution)/shard_map/forward_mixer/pallas_call | solution.py:181
  31.1 0.5 copy-done.23
  31.6 0.4 copy-done.5
  32.1 17.9 %feed_forward.2 = (bf16[2048,1024]{1,0:T(8,128)(2,1)}, bf16[2048,1024]{1,0:T(8,128)(2,1)}, f32[8,1024]{1,0:T(8,128)}, bf16[1024,1024]{1,0:T(8,128)(2,1)}, bf16[2048,512]{1,0:T(8,128)(2,1)}) custom-call(s32[1]{0:T(128)} %bitcast.core, bf16[4,512,512]{2,1,0:T(8,128)(2,1)} %refs_0_.1, bf16[2,512,512]{2,1,0:T(8,128)(2,1)} %collective-permute-done.5.refs_1_, ...), custom_call_target="tpu_custom_call" | custom-call | flops 8589934592 | bytes 8388608 | tf_op jit(solution)/shard_map/feed_forward/pallas_call | solution.py:312
  50.1 16.2 %feed_forward.3 = (bf16[2048,1024]{1,0:T(8,128)(2,1)}, bf16[2048,1024]{1,0:T(8,128)(2,1)}, f32[8,1024]{1,0:T(8,128)}, f32[1024,1024]{1,0:T(8,128)}) custom-call(s32[1]{0:T(128)} %bitcast.core, bf16[2048,512]{1,0:T(8,128)(2,1)} %get-tuple-element.158.refs_0_.tangent, bf16[2048,512]{1,0:T(8,128)(2,1)} %get-tuple-element.155.refs_3_.refs_1_, ...), custom_call_target="tpu_custom_call" | custom-call | flops 8589934592 | bytes 8388608 | tf_op jit(solution)/shard_map/feed_forward/pallas_call | solution.py:312
  66.3 1.3 copy-done.3
  67.6 3.5 %convert_add_fusion = (f32[512,1024]{1,0:T(8,128)S(1)}, bf16[512,1024]{1,0:T(8,128)(2,1)S(1)}) fusion(f32[1024,1024]{1,0:T(8,128)} %get-tuple-element.162, s32[]{:T(128)S(6)} %select_n.159, bf16[1024,1024]{1,0:T(8,128)(2,1)} %copy-done.3, s32[]{:T(128)S(6)} %select_n.162), kind=kLoop, calls=%fused_computation.1 | loop fusion | flops 2621440 | bytes 9437192 | tf_op jit(solution)/shard_map/add | solution.py:795
  71.1 2.8 %collective-permute-start.10 = (bf16[512,1024]{1,0:T(8,128)(2,1)S(1)}, bf16[512,1024]{1,0:T(8,128)(2,1)}, u32[]{:S(2)}, u32[]{:S(2)}) collective-permute-start(bf16[512,1024]{1,0:T(8,128)(2,1)S(1)} %get-tuple-element.171), channel_id=1, source_target_pairs={{0,2},{1,5},{2,0},{3,7},{4,6},{5,1},{6,4},{7,3},{8,10},{9,13},{10,... | collective-permute-start | bytes 3145736 | tf_op jit(solution)/shard_map/ppermute | solution.py:778
  73.9 11.8 %norm_back.1 = (f32[2048,512]{1,0:T(8,128)}, bf16[2048,512]{1,0:T(8,128)(2,1)}, f32[1,512]{1,0:T(1,128)}) custom-call(bf16[2048,512]{1,0:T(8,128)(2,1)} %get-tuple-element.158.refs_0_.tangent, bf16[2048,1024]{1,0:T(8,128)(2,1)} %get-tuple-element.165.back_own, bf16[2048,1024]{1,0:T(8,128)(2,1)} %get-tuple-element.166.back_other, ...), custom_call_target="tpu_custom_call" | custom-call | flops 4294967296 | bytes 25165824 | tf_op jit(solution)/shard_map/norm_back/pallas_call | solution.py:353
  85.7 1.1 collective-permute-done.10
  86.8 1.6 convert_add_fusion.2
  88.4 2.1 collective-permute-start.11
  90.5 11.9 %scan_back.2 = (bf16[2048,512]{1,0:T(8,128)(2,1)}, bf16[2048,512]{1,0:T(8,128)(2,1)}, f32[2,1,512]{2,1,0:T(1,128)}, f32[8,512]{1,0:T(8,128)}, bf16[1536,512]{1,0:T(8,128)(2,1)}) custom-call(bf16[2048,512]{1,0:T(8,128)(2,1)} %get-tuple-element.189.mixed, bf16[2048,512]{1,0:T(8,128)(2,1)} %get-tuple-element.175.filtered, bf16[512,512]{1,0:T(8,128)(2,1)} %copy-done.12, ...), custom_call_target="tpu_custom_call" | custom-call | flops 4294967296 | bytes 14680064 | tf_op jit(solution)/shard_map/scan_back/pallas_call | solution.py:443
  102.6 1.6 collective-permute-start.12
  104.2 2.6 %collective-permute-start.13 = (bf16[64,1024]{1,0:T(8,128)(2,1)S(1)}, bf16[64,1024]{1,0:T(8,128)(2,1)S(1)}, u32[]{:S(2)}, u32[]{:S(2)}) collective-permute-start(bf16[64,1024]{1,0:T(8,128)(2,1)S(1)} %get-tuple-element.196), channel_id=1, source_target_pairs={{0,16},{1,17},{2,18},{3,19},{4,20},{5,21},{6,22},{7,23},{8,24},{9,... | collective-permute-start | bytes 393224 | tf_op jit(solution)/shard_map/ppermute | solution.py:778
  107.0 12.4 %scan_back.3 = (bf16[2048,512]{1,0:T(8,128)(2,1)}, bf16[2048,512]{1,0:T(8,128)(2,1)}, f32[2,1,512]{2,1,0:T(1,128)}, f32[8,512]{1,0:T(8,128)}, f32[1536,512]{1,0:T(8,128)}) custom-call(bf16[2048,512]{1,0:T(8,128)(2,1)} %get-tuple-element.189.mixed, bf16[2048,512]{1,0:T(8,128)(2,1)} %get-tuple-element.175.filtered, bf16[512,512]{1,0:T(8,128)(2,1)} %read.1, ...), custom_call_target="tpu_custom_call" | custom-call | flops 4294967296 | bytes 14680064 | tf_op jit(solution)/shard_map/scan_back/pallas_call | solution.py:443
  119.6 2.8 %convert_add_fusion.1 = (f32[768,512]{1,0:T(8,128)S(1)}, bf16[768,512]{1,0:T(8,128)(2,1)S(1)}) fusion(f32[1536,512]{1,0:T(8,128)} %get-tuple-element.204, s32[]{:T(128)S(6)} %select_n.172, bf16[1536,512]{1,0:T(8,128)(2,1)} %collective-permute-done.15, s32[]{:T(128)S(6)} %select_n.168), kind=kLoop, calls=%fused_computation.2 | loop fusion | flops 1966080 | bytes 7077896 | tf_op jit(solution)/shard_map/add | solution.py:795
  122.5 1.6 collective-permute-start.19
  124.0 0.6 collective-permute-start.16
  124.6 3.4 %collective-permute-start.17 = (bf16[64,1024]{1,0:T(8,128)(2,1)S(1)}, bf16[64,1024]{1,0:T(8,128)(2,1)S(1)}, u32[]{:S(2)}, u32[]{:S(2)}) collective-permute-start(bf16[64,1024]{1,0:T(8,128)(2,1)S(1)} %add_convert_fusion.4), channel_id=1, source_target_pairs={{0,16},{1,17},{2,18},{3,19},{4,20},{5,21},{6,22},{7,23},{8,24},{9,... | collective-permute-start | bytes 393224 | tf_op jit(solution)/shard_map/ppermute | solution.py:778
  128.4 15.4 %input_gradient.1 = (bf16[4,512,512]{2,1,0:T(8,128)(2,1)}, bf16[2,512,512]{2,1,0:T(8,128)(2,1)}, f32[1,512]{1,0:T(1,128)}, f32[4,512]{1,0:T(4,128)}) custom-call(s32[1]{0:T(128)} %bitcast.core, bf16[4,512,512]{2,1,0:T(8,128)(2,1)} %own.3, bf16[2,512,512]{2,1,0:T(8,128)(2,1)} %copy-done.8, bf16[512,512]{1,0:T(8,128)(2,1)} %get-tuple-element.154.refs_2_.order, ...), custom_call_target="tpu_custom_call" | custom-call | flops 4294967296 | bytes 12582912 | tf_op jit(solution)/shard_map/input_gradient/pallas_call | solution.py:567
  143.9 1.0 add_convert_fusion.3
  144.9 0.6 collective-permute-start.23
  145.5 1.5 pack_short.1
  147.5 1.1 maximum_select_fusion.4
  148.8 4.1 %collective-permute-done.23 = bf16[384,512]{1,0:T(8,128)(2,1)S(1)} collective-permute-done((bf16[384,512]{1,0:T(8,128)(2,1)}, bf16[384,512]{1,0:T(8,128)(2,1)S(1)}, u32[]{:S(2)}, u32[]{:S(2)}) %collective-permute-start.23) | collective-permute-done | bytes 393248 | tf_op jit(solution)/shard_map/ppermute | solution.py:778
  153.0 0.7 copy-done.14
  153.7 0.5 collective-permute-start.24
  154.4 3.8 %collective-permute-start.26 = (bf16[96,512]{1,0:T(8,128)(2,1)S(1)}, bf16[96,512]{1,0:T(8,128)(2,1)S(1)}, u32[]{:S(2)}, u32[]{:S(2)}) collective-permute-start(bf16[96,512]{1,0:T(8,128)(2,1)S(1)} %get-tuple-element.245), channel_id=1, source_target_pairs={{0,16},{1,17},{2,18},{3,19},{4,20},{5,21},{6,22},{7,23},{8,24},{9,... | collective-permute-start | bytes 294920 | tf_op jit(solution)/shard_map/ppermute | solution.py:778
  158.6 0.6 collective-permute-start.28
  159.2 11.2 %block_output.1 = (bf16[4,512,512]{2,1,0:T(8,128)(2,1)}, bf16[2,512,512]{2,1,0:T(8,128)(2,1)}) custom-call(s32[1]{0:T(128)} %bitcast.core, bf16[512,512]{1,0:T(8,128)(2,1)} %get-tuple-element.153.back_order, bf16[2048,1024]{1,0:T(8,128)(2,1)} %get-tuple-element.239.active_own, bf16[2048,1024]{1,0:T(8,128)(2,1)} %get-tuple-element.240.active_other, ...), custom_call_target="tpu_custom_call" | custom-call | flops 4294967296 | bytes 12582912 | tf_op jit(solution)/shard_map/block_output/pallas_call | solution.py:625
  170.4 0.5 maximum_select_fusion.piece
  170.9 1.3 add_convert_fusion.8
  172.5 3.8 %collective-permute-start.31 = (bf16[96,512]{1,0:T(8,128)(2,1)S(1)}, bf16[96,512]{1,0:T(8,128)(2,1)S(1)}, u32[]{:S(2)}, u32[]{:S(2)}) collective-permute-start(bf16[96,512]{1,0:T(8,128)(2,1)S(1)} %add_convert_fusion.8), channel_id=1, source_target_pairs={{0,16},{1,17},{2,18},{3,19},{4,20},{5,21},{6,22},{7,23},{8,24},{9,... | collective-permute-start | bytes 294920 | tf_op jit(solution)/shard_map/ppermute | solution.py:778
  176.4 1.5 collective-permute-start.33
  177.9 1.5 collective-permute-start.34
  179.4 1.1 collective-permute-done.33
  180.9 0.6 maximum_select_fusion.8
  181.8 5.1 %collective-permute-done.32 = bf16[96,512]{1,0:T(8,128)(2,1)S(1)} collective-permute-done((bf16[96,512]{1,0:T(8,128)(2,1)S(1)}, bf16[96,512]{1,0:T(8,128)(2,1)S(1)}, u32[]{:S(2)}, u32[]{:S(2)}) %collective-permute-start.32) | collective-permute-done | bytes 98336 | tf_op jit(solution)/shard_map/ppermute | solution.py:778
  187.2 1.7 collective-permute-start.35
  188.9 1.0 collective-permute-start.37
  189.9 3.4 %collective-permute-start.38 = (f32[16,512]{1,0:T(8,128)S(1)}, f32[16,512]{1,0:T(8,128)S(1)}, u32[]{:S(2)}, u32[]{:S(2)}) collective-permute-start(f32[16,512]{1,0:T(8,128)S(1)} %add.200), channel_id=1, source_target_pairs={{0,24},{1,25},{2,26},{3,27},{4,28},{5,29},{6,30},{7,31},{8,16},{9,... | collective-permute-start | bytes 98312 | tf_op jit(solution)/shard_map/ppermute | solution.py:778
  193.2 0.4 collective-permute-done.37
  193.7 1.9 collective-permute-done.38
  196.1 0.8 collective-permute-done.34.got
  196.9 1.5 collective-permute-start.39
  198.4 0.6 slice.21
  199.0 0.6 copy.27
  199.6 3.4 %finish_feed.1 = (f32[1024,512]{1,0:T(8,128)}, f32[512,1024]{1,0:T(8,128)}) custom-call(s32[1]{0:T(128)} %bitcast.7.bit, bf16[512,1024]{1,0:T(8,128)(2,1)} %copy-done, bf16[512,1024]{1,0:T(8,128)(2,1)} %copy-done.6), custom_call_target="tpu_custom_call" | custom-call | tf_op jit(solution)/shard_map/finish_feed/pallas_call | solution.py:687
  203.0 1.0 constant_dynamic-update-slice_fusion
  204.0 0.6 fusion
  204.6 4.3 %collective-permute-done.39.got = bf16[768,512]{1,0:T(8,128)(2,1)S(1)} collective-permute-done((bf16[768,512]{1,0:T(8,128)(2,1)S(1)}, bf16[768,512]{1,0:T(8,128)(2,1)S(1)}, u32[]{:S(2)}, u32[]{:S(2)}) %collective-permute-start.39) | collective-permute-done | bytes 786464 | tf_op jit(solution)/shard_map/ppermute | solution.py:778
  208.9 0.9 copy-done.10
  209.8 3.5 %finish_mixer.1 = (f32[512,2,512]{2,1,0:T(2,128)}, f32[512,512]{1,0:T(8,128)}) custom-call(s32[1]{0:T(128)} %bitcast.7.bit, bf16[768,512]{1,0:T(8,128)(2,1)} %copy-done.2, bf16[768,512]{1,0:T(8,128)(2,1)} %copy-done.10), custom_call_target="tpu_custom_call" | custom-call | tf_op jit(solution)/shard_map/finish_mixer/pallas_call | solution.py:719
  (112 shorter events, 5.9 us)
Async XLA Ops:
  0.6 2.0 copy-start.7
  0.7 2.4 %copy-start.11 = (bf16[512,512]{1,0:T(8,128)(2,1)S(1)}, bf16[512,512]{1,0:T(8,128)(2,1)}, u32[]{:S(2)}) copy-start(bf16[512,512]{1,0:T(8,128)(2,1)} %read.1) | copy-start | bytes 1572868
  0.7 2.8 %copy-start.17 = (f32[4,512]{1,0:T(4,128)S(1)}, f32[4,512]{1,0:T(4,128)}, u32[]{:S(2)}) copy-start(f32[4,512]{1,0:T(4,128)} %param.13) | copy-start | bytes 24580
  0.7 2.9 %copy-start.24 = (f32[512]{0:T(512)S(1)}, f32[512]{0:T(512)}, u32[]{:S(2)}) copy-start(f32[512]{0:T(512)} %param.17) | copy-start | bytes 6148
  0.7 3.3 %copy-start.13 = (bf16[4,512,512]{2,1,0:T(8,128)(2,1)S(1)}, bf16[4,512,512]{2,1,0:T(8,128)(2,1)}, u32[]{:S(2)}) copy-start(bf16[4,512,512]{2,1,0:T(8,128)(2,1)} %refs_0_.1) | copy-start | bytes 6291460
  2.2 7.2 %collective-permute-start = (bf16[2,512,512]{2,1,0:T(8,128)(2,1)S(1)}, bf16[2,512,512]{2,1,0:T(8,128)(2,1)S(1)}, u32[]{:S(2)}, u32[]{:S(2)}) collective-permute-start(bf16[2,512,512]{2,1,0:T(8,128)(2,1)S(1)} %constant_dynamic-slice_fusion.1), channel_id=1, source_target_pairs={{0,1},{1,0},{2,3},{3,2},{4,5},{5,4},{6,7},{7,6},{8,9},{9,8},{10,11... | collective-permute-start | bytes 3145736 | tf_op jit(solution)/shard_map/ppermute | solution.py:740
  2.7 4.9 %copy-start.4 = (bf16[512,1024]{1,0:T(8,128)(2,1)S(1)}, bf16[512,1024]{1,0:T(8,128)(2,1)}, u32[]{:S(2)}) copy-start(bf16[512,1024]{1,0:T(8,128)(2,1)} %up_own.1) | copy-start | bytes 3145732
  2.7 6.7 %copy-start.22 = (f32[1024]{0:T(1024)S(1)}, f32[1024]{0:T(1024)}, u32[]{:S(2)}) copy-start(f32[1024]{0:T(1024)} %param.21) | copy-start | bytes 12292
  2.9 8.4 %copy-start.1 = (bf16[64,8,2,512]{3,1,2,0:T(8,128)(2,1)}, bf16[64,8,2,512]{3,1,2,0:T(8,128)(2,1)S(1)}, u32[]{:S(2)}) copy-start(bf16[64,8,2,512]{3,1,2,0:T(8,128)(2,1)S(1)} %copy.26) | copy-start | bytes 3145732
  2.9 6.6 %collective-permute-start.1 = (bf16[512,1024]{1,0:T(8,128)(2,1)S(1)}, bf16[512,1024]{1,0:T(8,128)(2,1)S(1)}, u32[]{:S(2)}, u32[]{:S(2)}) collective-permute-start(bf16[512,1024]{1,0:T(8,128)(2,1)S(1)} %bitcast.22), channel_id=1, source_target_pairs={{0,1},{1,0},{2,3},{3,2},{4,5},{5,4},{6,7},{7,6},{8,9},{9,8},{10,11... | collective-permute-start | bytes 3145736 | tf_op jit(solution)/shard_map/ppermute | solution.py:740
  3.1 4.7 %collective-permute-start.4 = (bf16[512,512]{1,0:T(8,128)(2,1)S(1)}, bf16[512,512]{1,0:T(8,128)(2,1)S(1)}, u32[]{:S(2)}, u32[]{:S(2)}) collective-permute-start(bf16[512,512]{1,0:T(8,128)(2,1)S(1)} %copy-done.11), channel_id=1, source_target_pairs={{0,1},{1,0},{2,3},{3,2},{4,5},{5,4},{6,7},{7,6},{8,9},{9,8},{10,11... | collective-permute-start | bytes 1572872 | tf_op jit(solution)/shard_map/ppermute | solution.py:740
  3.5 4.1 %collective-permute-start.3 = (f32[4,512]{1,0:T(4,128)S(1)}, f32[4,512]{1,0:T(4,128)S(1)}, u32[]{:S(2)}, u32[]{:S(2)}) collective-permute-start(f32[4,512]{1,0:T(4,128)S(1)} %copy-done.17), channel_id=1, source_target_pairs={{0,1},{1,0},{2,3},{3,2},{4,5},{5,4},{6,7},{7,6},{8,9},{9,8},{10,11... | collective-permute-start | bytes 24584 | tf_op jit(solution)/shard_map/ppermute | solution.py:740
  3.6 3.6 %collective-permute-start.2 = (f32[512]{0:T(512)S(1)}, f32[512]{0:T(512)S(1)}, u32[]{:S(2)}, u32[]{:S(2)}) collective-permute-start(f32[512]{0:T(512)S(1)} %copy-done.24), channel_id=1, source_target_pairs={{0,1},{1,0},{2,3},{3,2},{4,5},{5,4},{6,7},{7,6},{8,9},{9,8},{10,11... | collective-permute-start | bytes 6152 | tf_op jit(solution)/shard_map/ppermute | solution.py:740
  7.2 4.1 %copy-start.25 = (f32[512]{0:T(512)}, f32[512]{0:T(512)S(1)}, u32[]{:S(2)}) copy-start(f32[512]{0:T(512)S(1)} %collective-permute-done.2) | copy-start | bytes 6148
  7.2 23.8 %collective-permute-start.5 = (bf16[2,512,512]{2,1,0:T(8,128)(2,1)}, bf16[2,512,512]{2,1,0:T(8,128)(2,1)}, u32[]{:S(2)}, u32[]{:S(2)}) collective-permute-start(bf16[2,512,512]{2,1,0:T(8,128)(2,1)} %constant_dynamic-slice_fusion), channel_id=1, source_target_pairs={{0,1},{1,0},{2,3},{3,2},{4,5},{5,4},{6,7},{7,6},{8,9},{9,8},{10,11... | collective-permute-start | bytes 3145736 | tf_op jit(solution)/shard_map/ppermute | solution.py:740
  7.6 23.5 %collective-permute-start.6 = (bf16[512,1024]{1,0:T(8,128)(2,1)S(1)}, bf16[512,1024]{1,0:T(8,128)(2,1)S(1)}, u32[]{:S(2)}, u32[]{:S(2)}) collective-permute-start(bf16[512,1024]{1,0:T(8,128)(2,1)S(1)} %copy-done.4), channel_id=1, source_target_pairs={{0,1},{1,0},{2,3},{3,2},{4,5},{5,4},{6,7},{7,6},{8,9},{9,8},{10,11... | collective-permute-start | bytes 3145736 | tf_op jit(solution)/shard_map/ppermute | solution.py:740
  7.8 3.6 %copy-start.12 = (bf16[512,512]{1,0:T(8,128)(2,1)}, bf16[512,512]{1,0:T(8,128)(2,1)S(1)}, u32[]{:S(2)}) copy-start(bf16[512,512]{1,0:T(8,128)(2,1)S(1)} %collective-permute-done.4.read_other.read) | copy-start | bytes 1572868
  7.8 23.3 %collective-permute-start.8 = (bf16[1024,512]{1,0:T(8,128)(2,1)}, bf16[1024,512]{1,0:T(8,128)(2,1)}, u32[]{:S(2)}, u32[]{:S(2)}) collective-permute-start(bf16[1024,512]{1,0:T(8,128)(2,1)} %down_own.1), channel_id=1, source_target_pairs={{0,1},{1,0},{2,3},{3,2},{4,5},{5,4},{6,7},{7,6},{8,9},{9,8},{10,11... | collective-permute-start | bytes 3145736 | tf_op jit(solution)/shard_map/ppermute | solution.py:740
  9.3 1.0 copy-start.8
  9.3 21.7 %collective-permute-start.7 = (f32[1024]{0:T(1024)S(1)}, f32[1024]{0:T(1024)S(1)}, u32[]{:S(2)}, u32[]{:S(2)}) collective-permute-start(f32[1024]{0:T(1024)S(1)} %copy-done.22), channel_id=1, source_target_pairs={{0,1},{1,0},{2,3},{3,2},{4,5},{5,4},{6,7},{7,6},{8,9},{9,8},{10,11... | collective-permute-start | bytes 12296 | tf_op jit(solution)/shard_map/ppermute | solution.py:740
  10.3 1.0 copy-start.9
  31.1 1.0 copy-start.5
  49.9 16.3 %collective-permute-start.9 = (bf16[1024,1024]{1,0:T(8,128)(2,1)}, bf16[1024,1024]{1,0:T(8,128)(2,1)S(1)}, u32[]{:S(2)}, u32[]{:S(2)}) collective-permute-start(bf16[1024,1024]{1,0:T(8,128)(2,1)} %get-tuple-element.161), channel_id=1, source_target_pairs={{0,1},{1,0},{2,3},{3,2},{4,5},{5,4},{6,7},{7,6},{8,9},{9,8},{10,11... | collective-permute-start | bytes 6291464 | tf_op jit(solution)/shard_map/ppermute | solution.py:740
  66.3 1.3 copy-start.3
  71.1 15.7 %collective-permute-start.10 = (bf16[512,1024]{1,0:T(8,128)(2,1)S(1)}, bf16[512,1024]{1,0:T(8,128)(2,1)}, u32[]{:S(2)}, u32[]{:S(2)}) collective-permute-start(bf16[512,1024]{1,0:T(8,128)(2,1)S(1)} %get-tuple-element.171), channel_id=1, source_target_pairs={{0,2},{1,5},{2,0},{3,7},{4,6},{5,1},{6,4},{7,3},{8,10},{9,13},{10,... | collective-permute-start | bytes 3145736 | tf_op jit(solution)/shard_map/ppermute | solution.py:778
  88.4 14.0 %collective-permute-start.11 = (bf16[256,1024]{1,0:T(8,128)(2,1)S(1)}, bf16[256,1024]{1,0:T(8,128)(2,1)S(1)}, u32[]{:S(2)}, u32[]{:S(2)}) collective-permute-start(bf16[256,1024]{1,0:T(8,128)(2,1)S(1)} %get-tuple-element.185), channel_id=1, source_target_pairs={{0,4},{1,3},{2,6},{3,1},{4,0},{5,7},{6,2},{7,5},{8,12},{9,11},{10,... | collective-permute-start | bytes 1572872 | tf_op jit(solution)/shard_map/ppermute | solution.py:778
  102.4 17.3 %collective-permute-start.15 = (bf16[1536,512]{1,0:T(8,128)(2,1)}, bf16[1536,512]{1,0:T(8,128)(2,1)}, u32[]{:S(2)}, u32[]{:S(2)}) collective-permute-start(bf16[1536,512]{1,0:T(8,128)(2,1)} %get-tuple-element.203), channel_id=1, source_target_pairs={{0,1},{1,0},{2,3},{3,2},{4,5},{5,4},{6,7},{7,6},{8,9},{9,8},{10,11... | collective-permute-start | bytes 4718600 | tf_op jit(solution)/shard_map/ppermute | solution.py:740
  102.6 16.9 %collective-permute-start.12 = (bf16[64,1024]{1,0:T(8,128)(2,1)S(1)}, bf16[64,1024]{1,0:T(8,128)(2,1)S(1)}, u32[]{:S(2)}, u32[]{:S(2)}) collective-permute-start(bf16[64,1024]{1,0:T(8,128)(2,1)S(1)} %get-tuple-element.195), channel_id=1, source_target_pairs={{0,8},{1,9},{2,10},{3,11},{4,12},{5,13},{6,14},{7,15},{8,0},{9,1},... | collective-permute-start | bytes 393224 | tf_op jit(solution)/shard_map/ppermute | solution.py:778
  104.2 15.3 %collective-permute-start.13 = (bf16[64,1024]{1,0:T(8,128)(2,1)S(1)}, bf16[64,1024]{1,0:T(8,128)(2,1)S(1)}, u32[]{:S(2)}, u32[]{:S(2)}) collective-permute-start(bf16[64,1024]{1,0:T(8,128)(2,1)S(1)} %get-tuple-element.196), channel_id=1, source_target_pairs={{0,16},{1,17},{2,18},{3,19},{4,20},{5,21},{6,22},{7,23},{8,24},{9,... | collective-permute-start | bytes 393224 | tf_op jit(solution)/shard_map/ppermute | solution.py:778
  106.8 12.7 %collective-permute-start.14 = (bf16[64,1024]{1,0:T(8,128)(2,1)S(1)}, bf16[64,1024]{1,0:T(8,128)(2,1)S(1)}, u32[]{:S(2)}, u32[]{:S(2)}) collective-permute-start(bf16[64,1024]{1,0:T(8,128)(2,1)S(1)} %get-tuple-element.197), channel_id=1, source_target_pairs={{0,24},{1,25},{2,26},{3,27},{4,28},{5,29},{6,30},{7,31},{8,16},{9,... | collective-permute-start | bytes 393224 | tf_op jit(solution)/shard_map/ppermute | solution.py:778
  119.6 4.4 %copy-start.19 = (f32[2,1,512]{2,1,0:T(1,128)S(1)}, f32[2,1,512]{2,1,0:T(1,128)}, u32[]{:S(2)}) copy-start(f32[2,1,512]{2,1,0:T(1,128)} %get-tuple-element.223) | copy-start | bytes 12292
  122.5 21.4 %collective-permute-start.19 = (bf16[768,512]{1,0:T(8,128)(2,1)S(1)}, bf16[768,512]{1,0:T(8,128)(2,1)S(1)}, u32[]{:S(2)}, u32[]{:S(2)}) collective-permute-start(bf16[768,512]{1,0:T(8,128)(2,1)S(1)} %get-tuple-element.216), channel_id=1, source_target_pairs={{0,2},{1,5},{2,0},{3,7},{4,6},{5,1},{6,4},{7,3},{8,10},{9,13},{10,... | collective-permute-start | bytes 2359304 | tf_op jit(solution)/shard_map/ppermute | solution.py:778
  124.0 19.8 %collective-permute-start.16 = (bf16[64,1024]{1,0:T(8,128)(2,1)S(1)}, bf16[64,1024]{1,0:T(8,128)(2,1)S(1)}, u32[]{:S(2)}, u32[]{:S(2)}) collective-permute-start(bf16[64,1024]{1,0:T(8,128)(2,1)S(1)} %add_convert_fusion.4), channel_id=1, source_target_pairs={{0,8},{1,9},{2,10},{3,11},{4,12},{5,13},{6,14},{7,15},{8,0},{9,1},... | collective-permute-start | bytes 393224 | tf_op jit(solution)/shard_map/ppermute | solution.py:778
  124.6 19.2 %collective-permute-start.17 = (bf16[64,1024]{1,0:T(8,128)(2,1)S(1)}, bf16[64,1024]{1,0:T(8,128)(2,1)S(1)}, u32[]{:S(2)}, u32[]{:S(2)}) collective-permute-start(bf16[64,1024]{1,0:T(8,128)(2,1)S(1)} %add_convert_fusion.4), channel_id=1, source_target_pairs={{0,16},{1,17},{2,18},{3,19},{4,20},{5,21},{6,22},{7,23},{8,24},{9,... | collective-permute-start | bytes 393224 | tf_op jit(solution)/shard_map/ppermute | solution.py:778
  128.0 15.8 %collective-permute-start.18 = (bf16[64,1024]{1,0:T(8,128)(2,1)S(1)}, bf16[64,1024]{1,0:T(8,128)(2,1)S(1)}, u32[]{:S(2)}, u32[]{:S(2)}) collective-permute-start(bf16[64,1024]{1,0:T(8,128)(2,1)S(1)} %add_convert_fusion.4), channel_id=1, source_target_pairs={{0,24},{1,25},{2,26},{3,27},{4,28},{5,29},{6,30},{7,31},{8,16},{9,... | collective-permute-start | bytes 393224 | tf_op jit(solution)/shard_map/ppermute | solution.py:778
  143.9 1.0 copy-start.15
  144.9 9.3 %copy-start.18 = (f32[2,1,512]{2,1,0:T(1,128)S(1)}, f32[2,1,512]{2,1,0:T(1,128)}, u32[]{:S(2)}) copy-start(f32[2,1,512]{2,1,0:T(1,128)} %get-tuple-element.251) | copy-start | bytes 12292
  144.9 8.1 %collective-permute-start.22 = (bf16[2,512,512]{2,1,0:T(8,128)(2,1)}, bf16[2,512,512]{2,1,0:T(8,128)(2,1)S(1)}, u32[]{:S(2)}, u32[]{:S(2)}) collective-permute-start(bf16[2,512,512]{2,1,0:T(8,128)(2,1)} %get-tuple-element.235), channel_id=1, source_target_pairs={{0,1},{1,0},{2,3},{3,2},{4,5},{5,4},{6,7},{7,6},{8,9},{9,8},{10,11... | collective-permute-start | bytes 3145736 | tf_op jit(solution)/shard_map/ppermute | solution.py:740
  144.9 8.0 %collective-permute-start.23 = (bf16[384,512]{1,0:T(8,128)(2,1)}, bf16[384,512]{1,0:T(8,128)(2,1)S(1)}, u32[]{:S(2)}, u32[]{:S(2)}) collective-permute-start(bf16[384,512]{1,0:T(8,128)(2,1)} %get-tuple-element.236), channel_id=1, source_target_pairs={{0,4},{1,3},{2,6},{3,1},{4,0},{5,7},{6,2},{7,5},{8,12},{9,11},{10,... | collective-permute-start | bytes 1179656 | tf_op jit(solution)/shard_map/ppermute | solution.py:778
  147.0 1.8 copy-start.16
  147.0 1.8 collective-permute-start.20
  147.2 1.6 collective-permute-start.21
  153.7 16.7 %collective-permute-start.24 = (bf16[256,1024]{1,0:T(8,128)(2,1)S(1)}, bf16[256,1024]{1,0:T(8,128)(2,1)S(1)}, u32[]{:S(2)}, u32[]{:S(2)}) collective-permute-start(bf16[256,1024]{1,0:T(8,128)(2,1)S(1)} %maximum_select_fusion.2), channel_id=1, source_target_pairs={{0,4},{1,3},{2,6},{3,1},{4,0},{5,7},{6,2},{7,5},{8,12},{9,11},{10,... | collective-permute-start | bytes 1572872 | tf_op jit(solution)/shard_map/ppermute | solution.py:778
  154.2 16.2 %collective-permute-start.25 = (bf16[96,512]{1,0:T(8,128)(2,1)S(1)}, bf16[96,512]{1,0:T(8,128)(2,1)S(1)}, u32[]{:S(2)}, u32[]{:S(2)}) collective-permute-start(bf16[96,512]{1,0:T(8,128)(2,1)S(1)} %get-tuple-element.244), channel_id=1, source_target_pairs={{0,8},{1,9},{2,10},{3,11},{4,12},{5,13},{6,14},{7,15},{8,0},{9,1},... | collective-permute-start | bytes 294920 | tf_op jit(solution)/shard_map/ppermute | solution.py:778
  154.4 16.0 %collective-permute-start.26 = (bf16[96,512]{1,0:T(8,128)(2,1)S(1)}, bf16[96,512]{1,0:T(8,128)(2,1)S(1)}, u32[]{:S(2)}, u32[]{:S(2)}) collective-permute-start(bf16[96,512]{1,0:T(8,128)(2,1)S(1)} %get-tuple-element.245), channel_id=1, source_target_pairs={{0,16},{1,17},{2,18},{3,19},{4,20},{5,21},{6,22},{7,23},{8,24},{9,... | collective-permute-start | bytes 294920 | tf_op jit(solution)/shard_map/ppermute | solution.py:778
  158.2 12.2 %collective-permute-start.27 = (bf16[96,512]{1,0:T(8,128)(2,1)S(1)}, bf16[96,512]{1,0:T(8,128)(2,1)S(1)}, u32[]{:S(2)}, u32[]{:S(2)}) collective-permute-start(bf16[96,512]{1,0:T(8,128)(2,1)S(1)} %get-tuple-element.246), channel_id=1, source_target_pairs={{0,24},{1,25},{2,26},{3,27},{4,28},{5,29},{6,30},{7,31},{8,16},{9,... | collective-permute-start | bytes 294920 | tf_op jit(solution)/shard_map/ppermute | solution.py:778
  158.6 11.8 %collective-permute-start.28 = (f32[16,512]{1,0:T(8,128)S(1)}, f32[16,512]{1,0:T(8,128)S(1)}, u32[]{:S(2)}, u32[]{:S(2)}) collective-permute-start(f32[16,512]{1,0:T(8,128)S(1)} %add.188), channel_id=1, source_target_pairs={{0,2},{1,3},{2,0},{3,1},{4,6},{5,7},{6,4},{7,5},{8,10},{9,11},{10,... | collective-permute-start | bytes 98312 | tf_op jit(solution)/shard_map/ppermute | solution.py:778
  170.4 9.0 %copy-start.20 = (bf16[4,512,512]{2,1,0:T(8,128)(2,1)S(1)}, bf16[4,512,512]{2,1,0:T(8,128)(2,1)}, u32[]{:S(2)}) copy-start(bf16[4,512,512]{2,1,0:T(8,128)(2,1)} %get-tuple-element.259) | copy-start | bytes 6291460
  170.9 16.2 %copy-start = (bf16[512,1024]{1,0:T(8,128)(2,1)}, bf16[512,1024]{1,0:T(8,128)(2,1)S(1)}, u32[]{:S(2)}) copy-start(bf16[512,1024]{1,0:T(8,128)(2,1)S(1)} %maximum_select_fusion.piece) | copy-start | bytes 3145732
  172.2 14.7 %collective-permute-start.29 = (bf16[2,512,512]{2,1,0:T(8,128)(2,1)}, bf16[2,512,512]{2,1,0:T(8,128)(2,1)S(1)}, u32[]{:S(2)}, u32[]{:S(2)}) collective-permute-start(bf16[2,512,512]{2,1,0:T(8,128)(2,1)} %get-tuple-element.263), channel_id=1, source_target_pairs={{0,1},{1,0},{2,3},{3,2},{4,5},{5,4},{6,7},{7,6},{8,9},{9,8},{10,11... | collective-permute-start | bytes 3145736 | tf_op jit(solution)/shard_map/ppermute | solution.py:740
  172.3 9.2 %collective-permute-start.30 = (bf16[96,512]{1,0:T(8,128)(2,1)S(1)}, bf16[96,512]{1,0:T(8,128)(2,1)S(1)}, u32[]{:S(2)}, u32[]{:S(2)}) collective-permute-start(bf16[96,512]{1,0:T(8,128)(2,1)S(1)} %add_convert_fusion.8), channel_id=1, source_target_pairs={{0,8},{1,9},{2,10},{3,11},{4,12},{5,13},{6,14},{7,15},{8,0},{9,1},... | collective-permute-start | bytes 294920 | tf_op jit(solution)/shard_map/ppermute | solution.py:778
  172.5 9.3 %collective-permute-start.31 = (bf16[96,512]{1,0:T(8,128)(2,1)S(1)}, bf16[96,512]{1,0:T(8,128)(2,1)S(1)}, u32[]{:S(2)}, u32[]{:S(2)}) collective-permute-start(bf16[96,512]{1,0:T(8,128)(2,1)S(1)} %add_convert_fusion.8), channel_id=1, source_target_pairs={{0,16},{1,17},{2,18},{3,19},{4,20},{5,21},{6,22},{7,23},{8,24},{9,... | collective-permute-start | bytes 294920 | tf_op jit(solution)/shard_map/ppermute | solution.py:778
  176.4 4.1 %collective-permute-start.33 = (f32[16,512]{1,0:T(8,128)S(1)}, f32[16,512]{1,0:T(8,128)S(1)}, u32[]{:S(2)}, u32[]{:S(2)}) collective-permute-start(f32[16,512]{1,0:T(8,128)S(1)} %add.199), channel_id=1, source_target_pairs={{0,4},{1,5},{2,6},{3,7},{4,0},{5,1},{6,2},{7,3},{8,12},{9,13},{10,... | collective-permute-start | bytes 98312 | tf_op jit(solution)/shard_map/ppermute | solution.py:778
  177.9 19.0 %collective-permute-start.34 = (bf16[512,1024]{1,0:T(8,128)(2,1)S(1)}, bf16[512,1024]{1,0:T(8,128)(2,1)S(1)}, u32[]{:S(2)}, u32[]{:S(2)}) collective-permute-start(bf16[512,1024]{1,0:T(8,128)(2,1)S(1)} %maximum_select_fusion.piece), channel_id=1, source_target_pairs={{0,2},{1,5},{2,0},{3,7},{4,6},{5,1},{6,4},{7,3},{8,10},{9,13},{10,... | collective-permute-start | bytes 3145736 | tf_op jit(solution)/shard_map/ppermute | solution.py:778
  179.4 20.1 %copy-start.21 = (bf16[4,512,512]{2,1,0:T(8,128)(2,1)}, bf16[4,512,512]{2,1,0:T(8,128)(2,1)S(1)}, u32[]{:S(2)}) copy-start(bf16[4,512,512]{2,1,0:T(8,128)(2,1)S(1)} %constant_dynamic-update-slice_fusion.1) | copy-start | bytes 6291460
  180.5 6.4 %collective-permute-start.32 = (bf16[96,512]{1,0:T(8,128)(2,1)S(1)}, bf16[96,512]{1,0:T(8,128)(2,1)S(1)}, u32[]{:S(2)}, u32[]{:S(2)}) collective-permute-start(bf16[96,512]{1,0:T(8,128)(2,1)S(1)} %add_convert_fusion.8), channel_id=1, source_target_pairs={{0,24},{1,25},{2,26},{3,27},{4,28},{5,29},{6,30},{7,31},{8,16},{9,... | collective-permute-start | bytes 294920 | tf_op jit(solution)/shard_map/ppermute | solution.py:778
  187.2 8.6 %collective-permute-start.35 = (bf16[384,512]{1,0:T(8,128)(2,1)S(1)}, bf16[384,512]{1,0:T(8,128)(2,1)S(1)}, u32[]{:S(2)}, u32[]{:S(2)}) collective-permute-start(bf16[384,512]{1,0:T(8,128)(2,1)S(1)} %maximum_select_fusion.3), channel_id=1, source_target_pairs={{0,4},{1,3},{2,6},{3,1},{4,0},{5,7},{6,2},{7,5},{8,12},{9,11},{10,... | collective-permute-start | bytes 1179656 | tf_op jit(solution)/shard_map/ppermute | solution.py:778
  188.9 4.4 %collective-permute-start.36 = (f32[16,512]{1,0:T(8,128)S(1)}, f32[16,512]{1,0:T(8,128)S(1)}, u32[]{:S(2)}, u32[]{:S(2)}) collective-permute-start(f32[16,512]{1,0:T(8,128)S(1)} %add.200), channel_id=1, source_target_pairs={{0,8},{1,9},{2,10},{3,11},{4,12},{5,13},{6,14},{7,15},{8,0},{9,1},... | collective-permute-start | bytes 98312 | tf_op jit(solution)/shard_map/ppermute | solution.py:778
  188.9 4.8 %collective-permute-start.37 = (f32[16,512]{1,0:T(8,128)S(1)}, f32[16,512]{1,0:T(8,128)S(1)}, u32[]{:S(2)}, u32[]{:S(2)}) collective-permute-start(f32[16,512]{1,0:T(8,128)S(1)} %add.200), channel_id=1, source_target_pairs={{0,16},{1,17},{2,18},{3,19},{4,20},{5,21},{6,22},{7,23},{8,24},{9,... | collective-permute-start | bytes 98312 | tf_op jit(solution)/shard_map/ppermute | solution.py:778
  189.9 5.7 %collective-permute-start.38 = (f32[16,512]{1,0:T(8,128)S(1)}, f32[16,512]{1,0:T(8,128)S(1)}, u32[]{:S(2)}, u32[]{:S(2)}) collective-permute-start(f32[16,512]{1,0:T(8,128)S(1)} %add.200), channel_id=1, source_target_pairs={{0,24},{1,25},{2,26},{3,27},{4,28},{5,29},{6,30},{7,31},{8,16},{9,... | collective-permute-start | bytes 98312 | tf_op jit(solution)/shard_map/ppermute | solution.py:778
  196.0 8.0 %copy-start.2 = (bf16[768,512]{1,0:T(8,128)(2,1)}, bf16[768,512]{1,0:T(8,128)(2,1)S(1)}, u32[]{:S(2)}) copy-start(bf16[768,512]{1,0:T(8,128)(2,1)S(1)} %maximum_select_fusion.1.piece) | copy-start | bytes 2359300
  196.9 2.7 %copy-start.6 = (bf16[512,1024]{1,0:T(8,128)(2,1)}, bf16[512,1024]{1,0:T(8,128)(2,1)S(1)}, u32[]{:S(2)}) copy-start(bf16[512,1024]{1,0:T(8,128)(2,1)S(1)} %collective-permute-done.34.got) | copy-start | bytes 3145732
  196.9 12.0 %collective-permute-start.39 = (bf16[768,512]{1,0:T(8,128)(2,1)S(1)}, bf16[768,512]{1,0:T(8,128)(2,1)S(1)}, u32[]{:S(2)}, u32[]{:S(2)}) collective-permute-start(bf16[768,512]{1,0:T(8,128)(2,1)S(1)} %maximum_select_fusion.1.piece), channel_id=1, source_target_pairs={{0,2},{1,5},{2,0},{3,7},{4,6},{5,1},{6,4},{7,3},{8,10},{9,13},{10,... | collective-permute-start | bytes 2359304 | tf_op jit(solution)/shard_map/ppermute | solution.py:778
  208.9 0.9 copy-start.10
  (2 other events, 1.3 us)
where the time goes:
time: 214 us; the launch traced here: 213 us
  Pallas kernels  125 us (58%)
  starting transfers between devices  39.9 us (19%)
  waiting for transfers between devices  21.5 us (10%)
  other arithmetic  13.4 us (6%)
  local copies, waits for them, and re-layouts  12.5 us (6%)
    ppermute x25, starting transfers between devices, exchange(): return lax.ppermute(array, ('dp', 'tensor'), route)  36.3 us
    pallas_call x2, Pallas kernels, feed(): pl.pallas_call(kernel, grid_spec=pltpu.PrefetchScalarGridSpec(num_scalar_...  34 us
    pallas_call x2, Pallas kernels, scan_back(): pl.pallas_call(functools.partial(scan_kernel, windows, chunk), grid=(coun...  24.3 us
    pallas_call x1, Pallas kernels, forward(): pl.pallas_call(forward_kernel, grid_spec=pltpu.PrefetchScalarGridSpec(num...  19.7 us
    ppermute x25, waiting for transfers between devices, exchange(): return lax.ppermute(array, ('dp', 'tensor'), route)  19.3 us
    pallas_call x1, Pallas kernels, entry(): pl.pallas_call(entry_kernel, grid_spec=pltpu.PrefetchScalarGridSpec(num_s...  15.4 us
    pallas_call x1, Pallas kernels, norm_back(): pl.pallas_call(norm_kernel, grid=(rows // chunk,), in_specs=[row(width),...  11.8 us
    pallas_call x1, Pallas kernels, leave(): pl.pallas_call(leave_kernel, grid_spec=pltpu.PrefetchScalarGridSpec(num_s...  11.2 us
  transfers between devices with their start and end apart: 40, of which 11 were waited for; matrix products, arithmetic and copies ran while one was open for 4% of the time, Pallas kernels for 49%

commit v1 on v0

--- a/solution.py
+++ b/solution.py
@@ -80,7 +80,8 @@
     def _():
         tail[...] = jnp.zeros_like(tail)
         for at, start in enumerate((start_own, start_other)):
-            carry[:, at * channels : (at + 1) * channels] = jnp.broadcast_to(start[0], (8, channels))
+            row = start[pl.ds(core[0] * pl.num_programs(0) + pl.program_id(0), 1), :]
+            carry[:, at * channels : (at + 1) * channels] = jnp.broadcast_to(row, (8, channels))
 
     rim[edge:, :] = normed
     first = lax.broadcasted_iota(jnp.int32, (8, width), 0) == 0
@@ -191,10 +192,8 @@
                 whole(mixers[1]),
                 whole(biases[0]),
                 whole(biases[1]),
-                *[
-                    pl.BlockSpec((1, 1, channels), lambda w, t, core: (windows * core[0] + w, 0, 0))
-                    for _ in starts
-                ],
+                whole(starts[0]),
+                whole(starts[1]),
                 whole(reads[0]),
                 whole(reads[1]),
                 whole(gain_two),
@@ -266,7 +265,7 @@
                                 jnp.where(mine, own[window, rows_at, :], came[window, rows_at, :]),
                             ).astype(low)
 
-        sums = [jnp.zeros((8, block), wide), 0.0, 0.0]
+        total = jnp.zeros((8, block), wide)
         for at in range(0, rows, chunk):
             rows_at = slice(at, at + chunk)
             v = mm(normed_in[rows_at, :], up_in[...]) + bias_in[...]
@@ -277,15 +276,12 @@
             slope = s + (active * (1.0 - s)) * (2.0 * root + (6.0 * root * cubic) * square)
             back = back * slope
             for row in range(0, chunk, 8):
-                sums[0] = sums[0] + back[row : row + 8, :]
-            active_low, back_low = active.astype(low), back.astype(low)
-            active_out[rows_at, :] = active_low
-            back_out[rows_at, :] = back_low
-            sums[1] = sums[1] + mm_tn(tangent_in[rows_at, :], active_low)
-            sums[2] = sums[2] + mm_tn(normed_in[rows_at, :], back_low)
-        bias_out[...] = sums[0]
-        grad_out[0:width, :] = sums[1].astype(dtype)
-        grad_out[width:, :] = sums[2].astype(dtype)
+                total = total + back[row : row + 8, :]
+            active_out[rows_at, :] = active.astype(low)
+            back_out[rows_at, :] = back.astype(low)
+        bias_out[...] = total
+        grad_out[0:width, :] = mm_tn(tangent_in[...], active_out[...]).astype(dtype)
+        grad_out[width:, :] = mm_tn(normed_in[...], back_out[...]).astype(dtype)
 
     lanes = lambda count: pl.BlockSpec((count, block), lambda j, core: (0, j))
     in_specs = [whole(normed), lanes(width), lanes(1), pl.BlockSpec((block, width), lambda j, core: (j, 0))]
@@ -673,24 +669,37 @@
     )(*arrays)
 
 
-def finish_feed_kernel(bit, piece, got, down_out, up_out):
-    lead = bit[0] == 0
-    a, b = piece[...].astype(wide), got[...].astype(wide)
-    down_out[...] = jnp.where(lead, a, b).T
-    up_out[...] = jnp.where(lead, b, a)
-
-
-def finish_feed(bit, piece, got):
-    width, units = piece.shape
+def in_order(place, parts):
+    for at in range(len(parts).bit_length() - 1):
+        lead = place[at] == 0
+        parts = [
+            jnp.where(lead, parts[one], parts[one ^ (1 << at)]) for one in range(len(parts))
+        ]
+    return parts
+
+
+def finish_feed_kernel(place, *refs):
+    *shares, down_out, up_out = refs
+    total = jnp.concatenate(in_order(place, [share[...].astype(wide) for share in shares]))
+    width = up_out.shape[0]
+    down_out[...] = total[:width].T
+    up_out[...] = total[width:]
+
+
+def finish_feed(place, shares):
+    cut, units = shares[0].shape
+    width = cut * len(shares) // 2
     block = min(units, 512)
-    half = pl.BlockSpec((width, block), lambda j, bit: (0, j))
     return pl.pallas_call(
         finish_feed_kernel,
         grid_spec=pltpu.PrefetchScalarGridSpec(
             num_scalar_prefetch=1,
             grid=(units // block,),
-            in_specs=[half, half],
-            out_specs=[pl.BlockSpec((block, width), lambda j, bit: (j, 0)), half],
+            in_specs=[pl.BlockSpec((cut, block), lambda j, place: (0, j))] * len(shares),
+            out_specs=[
+                pl.BlockSpec((block, width), lambda j, place: (j, 0)),
+                pl.BlockSpec((width, block), lambda j, place: (0, j)),
+            ],
         ),
         out_shape=[
             jax.ShapeDtypeStruct((units, width), wide),
@@ -698,42 +707,49 @@
         ],
         compiler_params=params(60, 1),
         name="finish_feed",
-    )(bit, piece, got)
-
-
-def finish_mixer_kernel(bit, piece, got, mixer_out, read_out):
-    lead = bit[0] == 0
+    )(place, *shares)
+
+
+def finish_mixer_kernel(place, *refs):
+    *shares, mixer_out, read_out, gain_out, taps_out, gain_two_out, gate_out, up_out = refs
     width = mixer_out.shape[0]
-    cut = piece.shape[0]
-    a, b = piece[...].astype(wide), got[...].astype(wide)
-    a, b = jnp.where(lead, a, b), jnp.where(lead, b, a)
-    mixer_out[:, 0, :] = a[:width]
-    mixer_out[0 : cut - width, 1, :] = a[width:]
-    mixer_out[cut - width :, 1, :] = b[: 2 * width - cut]
-    read_out[...] = b[2 * width - cut :].T
-
-
-def finish_mixer(bit, piece, got):
-    cut, channels = piece.shape
-    width = 2 * cut // 3
+    cut = 3 * width // len(shares)
+    total = jnp.concatenate(in_order(place, [share[:cut, :].astype(wide) for share in shares]))
+    short = sum_alike([share[cut:, :] for share in shares])
+    row = 0
+    for out in (gain_out, taps_out, gain_two_out, gate_out, up_out):
+        for lane in range(0, out.shape[1], width):
+            some = min(width, out.shape[1])
+            out[:, lane : lane + some] = short[row : row + out.shape[0], :some]
+            row += out.shape[0]
+    mixer_out[:, 0, :] = total[:width]
+    mixer_out[:, 1, :] = total[width : 2 * width]
+    read_out[...] = total[2 * width :].T
+
+
+def finish_mixer(place, shares, width, taps, units):
+    channels = shares[0].shape[1]
+    short = [(1, width), (taps, width), (1, width), (1, channels), (1, units)]
     return pl.pallas_call(
         finish_mixer_kernel,
         grid_spec=pltpu.PrefetchScalarGridSpec(
             num_scalar_prefetch=1,
             grid=(1,),
-            in_specs=[whole(piece), whole(got)],
+            in_specs=[whole(share) for share in shares],
             out_specs=[
-                pl.BlockSpec((width, 2, channels), lambda j, bit: (0, 0, 0)),
-                pl.BlockSpec((channels, width), lambda j, bit: (0, 0)),
+                pl.BlockSpec((width, 2, channels), lambda j, place: (0, 0, 0)),
+                pl.BlockSpec((channels, width), lambda j, place: (0, 0)),
+                *[pl.BlockSpec(shape, lambda j, place: (0, 0)) for shape in short],
             ],
         ),
         out_shape=[
             jax.ShapeDtypeStruct((width, 2, channels), wide),
             jax.ShapeDtypeStruct((channels, width), wide),
+            *[jax.ShapeDtypeStruct(shape, wide) for shape in short],
         ],
         compiler_params=params(60, 1),
         name="finish_mixer",
-    )(bit, piece, got)
+    )(place, *shares)
 
 
 def partner(array):
@@ -745,17 +761,16 @@
 
 
 class DpSum:
+    paired = True
+
     def __init__(self, *terms):
         self.terms = terms
         self.piece = None
         count = lax.axis_size("dp").bit_length() - 1
         first = list(range(count))
-        if count >= 2:
-            groups = [((0,), (1,)), ((1,), (0,))] + [
-                (tuple(first[at : at + 2]),) * 2 for at in range(2, count, 2)
-            ]
-        else:
-            groups = [((bit,), (bit,)) for bit in first]
+        groups = [(tuple(first[at : at + 2]),) * 2 for at in range(0, count, 2)]
+        if self.paired and count >= 2:
+            groups[:1] = [((0,), (1,)), ((1,), (0,))]
         self.todo = [(False, group) for group in groups] + [(True, group) for group in groups[::-1]]
 
     def place(self, group):
@@ -820,31 +835,35 @@
         self.piece = parts[0]
 
 
-    def begin(self, piece):
-        self.sends = [piece]
-        self.start()
-        return self.got[0]
-
     def last(self):
         _, group = self.todo[0]
-        (bit,) = self.place(group)
-        return bit.reshape(1).astype(jnp.int32), self.piece, self.got[0]
-
-
-class DpSmall(DpSum):
-    def __init__(self, total):
-        super().__init__(total)
-        self.todo = [(join, (group[0], group[0])) for join, group in self.todo if not join]
+        return jnp.stack(self.place(group)).astype(jnp.int32), [self.sends[0], *self.got]
+
+
+class DpDirect(DpSum):
+    paired = False
+    rider = None
 
     def prepare(self):
-        self.sends = [self.terms[0]] * ((1 << len(self.todo[0][1][0])) - 1)
+        super().prepare()
+        self.rides = self.rider is not None and (not self.todo[0][0] or len(self.todo) == 1)
+        if self.rides:
+            self.low_rider = self.rider.astype(low)
+            self.sends = [jnp.concatenate([send, self.low_rider]) for send in self.sends]
 
     def finish(self):
-        _, group = self.todo.pop(0)
-        parts = [self.terms[0], *self.got]
-        while len(parts) > 1:
-            parts = [parts[at] + parts[at + 1] for at in range(0, len(parts), 2)]
-        self.terms = parts
+        if self.rides:
+            size = self.got[0].shape[0] - self.low_rider.shape[0]
+            self.rider = sum_alike([self.low_rider, *(got[size:] for got in self.got)])
+            self.got = [got[:size] for got in self.got]
+        super().finish()
+
+
+def sum_alike(parts):
+    parts = [part.astype(wide) for part in parts]
+    while len(parts) > 1:
+        parts = [parts[at] + parts[at + 1] for at in range(0, len(parts), 2)]
+    return parts[0]
 
 
 def beside(chains, work, *leads, loose=()):
@@ -896,7 +915,7 @@
     got_inputs = partner(other_windows(inputs))
     reads = (readout_weight, partner(readout_weight))
     biases = (gate_bias[None], partner(gate_bias)[None])
-    starts = (initial_state[:, None], partner(initial_state)[:, None])
+    starts = (initial_state, partner(initial_state))
     got_cotangent = partner(other_windows(cotangent))
     ups = (up_weight, partner(up_weight))
     up_biases = (up_bias[None], partner(up_bias)[None])
@@ -939,7 +958,7 @@
         [feed_sum], lambda lead: scan(0, lead, wide), mixed
     )
     mixer_own, mixer_got = hold(mixer_own, mixer_got)
-    mixer_sum = DpSum(mixer_own, mixer_got)
+    mixer_sum = DpDirect(mixer_own, mixer_got)
     def put_back(whole_rows, got):
         return lax.dynamic_update_slice_in_dim(whole_rows, got, (1 - core) * windows, 0)
 
@@ -951,20 +970,18 @@
         ),
         gate_own,
     )
-    def turn(gain_grad, taps_grad, state_other, grad_sent):
-        short, sent = pack(
-            width, gain_grad, taps_grad, gain_two_grad, bias_own, bias_other, up_bias_own, up_bias_other
-        )
-        return short + partner(sent), partner(state_other), partner(grad_sent)
-
-    short, state_got, grad_got = beside(
-        [mixer_sum], turn, gain_grad, taps_grad, state_other[:, 0], grad_sent
-    )
-    short_sum = DpSmall(short)
-    out_mine, out_sent = beside(
-        [feed_sum, mixer_sum, short_sum],
-        lambda lead: leave(windows, core_at, orders[1], [lead, active_other], middle, downs),
-        active_own,
+    short, sent = pack(
+        width, gain_grad, taps_grad, gain_two_grad, bias_own, bias_other, up_bias_own, up_bias_other
+    )
+
+    mixer_sum.rider = short + partner(sent)
+
+    def leave_all(lead, state_other, grad_sent):
+        moved = [partner(array) for array in (state_other, grad_sent)]
+        return *leave(windows, core_at, orders[1], [lead, active_other], middle, downs), *moved
+
+    out_mine, out_sent, state_got, grad_got = beside(
+        [feed_sum, mixer_sum], leave_all, active_own, state_other[:, 0], grad_sent
     )
 
     def exits(grad_mine, grad_got, state_own, state_got, out_sent):
@@ -975,46 +992,47 @@
         )
         return put_back(grad_mine, grad_got), state_gradient, partner(out_sent)
 
-    input_gradient, state_gradient, out_got = beside(
-        [mixer_sum, short_sum], exits, grad_mine, grad_got, state_own[:, 0], state_got, out_sent,
-        loose=[feed_sum],
-    )
-    while len(mixer_sum.todo) > 1 or short_sum.todo:
-        beside([mixer_sum, short_sum], lambda: ())
-
-    def feed_results(mine, got, *gots):
-        feed_sum.got = list(gots)
+    last = len(feed_sum.todo) == 1
+    if last:
+        feed_sum.prepare()
+        feed_sum.start()
+    input_gradient, state_gradient, out_got, *feed_got = beside(
+        [mixer_sum],
+        lambda *leads: (*exits(*leads), *(feed_sum.got if last else ())),
+        grad_mine, grad_got, state_own[:, 0], state_got, out_sent,
+    )
+    while len(mixer_sum.todo) > 1:
+        beside([mixer_sum], lambda: ())
+
+    mixer_sum.prepare()
+    (mixer_send, *feed_got) = hold(mixer_sum.sends[0], *feed_got)
+    mixer_sum.sends = [mixer_send]
+    mixer_sum.start()
+    if last:
+        feed_sum.got = list(feed_got)
+    else:
         while len(feed_sum.todo) > 1:
-            feed_sum.finish()
-            feed_sum.prepare()
-            feed_sum.start()
-        return put_back(mine, got), *finish_feed(*feed_sum.last())
-
-    block_output, down_sum, up_sum, mixer_last = beside(
-        [],
-        lambda *leads: (*feed_results(*leads[:-1]), mixer_sum.begin(leads[-1])),
-        out_mine,
-        out_got,
-        *feed_sum.got,
-        mixer_sum.piece,
-    )
-    mixer_sum.got = [mixer_last]
-    mixer_grad, read_grad = finish_mixer(*mixer_sum.last())
-    short_sum = short_sum.terms[0]
-    taps = causal_filter.shape[0]
-    end = taps + 3 + units // width
+            beside([feed_sum], lambda: ())
+        feed_sum.prepare()
+        feed_sum.start()
+    down_sum, up_sum = finish_feed(*feed_sum.last())
+    block_output = put_back(out_mine, out_got)
+    mixer_sum.got = list(hold(*mixer_sum.got, down_sum, block_output)[: len(mixer_sum.got)])
+    mixer_grad, read_grad, gain_sum, taps_sum, gain_two_sum, gate_bias_sum, up_bias_sum = finish_mixer(
+        *mixer_sum.last(), width, causal_filter.shape[0], units
+    )
     return (
         block_output,
         input_gradient,
         state_gradient,
-        short_sum[0],
-        short_sum[1 : 1 + taps],
+        gain_sum[0],
+        taps_sum,
         mixer_grad,
-        short_sum[taps + 2, :channels],
+        gate_bias_sum[0],
         read_grad,
-        short_sum[taps + 1],
+        gain_two_sum[0],
         up_sum,
-        short_sum[taps + 3 : end].reshape(units),
+        up_bias_sum[0],
         down_sum,
     )
 

time: 214 us -> 206 us (0.963)
  starting transfers between devices: 39.9 us -> 35.3 us
  local copies, waits for them, and re-layouts: 12.5 us -> 8.75 us
    ppermute x25 -> x22, starting transfers between devices: 36.3 us -> 31.9 us  [exchange(): return lax.ppermute(array, ('dp', 'tensor'), route)]
    unnamed x57 -> x67, local copies, waits for them, and re-layouts: 6.5 us -> 5.13 us
    ppermute x25 -> x22, waiting for transfers between devices: 19.3 us -> 20.1 us  [exchange(): return lax.ppermute(array, ('dp', 'tensor'), route)]
  transfers between devices with their start and end apart: 40 -> 37, of which waited for: 11 -> 11; matrix products, arithmetic and copies ran while one was open for 4% -> 3% of each run, Pallas kernels for 49% -> 49%
where the time goes in v1:
time: 206 us
  Pallas kernels  125 us (61%)
  starting transfers between devices  35.3 us (17%)
  waiting for transfers between devices  23.2 us (11%)
  other arithmetic  12.9 us (6%)
  local copies, waits for them, and re-layouts  8.75 us (4%)
    pallas_call x2, Pallas kernels, feed(): pl.pallas_call(kernel, grid_spec=pltpu.PrefetchScalarGridSpec(num_scalar_...  32.6 us
    ppermute x22, starting transfers between devices, exchange(): return lax.ppermute(array, ('dp', 'tensor'), route)  31.9 us
    pallas_call x2, Pallas kernels, scan_back(): pl.pallas_call(functools.partial(scan_kernel, windows, chunk), grid=(coun...  24.3 us
    ppermute x22, waiting for transfers between devices, exchange(): return lax.ppermute(array, ('dp', 'tensor'), route)  20.1 us
    pallas_call x1, Pallas kernels, forward(): pl.pallas_call(forward_kernel, grid_spec=pltpu.PrefetchScalarGridSpec(num...  19.6 us
    pallas_call x1, Pallas kernels, entry(): pl.pallas_call(entry_kernel, grid_spec=pltpu.PrefetchScalarGridSpec(num_s...  15.4 us
    pallas_call x1, Pallas kernels, norm_back(): pl.pallas_call(norm_kernel, grid=(rows // chunk,), in_specs=[row(width),...  11.8 us
    pallas_call x1, Pallas kernels, leave(): pl.pallas_call(leave_kernel, grid_spec=pltpu.PrefetchScalarGridSpec(num_s...  11.2 us
  transfers between devices with their start and end apart: 37, of which 11 were waited for; matrix products, arithmetic and copies ran while one was open for 3% of the time, Pallas kernels for 49%

profile of v1, /device:TPU:0, one launch (start us, length us, event | category | flops | bytes accessed | tf_op | source)
XLA Modules:
  0.0 205.9 jit_solution(18243569162067561726)
XLA Ops:
  0.7 1.4 constant_dynamic-slice_fusion.1
  2.2 0.5 collective-permute-start
  2.7 0.2 copy.26
  3.1 0.5 collective-permute-start.4
  3.6 0.4 collective-permute-start.2
  4.0 1.0 constant_dynamic-slice_fusion
  5.1 2.2 %collective-permute-done.2 = f32[512]{0:T(512)S(1)} collective-permute-done((f32[512]{0:T(512)S(1)}, f32[512]{0:T(512)S(1)}, u32[]{:S(2)}, u32[]{:S(2)}) %collective-permute-start.2) | collective-permute-done | bytes 2080 | tf_op jit(solution)/shard_map/ppermute | solution.py:756
  7.2 0.4 collective-permute-start.5
  7.8 0.4 collective-permute-start.8
  8.4 0.8 copy-done.8
  9.2 1.0 copy-done.9
  10.2 19.6 %forward_mixer.1 = (bf16[2048,512]{1,0:T(8,128)(2,1)}, f32[2048,1024]{1,0:T(8,128)}, bf16[2048,1024]{1,0:T(8,128)(2,1)}, bf16[2048,1024]{1,0:T(8,128)(2,1)}, bf1...) custom-call(s32[1]{0:T(128)} %bitcast.core, ...), custom_call_target="tpu_custom_call" | custom-call | flops 6442450944 | bytes 25165824 | tf_op jit(solution)/shard_map/forward_mixer/pallas_call | solution.py:182
  29.9 0.5 copy-done.29
  30.4 0.4 copy-done.5
  30.8 17.5 %feed_forward.2 = (bf16[2048,1024]{1,0:T(8,128)(2,1)}, bf16[2048,1024]{1,0:T(8,128)(2,1)}, f32[8,1024]{1,0:T(8,128)}, bf16[1024,1024]{1,0:T(8,128)(2,1)}, bf16[2048,512]{1,0:T(8,128)(2,1)}) custom-call(s32[1]{0:T(128)} %bitcast.core, bf16[4,512,512]{2,1,0:T(8,128)(2,1)} %refs_0_.1, bf16[2,512,512]{2,1,0:T(8,128)(2,1)} %collective-permute-done.5.refs_1_, ...), custom_call_target="tpu_custom_call" | custom-call | flops 8589934592 | bytes 8388608 | tf_op jit(solution)/shard_map/feed_forward/pallas_call | solution.py:308
  48.5 15.1 %feed_forward.3 = (bf16[2048,1024]{1,0:T(8,128)(2,1)}, bf16[2048,1024]{1,0:T(8,128)(2,1)}, f32[8,1024]{1,0:T(8,128)}, f32[1024,1024]{1,0:T(8,128)}) custom-call(s32[1]{0:T(128)} %bitcast.core, bf16[2048,512]{1,0:T(8,128)(2,1)} %get-tuple-element.147.refs_0_.tangent, bf16[2048,512]{1,0:T(8,128)(2,1)} %get-tuple-element.144.refs_3_.refs_1_, ...), custom_call_target="tpu_custom_call" | custom-call | flops 8589934592 | bytes 8388608 | tf_op jit(solution)/shard_map/feed_forward/pallas_call | solution.py:308
  63.6 1.3 copy-done.2
  64.9 3.5 %convert_add_fusion = (f32[512,1024]{1,0:T(8,128)S(1)}, bf16[512,1024]{1,0:T(8,128)(2,1)S(1)}) fusion(f32[1024,1024]{1,0:T(8,128)} %get-tuple-element.152, s32[]{:T(128)S(6)} %select_n.158, bf16[1024,1024]{1,0:T(8,128)(2,1)} %copy-done.2, s32[]{:T(128)S(6)} %select_n.157), kind=kLoop, calls=%fused_computation | loop fusion | flops 2621440 | bytes 9437192 | tf_op jit(solution)/shard_map/add | solution.py:810
  68.4 2.8 %collective-permute-start.10 = (bf16[512,1024]{1,0:T(8,128)(2,1)S(1)}, bf16[512,1024]{1,0:T(8,128)(2,1)}, u32[]{:S(2)}, u32[]{:S(2)}) collective-permute-start(bf16[512,1024]{1,0:T(8,128)(2,1)S(1)} %get-tuple-element.160), channel_id=1, source_target_pairs={{0,2},{1,5},{2,0},{3,7},{4,6},{5,1},{6,4},{7,3},{8,10},{9,13},{10,... | collective-permute-start | bytes 3145736 | tf_op jit(solution)/shard_map/ppermute | solution.py:793
  71.2 11.8 %norm_back.1 = (f32[2048,512]{1,0:T(8,128)}, bf16[2048,512]{1,0:T(8,128)(2,1)}, f32[1,512]{1,0:T(1,128)}) custom-call(bf16[2048,512]{1,0:T(8,128)(2,1)} %get-tuple-element.147.refs_0_.tangent, bf16[2048,1024]{1,0:T(8,128)(2,1)} %get-tuple-element.154.back_own, bf16[2048,1024]{1,0:T(8,128)(2,1)} %get-tuple-element.155.back_other, ...), custom_call_target="tpu_custom_call" | custom-call | flops 4294967296 | bytes 25165824 | tf_op jit(solution)/shard_map/norm_back/pallas_call | solution.py:349
  83.0 1.1 collective-permute-done.10
  84.1 1.6 convert_add_fusion.1
  85.7 2.1 %collective-permute-start.11 = (bf16[256,1024]{1,0:T(8,128)(2,1)S(1)}, bf16[256,1024]{1,0:T(8,128)(2,1)S(1)}, u32[]{:S(2)}, u32[]{:S(2)}) collective-permute-start(bf16[256,1024]{1,0:T(8,128)(2,1)S(1)} %get-tuple-element.174), channel_id=1, source_target_pairs={{0,4},{1,3},{2,6},{3,1},{4,0},{5,7},{6,2},{7,5},{8,12},{9,11},{10,... | collective-permute-start | bytes 1572872 | tf_op jit(solution)/shard_map/ppermute | solution.py:793
  87.8 11.9 %scan_back.2 = (bf16[2048,512]{1,0:T(8,128)(2,1)}, bf16[2048,512]{1,0:T(8,128)(2,1)}, f32[2,1,512]{2,1,0:T(1,128)}, f32[8,512]{1,0:T(8,128)}, bf16[1536,512]{1,0:T(8,128)(2,1)}) custom-call(bf16[2048,512]{1,0:T(8,128)(2,1)} %get-tuple-element.179.mixed, bf16[2048,512]{1,0:T(8,128)(2,1)} %get-tuple-element.164.filtered, bf16[512,512]{1,0:T(8,128)(2,1)} %copy-done.11, ...), custom_call_target="tpu_custom_call" | custom-call | flops 4294967296 | bytes 14680064 | tf_op jit(solution)/shard_map/scan_back/pallas_call | solution.py:439
  99.9 1.6 collective-permute-start.12
  101.6 2.6 %collective-permute-start.13 = (bf16[64,1024]{1,0:T(8,128)(2,1)S(1)}, bf16[64,1024]{1,0:T(8,128)(2,1)S(1)}, u32[]{:S(2)}, u32[]{:S(2)}) collective-permute-start(bf16[64,1024]{1,0:T(8,128)(2,1)S(1)} %get-tuple-element.186), channel_id=1, source_target_pairs={{0,16},{1,17},{2,18},{3,19},{4,20},{5,21},{6,22},{7,23},{8,24},{9,... | collective-permute-start | bytes 393224 | tf_op jit(solution)/shard_map/ppermute | solution.py:793
  104.4 12.4 %scan_back.3 = (bf16[2048,512]{1,0:T(8,128)(2,1)}, bf16[2048,512]{1,0:T(8,128)(2,1)}, f32[2,1,512]{2,1,0:T(1,128)}, f32[8,512]{1,0:T(8,128)}, f32[1536,512]{1,0:T(8,128)}) custom-call(bf16[2048,512]{1,0:T(8,128)(2,1)} %get-tuple-element.179.mixed, bf16[2048,512]{1,0:T(8,128)(2,1)} %get-tuple-element.164.filtered, bf16[512,512]{1,0:T(8,128)(2,1)} %read.1, ...), custom_call_target="tpu_custom_call" | custom-call | flops 4294967296 | bytes 14680064 | tf_op jit(solution)/shard_map/scan_back/pallas_call | solution.py:439
  117.0 3.3 %convert_add_fusion.2 = (f32[384,512]{1,0:T(8,128)S(1)}, bf16[384,512]{1,0:T(8,128)(2,1)S(1)}, bf16[384,512]{1,0:T(8,128)(2,1)}, bf16[384,512]{1,0:T(8,128)(2,1)}) fusion(f32[1536,512]{1,0:T(8,128)} %get-tuple-element.194, s32[]{:T(128)S(6)} %select_n.174, bf16[1536,512]{1,0:T(8,128)(2,1)S(1)} %collective-permute-done.15, s32[]{:T(128)S(6)} %select_n.168, ...), kind=kLoop, calls=%fused_computation.5 | loop fusion | flops 2162688 | bytes 6684688 | tf_op jit(solution)/shard_map/add | solution.py:810
  120.3 0.6 collective-permute-start.16
  120.9 3.4 %collective-permute-start.17 = (bf16[64,1024]{1,0:T(8,128)(2,1)S(1)}, bf16[64,1024]{1,0:T(8,128)(2,1)S(1)}, u32[]{:S(2)}, u32[]{:S(2)}) collective-permute-start(bf16[64,1024]{1,0:T(8,128)(2,1)S(1)} %add_convert_fusion.5), channel_id=1, source_target_pairs={{0,16},{1,17},{2,18},{3,19},{4,20},{5,21},{6,22},{7,23},{8,24},{9,... | collective-permute-start | bytes 393224 | tf_op jit(solution)/shard_map/ppermute | solution.py:793
  124.3 0.4 collective-permute-start.18
  124.7 1.5 collective-permute-start.19
  126.1 0.5 collective-permute-start.20
  126.7 0.4 collective-permute-done.16
  127.1 1.4 collective-permute-start.21
  128.5 15.4 %input_gradient.1 = (bf16[4,512,512]{2,1,0:T(8,128)(2,1)}, bf16[2,512,512]{2,1,0:T(8,128)(2,1)}, f32[1,512]{1,0:T(1,128)}, f32[4,512]{1,0:T(4,128)}) custom-call(s32[1]{0:T(128)} %bitcast.core, bf16[4,512,512]{2,1,0:T(8,128)(2,1)} %own.3, bf16[2,512,512]{2,1,0:T(8,128)(2,1)} %copy-done.8, bf16[512,512]{1,0:T(8,128)(2,1)} %get-tuple-element.143.refs_2_.order, ...), custom_call_target="tpu_custom_call" | custom-call | flops 4294967296 | bytes 12582912 | tf_op jit(solution)/shard_map/input_gradient/pallas_call | solution.py:563
  144.0 0.4 collective-permute-done.20
  144.4 1.8 pack_short.1
  146.7 0.9 collective-permute-done.22
  148.0 1.1 collective-permute-start.25
  149.2 4.0 %collective-permute-start.27 = (bf16[112,512]{1,0:T(8,128)(2,1)S(1)}, bf16[112,512]{1,0:T(8,128)(2,1)S(1)}, u32[]{:S(2)}, u32[]{:S(2)}) collective-permute-start(bf16[112,512]{1,0:T(8,128)(2,1)S(1)} %get-tuple-element.233), channel_id=1, source_target_pairs={{0,16},{1,17},{2,18},{3,19},{4,20},{5,21},{6,22},{7,23},{8,24},{9,... | collective-permute-start | bytes 344072 | tf_op jit(solution)/shard_map/ppermute | solution.py:793
  153.2 0.6 collective-permute-start.28
  153.8 11.2 %block_output.1 = (bf16[4,512,512]{2,1,0:T(8,128)(2,1)}, bf16[2,512,512]{2,1,0:T(8,128)(2,1)}) custom-call(s32[1]{0:T(128)} %bitcast.core, bf16[512,512]{1,0:T(8,128)(2,1)} %get-tuple-element.142.back_order, bf16[2048,1024]{1,0:T(8,128)(2,1)} %get-tuple-element.225.active_own, bf16[2048,1024]{1,0:T(8,128)(2,1)} %get-tuple-element.226.active_other, ...), custom_call_target="tpu_custom_call" | custom-call | flops 4294967296 | bytes 12582912 | tf_op jit(solution)/shard_map/block_output/pallas_call | solution.py:621
  165.0 0.5 maximum_select_fusion.refs_0_
  165.5 0.9 collective-permute-start.30
  166.5 1.1 add_convert_fusion.9
  167.7 3.7 %collective-permute-start.32 = (bf16[96,512]{1,0:T(8,128)(2,1)S(1)}, bf16[96,512]{1,0:T(8,128)(2,1)S(1)}, u32[]{:S(2)}, u32[]{:S(2)}) collective-permute-start(bf16[96,512]{1,0:T(8,128)(2,1)S(1)} %add_convert_fusion.9), channel_id=1, source_target_pairs={{0,16},{1,17},{2,18},{3,19},{4,20},{5,21},{6,22},{7,23},{8,24},{9,... | collective-permute-start | bytes 294920 | tf_op jit(solution)/shard_map/ppermute | solution.py:793
  171.4 0.7 collective-permute-start.33
  172.2 0.8 add_convert_fusion.13
  173.0 0.6 maximum_select_fusion.7
  173.6 1.0 collective-permute-done.31
  174.6 4.6 %collective-permute-done.32 = bf16[96,512]{1,0:T(8,128)(2,1)S(1)} collective-permute-done((bf16[96,512]{1,0:T(8,128)(2,1)S(1)}, bf16[96,512]{1,0:T(8,128)(2,1)S(1)}, u32[]{:S(2)}, u32[]{:S(2)}) %collective-permute-start.32) | collective-permute-done | bytes 98336 | tf_op jit(solution)/shard_map/ppermute | solution.py:793
  179.2 1.2 collective-permute-done.30.refs_1_
  180.7 0.9 collective-permute-start.34
  181.6 1.0 collective-permute-start.35
  182.6 1.7 collective-permute-start.36
  184.2 0.6 pad_add_fusion.place
  184.9 3.4 %finish_feed.1 = (f32[1024,512]{1,0:T(8,128)}, f32[512,1024]{1,0:T(8,128)}) custom-call(s32[1]{0:T(128)} %bitcast.9.place, bf16[512,1024]{1,0:T(8,128)(2,1)} %copy-done, bf16[512,1024]{1,0:T(8,128)(2,1)} %copy-done.6), custom_call_target="tpu_custom_call" | custom-call | tf_op jit(solution)/shard_map/finish_feed/pallas_call | solution.py:693
  188.3 1.0 constant_dynamic-update-slice_fusion.1
  189.3 3.9 %collective-permute-done.34.refs_1_ = bf16[400,512]{1,0:T(8,128)(2,1)S(1)} collective-permute-done((bf16[400,512]{1,0:T(8,128)(2,1)S(1)}, bf16[400,512]{1,0:T(8,128)(2,1)S(1)}, u32[]{:S(2)}, u32[]{:S(2)}) %collective-permute-start.34) | collective-permute-done | bytes 409632 | tf_op jit(solution)/shard_map/ppermute | solution.py:793
  193.2 0.5 collective-permute-done.35.refs_2_
  193.6 7.0 %collective-permute-done.36.refs_3_ = bf16[400,512]{1,0:T(8,128)(2,1)S(1)} collective-permute-done((bf16[400,512]{1,0:T(8,128)(2,1)S(1)}, bf16[400,512]{1,0:T(8,128)(2,1)S(1)}, u32[]{:S(2)}, u32[]{:S(2)}) %collective-permute-start.36) | collective-permute-done | bytes 409632 | tf_op jit(solution)/shard_map/ppermute | solution.py:793
  200.6 0.7 copy-done.15
  201.4 4.5 %finish_mixer.1 = (f32[512,2,512]{2,1,0:T(2,128)}, f32[512,512]{1,0:T(8,128)}, f32[1,512]{1,0:T(1,128)}, f32[4,512]{1,0:T(4,128)}, f32[1,512]{1,0:T(1,128)}, /*index=5*/f32[1,512]{1,0:T(1,128)}, f32[1,1024]{1,0:T(1,128)}) custom-call(s32[2]{0:T(128)} %pad_add_fusion.place, bf16[400,512]{1,0:T(8,128)(2,1)} %copy-done.3, bf16[400,512]{1,0:T(8,128)(2,1)} %copy-done.13, ...), custom_call_target="tpu_custom_call" | custom-call | tf_op jit(solution)/shard_map/finish_mixer/pallas_call | solution.py:733
  (111 shorter events, 2.8 us)
Async XLA Ops:
  0.6 2.0 copy-start.7
  0.7 2.4 %copy-start.10 = (bf16[512,512]{1,0:T(8,128)(2,1)S(1)}, bf16[512,512]{1,0:T(8,128)(2,1)}, u32[]{:S(2)}) copy-start(bf16[512,512]{1,0:T(8,128)(2,1)} %read.1) | copy-start | bytes 1572868
  0.7 2.9 %copy-start.26 = (f32[4,512]{1,0:T(4,128)S(1)}, f32[4,512]{1,0:T(4,128)}, u32[]{:S(2)}) copy-start(f32[4,512]{1,0:T(4,128)} %start_own.1) | copy-start | bytes 24580
  0.7 2.9 %copy-start.30 = (f32[512]{0:T(512)S(1)}, f32[512]{0:T(512)}, u32[]{:S(2)}) copy-start(f32[512]{0:T(512)} %param.17) | copy-start | bytes 6148
  0.7 3.3 %copy-start.12 = (bf16[4,512,512]{2,1,0:T(8,128)(2,1)S(1)}, bf16[4,512,512]{2,1,0:T(8,128)(2,1)}, u32[]{:S(2)}) copy-start(bf16[4,512,512]{2,1,0:T(8,128)(2,1)} %refs_0_.1) | copy-start | bytes 6291460
  2.2 6.0 %collective-permute-start = (bf16[2,512,512]{2,1,0:T(8,128)(2,1)S(1)}, bf16[2,512,512]{2,1,0:T(8,128)(2,1)S(1)}, u32[]{:S(2)}, u32[]{:S(2)}) collective-permute-start(bf16[2,512,512]{2,1,0:T(8,128)(2,1)S(1)} %constant_dynamic-slice_fusion.1), channel_id=1, source_target_pairs={{0,1},{1,0},{2,3},{3,2},{4,5},{5,4},{6,7},{7,6},{8,9},{9,8},{10,11... | collective-permute-start | bytes 3145736 | tf_op jit(solution)/shard_map/ppermute | solution.py:756
  2.7 4.9 %copy-start.4 = (bf16[512,1024]{1,0:T(8,128)(2,1)S(1)}, bf16[512,1024]{1,0:T(8,128)(2,1)}, u32[]{:S(2)}) copy-start(bf16[512,1024]{1,0:T(8,128)(2,1)} %up_own.1) | copy-start | bytes 3145732
  2.7 5.5 %copy-start.28 = (f32[1024]{0:T(1024)S(1)}, f32[1024]{0:T(1024)}, u32[]{:S(2)}) copy-start(f32[1024]{0:T(1024)} %param.21) | copy-start | bytes 12292
  2.9 7.2 %copy-start.1 = (bf16[64,8,2,512]{3,1,2,0:T(8,128)(2,1)}, bf16[64,8,2,512]{3,1,2,0:T(8,128)(2,1)S(1)}, u32[]{:S(2)}) copy-start(bf16[64,8,2,512]{3,1,2,0:T(8,128)(2,1)S(1)} %copy.26) | copy-start | bytes 3145732
  2.9 5.5 %collective-permute-start.1 = (bf16[512,1024]{1,0:T(8,128)(2,1)S(1)}, bf16[512,1024]{1,0:T(8,128)(2,1)S(1)}, u32[]{:S(2)}, u32[]{:S(2)}) collective-permute-start(bf16[512,1024]{1,0:T(8,128)(2,1)S(1)} %bitcast.22), channel_id=1, source_target_pairs={{0,1},{1,0},{2,3},{3,2},{4,5},{5,4},{6,7},{7,6},{8,9},{9,8},{10,11... | collective-permute-start | bytes 3145736 | tf_op jit(solution)/shard_map/ppermute | solution.py:756
  3.1 4.7 %collective-permute-start.4 = (bf16[512,512]{1,0:T(8,128)(2,1)S(1)}, bf16[512,512]{1,0:T(8,128)(2,1)S(1)}, u32[]{:S(2)}, u32[]{:S(2)}) collective-permute-start(bf16[512,512]{1,0:T(8,128)(2,1)S(1)} %copy-done.10), channel_id=1, source_target_pairs={{0,1},{1,0},{2,3},{3,2},{4,5},{5,4},{6,7},{7,6},{8,9},{9,8},{10,11... | collective-permute-start | bytes 1572872 | tf_op jit(solution)/shard_map/ppermute | solution.py:756
  3.5 4.1 %collective-permute-start.3 = (f32[4,512]{1,0:T(4,128)S(1)}, f32[4,512]{1,0:T(4,128)S(1)}, u32[]{:S(2)}, u32[]{:S(2)}) collective-permute-start(f32[4,512]{1,0:T(4,128)S(1)} %copy-done.26), channel_id=1, source_target_pairs={{0,1},{1,0},{2,3},{3,2},{4,5},{5,4},{6,7},{7,6},{8,9},{9,8},{10,11... | collective-permute-start | bytes 24584 | tf_op jit(solution)/shard_map/ppermute | solution.py:756
  3.6 3.6 %collective-permute-start.2 = (f32[512]{0:T(512)S(1)}, f32[512]{0:T(512)S(1)}, u32[]{:S(2)}, u32[]{:S(2)}) collective-permute-start(f32[512]{0:T(512)S(1)} %copy-done.30), channel_id=1, source_target_pairs={{0,1},{1,0},{2,3},{3,2},{4,5},{5,4},{6,7},{7,6},{8,9},{9,8},{10,11... | collective-permute-start | bytes 6152 | tf_op jit(solution)/shard_map/ppermute | solution.py:756
  7.2 2.9 %copy-start.31 = (f32[512]{0:T(512)}, f32[512]{0:T(512)S(1)}, u32[]{:S(2)}) copy-start(f32[512]{0:T(512)S(1)} %collective-permute-done.2) | copy-start | bytes 6148
  7.2 22.6 %collective-permute-start.5 = (bf16[2,512,512]{2,1,0:T(8,128)(2,1)}, bf16[2,512,512]{2,1,0:T(8,128)(2,1)}, u32[]{:S(2)}, u32[]{:S(2)}) collective-permute-start(bf16[2,512,512]{2,1,0:T(8,128)(2,1)} %constant_dynamic-slice_fusion), channel_id=1, source_target_pairs={{0,1},{1,0},{2,3},{3,2},{4,5},{5,4},{6,7},{7,6},{8,9},{9,8},{10,11... | collective-permute-start | bytes 3145736 | tf_op jit(solution)/shard_map/ppermute | solution.py:756
  7.6 2.6 %copy-start.27 = (f32[4,512]{1,0:T(4,128)}, f32[4,512]{1,0:T(4,128)S(1)}, u32[]{:S(2)}) copy-start(f32[4,512]{1,0:T(4,128)S(1)} %collective-permute-done.3.start_other) | copy-start | bytes 24580
  7.6 22.2 %collective-permute-start.6 = (bf16[512,1024]{1,0:T(8,128)(2,1)S(1)}, bf16[512,1024]{1,0:T(8,128)(2,1)S(1)}, u32[]{:S(2)}, u32[]{:S(2)}) collective-permute-start(bf16[512,1024]{1,0:T(8,128)(2,1)S(1)} %copy-done.4), channel_id=1, source_target_pairs={{0,1},{1,0},{2,3},{3,2},{4,5},{5,4},{6,7},{7,6},{8,9},{9,8},{10,11... | collective-permute-start | bytes 3145736 | tf_op jit(solution)/shard_map/ppermute | solution.py:756
  7.8 2.3 %copy-start.11 = (bf16[512,512]{1,0:T(8,128)(2,1)}, bf16[512,512]{1,0:T(8,128)(2,1)S(1)}, u32[]{:S(2)}) copy-start(bf16[512,512]{1,0:T(8,128)(2,1)S(1)} %collective-permute-done.4.read_other.read) | copy-start | bytes 1572868
  7.8 22.0 %collective-permute-start.8 = (bf16[1024,512]{1,0:T(8,128)(2,1)}, bf16[1024,512]{1,0:T(8,128)(2,1)}, u32[]{:S(2)}, u32[]{:S(2)}) collective-permute-start(bf16[1024,512]{1,0:T(8,128)(2,1)} %down_own.1), channel_id=1, source_target_pairs={{0,1},{1,0},{2,3},{3,2},{4,5},{5,4},{6,7},{7,6},{8,9},{9,8},{10,11... | collective-permute-start | bytes 3145736 | tf_op jit(solution)/shard_map/ppermute | solution.py:756
  8.2 21.6 %collective-permute-start.7 = (f32[1024]{0:T(1024)S(1)}, f32[1024]{0:T(1024)S(1)}, u32[]{:S(2)}, u32[]{:S(2)}) collective-permute-start(f32[1024]{0:T(1024)S(1)} %copy-done.28), channel_id=1, source_target_pairs={{0,1},{1,0},{2,3},{3,2},{4,5},{5,4},{6,7},{7,6},{8,9},{9,8},{10,11... | collective-permute-start | bytes 12296 | tf_op jit(solution)/shard_map/ppermute | solution.py:756
  48.4 15.2 %collective-permute-start.9 = (bf16[1024,1024]{1,0:T(8,128)(2,1)}, bf16[1024,1024]{1,0:T(8,128)(2,1)S(1)}, u32[]{:S(2)}, u32[]{:S(2)}) collective-permute-start(bf16[1024,1024]{1,0:T(8,128)(2,1)} %get-tuple-element.151), channel_id=1, source_target_pairs={{0,1},{1,0},{2,3},{3,2},{4,5},{5,4},{6,7},{7,6},{8,9},{9,8},{10,11... | collective-permute-start | bytes 6291464 | tf_op jit(solution)/shard_map/ppermute | solution.py:756
  63.6 1.3 copy-start.2
  68.4 15.7 %collective-permute-start.10 = (bf16[512,1024]{1,0:T(8,128)(2,1)S(1)}, bf16[512,1024]{1,0:T(8,128)(2,1)}, u32[]{:S(2)}, u32[]{:S(2)}) collective-permute-start(bf16[512,1024]{1,0:T(8,128)(2,1)S(1)} %get-tuple-element.160), channel_id=1, source_target_pairs={{0,2},{1,5},{2,0},{3,7},{4,6},{5,1},{6,4},{7,3},{8,10},{9,13},{10,... | collective-permute-start | bytes 3145736 | tf_op jit(solution)/shard_map/ppermute | solution.py:793
  85.7 14.0 %collective-permute-start.11 = (bf16[256,1024]{1,0:T(8,128)(2,1)S(1)}, bf16[256,1024]{1,0:T(8,128)(2,1)S(1)}, u32[]{:S(2)}, u32[]{:S(2)}) collective-permute-start(bf16[256,1024]{1,0:T(8,128)(2,1)S(1)} %get-tuple-element.174), channel_id=1, source_target_pairs={{0,4},{1,3},{2,6},{3,1},{4,0},{5,7},{6,2},{7,5},{8,12},{9,11},{10,... | collective-permute-start | bytes 1572872 | tf_op jit(solution)/shard_map/ppermute | solution.py:793
  99.7 17.3 %collective-permute-start.15 = (bf16[1536,512]{1,0:T(8,128)(2,1)}, bf16[1536,512]{1,0:T(8,128)(2,1)S(1)}, u32[]{:S(2)}, u32[]{:S(2)}) collective-permute-start(bf16[1536,512]{1,0:T(8,128)(2,1)} %get-tuple-element.193), channel_id=1, source_target_pairs={{0,1},{1,0},{2,3},{3,2},{4,5},{5,4},{6,7},{7,6},{8,9},{9,8},{10,11... | collective-permute-start | bytes 4718600 | tf_op jit(solution)/shard_map/ppermute | solution.py:756
  99.9 16.9 %collective-permute-start.12 = (bf16[64,1024]{1,0:T(8,128)(2,1)S(1)}, bf16[64,1024]{1,0:T(8,128)(2,1)S(1)}, u32[]{:S(2)}, u32[]{:S(2)}) collective-permute-start(bf16[64,1024]{1,0:T(8,128)(2,1)S(1)} %get-tuple-element.185), channel_id=1, source_target_pairs={{0,8},{1,9},{2,10},{3,11},{4,12},{5,13},{6,14},{7,15},{8,0},{9,1},... | collective-permute-start | bytes 393224 | tf_op jit(solution)/shard_map/ppermute | solution.py:793
  101.6 15.3 %collective-permute-start.13 = (bf16[64,1024]{1,0:T(8,128)(2,1)S(1)}, bf16[64,1024]{1,0:T(8,128)(2,1)S(1)}, u32[]{:S(2)}, u32[]{:S(2)}) collective-permute-start(bf16[64,1024]{1,0:T(8,128)(2,1)S(1)} %get-tuple-element.186), channel_id=1, source_target_pairs={{0,16},{1,17},{2,18},{3,19},{4,20},{5,21},{6,22},{7,23},{8,24},{9,... | collective-permute-start | bytes 393224 | tf_op jit(solution)/shard_map/ppermute | solution.py:793
  104.2 12.7 %collective-permute-start.14 = (bf16[64,1024]{1,0:T(8,128)(2,1)S(1)}, bf16[64,1024]{1,0:T(8,128)(2,1)S(1)}, u32[]{:S(2)}, u32[]{:S(2)}) collective-permute-start(bf16[64,1024]{1,0:T(8,128)(2,1)S(1)} %get-tuple-element.187), channel_id=1, source_target_pairs={{0,24},{1,25},{2,26},{3,27},{4,28},{5,29},{6,30},{7,31},{8,16},{9,... | collective-permute-start | bytes 393224 | tf_op jit(solution)/shard_map/ppermute | solution.py:793
  117.0 3.9 %copy-start.23 = (f32[2,1,512]{2,1,0:T(1,128)S(1)}, f32[2,1,512]{2,1,0:T(1,128)}, u32[]{:S(2)}) copy-start(f32[2,1,512]{2,1,0:T(1,128)} %get-tuple-element.175) | copy-start | bytes 12292
  120.3 6.8 %collective-permute-start.16 = (bf16[64,1024]{1,0:T(8,128)(2,1)S(1)}, bf16[64,1024]{1,0:T(8,128)(2,1)S(1)}, u32[]{:S(2)}, u32[]{:S(2)}) collective-permute-start(bf16[64,1024]{1,0:T(8,128)(2,1)S(1)} %add_convert_fusion.5), channel_id=1, source_target_pairs={{0,8},{1,9},{2,10},{3,11},{4,12},{5,13},{6,14},{7,15},{8,0},{9,1},... | collective-permute-start | bytes 393224 | tf_op jit(solution)/shard_map/ppermute | solution.py:793
  120.9 23.1 %collective-permute-start.17 = (bf16[64,1024]{1,0:T(8,128)(2,1)S(1)}, bf16[64,1024]{1,0:T(8,128)(2,1)S(1)}, u32[]{:S(2)}, u32[]{:S(2)}) collective-permute-start(bf16[64,1024]{1,0:T(8,128)(2,1)S(1)} %add_convert_fusion.5), channel_id=1, source_target_pairs={{0,16},{1,17},{2,18},{3,19},{4,20},{5,21},{6,22},{7,23},{8,24},{9,... | collective-permute-start | bytes 393224 | tf_op jit(solution)/shard_map/ppermute | solution.py:793
  124.3 19.7 %collective-permute-start.18 = (bf16[64,1024]{1,0:T(8,128)(2,1)S(1)}, bf16[64,1024]{1,0:T(8,128)(2,1)S(1)}, u32[]{:S(2)}, u32[]{:S(2)}) collective-permute-start(bf16[64,1024]{1,0:T(8,128)(2,1)S(1)} %add_convert_fusion.5), channel_id=1, source_target_pairs={{0,24},{1,25},{2,26},{3,27},{4,28},{5,29},{6,30},{7,31},{8,16},{9,... | collective-permute-start | bytes 393224 | tf_op jit(solution)/shard_map/ppermute | solution.py:793
  124.7 19.3 %collective-permute-start.19 = (bf16[384,512]{1,0:T(8,128)(2,1)}, bf16[384,512]{1,0:T(8,128)(2,1)S(1)}, u32[]{:S(2)}, u32[]{:S(2)}) collective-permute-start(bf16[384,512]{1,0:T(8,128)(2,1)} %get-tuple-element.206), channel_id=1, source_target_pairs={{0,2},{1,3},{2,0},{3,1},{4,6},{5,7},{6,4},{7,5},{8,10},{9,11},{10,... | collective-permute-start | bytes 1179656 | tf_op jit(solution)/shard_map/ppermute | solution.py:793
  126.1 18.3 %collective-permute-start.20 = (bf16[384,512]{1,0:T(8,128)(2,1)}, bf16[384,512]{1,0:T(8,128)(2,1)S(1)}, u32[]{:S(2)}, u32[]{:S(2)}) collective-permute-start(bf16[384,512]{1,0:T(8,128)(2,1)} %get-tuple-element.207), channel_id=1, source_target_pairs={{0,4},{1,5},{2,6},{3,7},{4,0},{5,1},{6,2},{7,3},{8,12},{9,13},{10,... | collective-permute-start | bytes 1179656 | tf_op jit(solution)/shard_map/ppermute | solution.py:793
  127.1 17.3 %collective-permute-start.21 = (bf16[384,512]{1,0:T(8,128)(2,1)S(1)}, bf16[384,512]{1,0:T(8,128)(2,1)S(1)}, u32[]{:S(2)}, u32[]{:S(2)}) collective-permute-start(bf16[384,512]{1,0:T(8,128)(2,1)S(1)} %get-tuple-element.208), channel_id=1, source_target_pairs={{0,6},{1,7},{2,4},{3,5},{4,2},{5,3},{6,0},{7,1},{8,14},{9,15},{10,... | collective-permute-start | bytes 1179656 | tf_op jit(solution)/shard_map/ppermute | solution.py:793
  144.0 3.7 %copy-start.16 = (bf16[384,512]{1,0:T(8,128)(2,1)}, bf16[384,512]{1,0:T(8,128)(2,1)S(1)}, u32[]{:S(2)}) copy-start(bf16[384,512]{1,0:T(8,128)(2,1)S(1)} %collective-permute-done.19) | copy-start | bytes 1179652
  144.4 3.3 %copy-start.17 = (bf16[384,512]{1,0:T(8,128)(2,1)}, bf16[384,512]{1,0:T(8,128)(2,1)S(1)}, u32[]{:S(2)}) copy-start(bf16[384,512]{1,0:T(8,128)(2,1)S(1)} %collective-permute-done.20) | copy-start | bytes 1179652
  144.4 3.3 %copy-start.18 = (bf16[384,512]{1,0:T(8,128)(2,1)}, bf16[384,512]{1,0:T(8,128)(2,1)S(1)}, u32[]{:S(2)}) copy-start(bf16[384,512]{1,0:T(8,128)(2,1)S(1)} %collective-permute-done.21) | copy-start | bytes 1179652
  146.2 1.5 copy-start.21
  146.2 2.9 %copy-start.22 = (f32[2,1,512]{2,1,0:T(1,128)S(1)}, f32[2,1,512]{2,1,0:T(1,128)}, u32[]{:S(2)}) copy-start(f32[2,1,512]{2,1,0:T(1,128)} %get-tuple-element.238) | copy-start | bytes 12292
  146.2 1.5 collective-permute-start.22
  147.7 17.3 %collective-permute-start.24 = (bf16[2,512,512]{2,1,0:T(8,128)(2,1)}, bf16[2,512,512]{2,1,0:T(8,128)(2,1)S(1)}, u32[]{:S(2)}, u32[]{:S(2)}) collective-permute-start(bf16[2,512,512]{2,1,0:T(8,128)(2,1)} %get-tuple-element.230), channel_id=1, source_target_pairs={{0,1},{1,0},{2,3},{3,2},{4,5},{5,4},{6,7},{7,6},{8,9},{9,8},{10,11... | collective-permute-start | bytes 3145736 | tf_op jit(solution)/shard_map/ppermute | solution.py:756
  148.0 17.1 %collective-permute-start.25 = (bf16[256,1024]{1,0:T(8,128)(2,1)S(1)}, bf16[256,1024]{1,0:T(8,128)(2,1)S(1)}, u32[]{:S(2)}, u32[]{:S(2)}) collective-permute-start(bf16[256,1024]{1,0:T(8,128)(2,1)S(1)} %maximum_select_fusion.1), channel_id=1, source_target_pairs={{0,4},{1,3},{2,6},{3,1},{4,0},{5,7},{6,2},{7,5},{8,12},{9,11},{10,... | collective-permute-start | bytes 1572872 | tf_op jit(solution)/shard_map/ppermute | solution.py:793
  149.1 4.1 %collective-permute-start.23 = (f32[2,512]{1,0:T(2,128)S(1)}, f32[2,512]{1,0:T(2,128)S(1)}, u32[]{:S(2)}, u32[]{:S(2)}) collective-permute-start(f32[2,512]{1,0:T(2,128)S(1)} %bitcast.27), channel_id=1, source_target_pairs={{0,1},{1,0},{2,3},{3,2},{4,5},{5,4},{6,7},{7,6},{8,9},{9,8},{10,11... | collective-permute-start | bytes 12296 | tf_op jit(solution)/shard_map/ppermute | solution.py:756
  149.1 15.9 %collective-permute-start.26 = (bf16[112,512]{1,0:T(8,128)(2,1)S(1)}, bf16[112,512]{1,0:T(8,128)(2,1)S(1)}, u32[]{:S(2)}, u32[]{:S(2)}) collective-permute-start(bf16[112,512]{1,0:T(8,128)(2,1)S(1)} %get-tuple-element.232), channel_id=1, source_target_pairs={{0,8},{1,9},{2,10},{3,11},{4,12},{5,13},{6,14},{7,15},{8,0},{9,1},... | collective-permute-start | bytes 344072 | tf_op jit(solution)/shard_map/ppermute | solution.py:793
  149.2 15.8 %collective-permute-start.27 = (bf16[112,512]{1,0:T(8,128)(2,1)S(1)}, bf16[112,512]{1,0:T(8,128)(2,1)S(1)}, u32[]{:S(2)}, u32[]{:S(2)}) collective-permute-start(bf16[112,512]{1,0:T(8,128)(2,1)S(1)} %get-tuple-element.233), channel_id=1, source_target_pairs={{0,16},{1,17},{2,18},{3,19},{4,20},{5,21},{6,22},{7,23},{8,24},{9,... | collective-permute-start | bytes 344072 | tf_op jit(solution)/shard_map/ppermute | solution.py:793
  153.2 11.8 %collective-permute-start.28 = (bf16[112,512]{1,0:T(8,128)(2,1)S(1)}, bf16[112,512]{1,0:T(8,128)(2,1)S(1)}, u32[]{:S(2)}, u32[]{:S(2)}) collective-permute-start(bf16[112,512]{1,0:T(8,128)(2,1)S(1)} %get-tuple-element.234), channel_id=1, source_target_pairs={{0,24},{1,25},{2,26},{3,27},{4,28},{5,29},{6,30},{7,31},{8,16},{9,... | collective-permute-start | bytes 344072 | tf_op jit(solution)/shard_map/ppermute | solution.py:793
  165.0 7.1 %copy-start.24 = (bf16[4,512,512]{2,1,0:T(8,128)(2,1)S(1)}, bf16[4,512,512]{2,1,0:T(8,128)(2,1)}, u32[]{:S(2)}) copy-start(bf16[4,512,512]{2,1,0:T(8,128)(2,1)} %get-tuple-element.244) | copy-start | bytes 6291460
  165.0 2.6 %copy-start.19 = (bf16[112,512]{1,0:T(8,128)(2,1)}, bf16[112,512]{1,0:T(8,128)(2,1)S(1)}, u32[]{:S(2)}) copy-start(bf16[112,512]{1,0:T(8,128)(2,1)S(1)} %collective-permute-done.27) | copy-start | bytes 344068
  165.0 2.5 %copy-start.20 = (bf16[112,512]{1,0:T(8,128)(2,1)}, bf16[112,512]{1,0:T(8,128)(2,1)S(1)}, u32[]{:S(2)}) copy-start(bf16[112,512]{1,0:T(8,128)(2,1)S(1)} %collective-permute-done.28) | copy-start | bytes 344068
  165.5 15.1 %copy-start = (bf16[512,1024]{1,0:T(8,128)(2,1)}, bf16[512,1024]{1,0:T(8,128)(2,1)S(1)}, u32[]{:S(2)}) copy-start(bf16[512,1024]{1,0:T(8,128)(2,1)S(1)} %maximum_select_fusion.refs_0_) | copy-start | bytes 3145732
  165.5 14.9 %collective-permute-start.30 = (bf16[512,1024]{1,0:T(8,128)(2,1)S(1)}, bf16[512,1024]{1,0:T(8,128)(2,1)S(1)}, u32[]{:S(2)}, u32[]{:S(2)}) collective-permute-start(bf16[512,1024]{1,0:T(8,128)(2,1)S(1)} %maximum_select_fusion.refs_0_), channel_id=1, source_target_pairs={{0,2},{1,5},{2,0},{3,7},{4,6},{5,1},{6,4},{7,3},{8,10},{9,13},{10,... | collective-permute-start | bytes 3145736 | tf_op jit(solution)/shard_map/ppermute | solution.py:793
  167.6 12.9 %collective-permute-start.29 = (bf16[2,512,512]{2,1,0:T(8,128)(2,1)}, bf16[2,512,512]{2,1,0:T(8,128)(2,1)S(1)}, u32[]{:S(2)}, u32[]{:S(2)}) collective-permute-start(bf16[2,512,512]{2,1,0:T(8,128)(2,1)} %get-tuple-element.248), channel_id=1, source_target_pairs={{0,1},{1,0},{2,3},{3,2},{4,5},{5,4},{6,7},{7,6},{8,9},{9,8},{10,11... | collective-permute-start | bytes 3145736 | tf_op jit(solution)/shard_map/ppermute | solution.py:756
  167.6 7.0 %collective-permute-start.31 = (bf16[96,512]{1,0:T(8,128)(2,1)S(1)}, bf16[96,512]{1,0:T(8,128)(2,1)S(1)}, u32[]{:S(2)}, u32[]{:S(2)}) collective-permute-start(bf16[96,512]{1,0:T(8,128)(2,1)S(1)} %add_convert_fusion.9), channel_id=1, source_target_pairs={{0,8},{1,9},{2,10},{3,11},{4,12},{5,13},{6,14},{7,15},{8,0},{9,1},... | collective-permute-start | bytes 294920 | tf_op jit(solution)/shard_map/ppermute | solution.py:793
  167.7 11.5 %collective-permute-start.32 = (bf16[96,512]{1,0:T(8,128)(2,1)S(1)}, bf16[96,512]{1,0:T(8,128)(2,1)S(1)}, u32[]{:S(2)}, u32[]{:S(2)}) collective-permute-start(bf16[96,512]{1,0:T(8,128)(2,1)S(1)} %add_convert_fusion.9), channel_id=1, source_target_pairs={{0,16},{1,17},{2,18},{3,19},{4,20},{5,21},{6,22},{7,23},{8,24},{9,... | collective-permute-start | bytes 294920 | tf_op jit(solution)/shard_map/ppermute | solution.py:793
  171.4 7.8 %collective-permute-start.33 = (bf16[96,512]{1,0:T(8,128)(2,1)S(1)}, bf16[96,512]{1,0:T(8,128)(2,1)S(1)}, u32[]{:S(2)}, u32[]{:S(2)}) collective-permute-start(bf16[96,512]{1,0:T(8,128)(2,1)S(1)} %add_convert_fusion.9), channel_id=1, source_target_pairs={{0,24},{1,25},{2,26},{3,27},{4,28},{5,29},{6,30},{7,31},{8,16},{9,... | collective-permute-start | bytes 294920 | tf_op jit(solution)/shard_map/ppermute | solution.py:793
  172.2 9.4 %copy-start.25 = (bf16[4,512,512]{2,1,0:T(8,128)(2,1)}, bf16[4,512,512]{2,1,0:T(8,128)(2,1)S(1)}, u32[]{:S(2)}) copy-start(bf16[4,512,512]{2,1,0:T(8,128)(2,1)S(1)} %constant_dynamic-update-slice_fusion) | copy-start | bytes 6291460
  180.4 4.4 %copy-start.6 = (bf16[512,1024]{1,0:T(8,128)(2,1)}, bf16[512,1024]{1,0:T(8,128)(2,1)S(1)}, u32[]{:S(2)}) copy-start(bf16[512,1024]{1,0:T(8,128)(2,1)S(1)} %collective-permute-done.30.refs_1_) | copy-start | bytes 3145732
  180.7 8.6 %copy-start.3 = (bf16[400,512]{1,0:T(8,128)(2,1)}, bf16[400,512]{1,0:T(8,128)(2,1)S(1)}, u32[]{:S(2)}) copy-start(bf16[400,512]{1,0:T(8,128)(2,1)S(1)} %pad_maximum_fusion.refs_0_) | copy-start | bytes 1228804
  180.7 12.5 %collective-permute-start.34 = (bf16[400,512]{1,0:T(8,128)(2,1)S(1)}, bf16[400,512]{1,0:T(8,128)(2,1)S(1)}, u32[]{:S(2)}, u32[]{:S(2)}) collective-permute-start(bf16[400,512]{1,0:T(8,128)(2,1)S(1)} %pad_maximum_fusion.refs_0_), channel_id=1, source_target_pairs={{0,2},{1,3},{2,0},{3,1},{4,6},{5,7},{6,4},{7,5},{8,10},{9,11},{10,... | collective-permute-start | bytes 1228808 | tf_op jit(solution)/shard_map/ppermute | solution.py:793
  181.6 12.0 %collective-permute-start.35 = (bf16[400,512]{1,0:T(8,128)(2,1)S(1)}, bf16[400,512]{1,0:T(8,128)(2,1)S(1)}, u32[]{:S(2)}, u32[]{:S(2)}) collective-permute-start(bf16[400,512]{1,0:T(8,128)(2,1)S(1)} %pad_maximum_fusion.refs_0_), channel_id=1, source_target_pairs={{0,4},{1,5},{2,6},{3,7},{4,0},{5,1},{6,2},{7,3},{8,12},{9,13},{10,... | collective-permute-start | bytes 1228808 | tf_op jit(solution)/shard_map/ppermute | solution.py:793
  182.6 18.0 %collective-permute-start.36 = (bf16[400,512]{1,0:T(8,128)(2,1)S(1)}, bf16[400,512]{1,0:T(8,128)(2,1)S(1)}, u32[]{:S(2)}, u32[]{:S(2)}) collective-permute-start(bf16[400,512]{1,0:T(8,128)(2,1)S(1)} %pad_maximum_fusion.refs_0_), channel_id=1, source_target_pairs={{0,6},{1,7},{2,4},{3,5},{4,2},{5,3},{6,0},{7,1},{8,14},{9,15},{10,... | collective-permute-start | bytes 1228808 | tf_op jit(solution)/shard_map/ppermute | solution.py:793
  193.2 7.5 %copy-start.13 = (bf16[400,512]{1,0:T(8,128)(2,1)}, bf16[400,512]{1,0:T(8,128)(2,1)S(1)}, u32[]{:S(2)}) copy-start(bf16[400,512]{1,0:T(8,128)(2,1)S(1)} %collective-permute-done.34.refs_1_) | copy-start | bytes 1228804
  193.6 7.0 %copy-start.14 = (bf16[400,512]{1,0:T(8,128)(2,1)}, bf16[400,512]{1,0:T(8,128)(2,1)S(1)}, u32[]{:S(2)}) copy-start(bf16[400,512]{1,0:T(8,128)(2,1)S(1)} %collective-permute-done.35.refs_2_) | copy-start | bytes 1228804
  (5 other events, 4.3 us)

commit v2 on v1

--- a/solution.py
+++ b/solution.py
@@ -471,7 +471,8 @@
 
 def entry_kernel(
     core, own, got, order, back_order, gate_own, cand_own, gate_other, cand_other, middle_in, mixer_own,
-    mixer_other, gain, taps, mine_out, sent_out, gain_out, taps_out, rim, head,
+    mixer_other, gain, taps, gain_two, bias_own, up_own, bias_other, up_other, mine_out, sent_out, short_out,
+    rim, head, sums,
 ):
     step = pl.program_id(1)
     steps = pl.num_programs(1)
@@ -484,8 +485,7 @@
 
     @pl.when((step == 0) & (pl.program_id(0) == 0))
     def _():
-        gain_out[...] = jnp.zeros_like(gain_out)
-        taps_out[...] = jnp.zeros_like(taps_out)
+        sums[...] = jnp.zeros_like(sums)
 
     @pl.when(step == 0)
     def _():
@@ -507,19 +507,31 @@
     x = mm(order[...], jnp.where(position // half_chunks == core[0], own[0], got[0]))
     scale = lax.rsqrt(jnp.mean(x * x, axis=-1, keepdims=True) + epsilon)
     unit = x * scale
-    normed = unit * gain[...]
     back = jnp.zeros((rows, width), wide)
     for tap in range(tap_count):
         begin = 8 * (tap_count - 1 - tap)
         ahead = rim[begin : begin + rows, :]
         back = back + taps[tap : tap + 1, :] * ahead
-        taps_out[tap : tap + 1, :] += jnp.sum(ahead * normed, axis=0, keepdims=True)
-    gain_out[...] += jnp.sum(back * unit, axis=0, keepdims=True)
+        sums[tap : tap + 1, :] += jnp.sum(ahead * unit, axis=0, keepdims=True)
     weighted = gain[...] * back
     inner = jnp.mean(weighted * x, axis=-1, keepdims=True)
     gradient = middle_in[...] + scale * weighted - x * (scale * scale * scale * inner)
     gradient = mm(back_order[...], gradient.astype(low)).astype(low)
     give(gradient, position, half_chunks, core, mine_out, sent_out)
+
+    @pl.when((step == steps - 1) & (pl.program_id(0) == pl.num_programs(0) - 1))
+    def _():
+        totals = sums[0:tap_count, :]
+        parts = [jnp.sum(totals * taps[...], axis=0, keepdims=True), totals * gain[...], gain_two[...]]
+        for bias in (bias_own, up_own, bias_other, up_other):
+            parts.append(jnp.sum(bias[...], axis=0, keepdims=True))
+        short_out[...] = jnp.zeros_like(short_out)
+        row = 0
+        for part in parts:
+            for lane in range(0, part.shape[1], width):
+                some = min(width, part.shape[1])
+                short_out[row : row + part.shape[0], 0:some] = part[:, lane : lane + width]
+                row += part.shape[0]
 
 
 def give(values, position, half_chunks, core, mine_out, sent_out):
@@ -550,7 +562,7 @@
     )
 
 
-def entry(core, inputs, got, orders, projects, back_middle, mixers, gain, taps):
+def entry(core, inputs, got, orders, projects, back_middle, mixers, gain, taps, *shorts):
     windows, half, width = got.shape
     chunk = math.gcd(half, 512)
     halves = half // chunk
@@ -560,6 +572,8 @@
         (chunk, lanes), lambda w, t, core: (w * steps + steps - 1 - t, 0)
     )
     specs, shapes = side_specs(windows, half, width)
+    count = taps.shape[0] + 2 + sum(-(-bias.shape[1] // width) for bias in shorts[1:])
+    short = (-(-count // 16) * 16, width)
     return pl.pallas_call(
         entry_kernel,
         grid_spec=pltpu.PrefetchScalarGridSpec(
@@ -579,45 +593,41 @@
                 whole(mixers[1]),
                 whole(gain),
                 whole(taps),
+                *[whole(short) for short in shorts],
             ],
-            out_specs=[
-                *specs,
-                pl.BlockSpec((1, width), lambda w, t, core: (0, 0)),
-                pl.BlockSpec(taps.shape, lambda w, t, core: (0, 0)),
-            ],
+            out_specs=[*specs, pl.BlockSpec(short, lambda w, t, core: (0, 0))],
             scratch_shapes=[
                 pltpu.VMEM((chunk + 8 * (taps.shape[0] - 1), width), wide),
                 pltpu.VMEM((8 * (taps.shape[0] - 1), width), wide),
+                pltpu.VMEM((-(-taps.shape[0] // 8) * 8, width), wide),
             ],
         ),
-        out_shape=[
-            *shapes,
-            jax.ShapeDtypeStruct((1, width), wide),
-            jax.ShapeDtypeStruct(taps.shape, wide),
-        ],
+        out_shape=[*shapes, jax.ShapeDtypeStruct(short, wide)],
         compiler_params=params(60, 2),
         cost_estimate=cost(
             rows * width * 2 * mixers[0].shape[1], rows * mixers[0].shape[1] * 6
         ),
         name="input_gradient",
-    )(core, inputs, got, *orders, *projects, back_middle, *mixers, gain, taps)
-
-
-def leave_kernel(
-    core, back_order, active_own, active_other, middle, down_own, down_other, mine_out, sent_out
-):
+    )(core, inputs, got, *orders, *projects, back_middle, *mixers, gain, taps, *shorts)
+
+
+def leave_kernel(core, back_order, active_own, active_other, middle, down_own, down_other, *refs):
     total = middle[...] + mm(active_own[...], down_own[...]) + mm(active_other[...], down_other[...])
-    total = mm(back_order[...], total.astype(low)).astype(low)
-    give(total, pl.program_id(1), pl.num_programs(1) // 2, core, mine_out, sent_out)
-
-
-def leave(windows, core, back_order, actives, middle, downs):
-    rows, width = middle.shape
-    length = rows // windows
+    refs[-1][0] = mm(back_order[...], total.astype(low)).astype(low)
+
+
+def leave(windows, core, back_order, actives, middle, downs, base=None):
+    width = middle.shape[1]
+    half = middle.shape[0] // windows // 2
     chunk = back_order.shape[0]
-    steps = length // chunk
-    row = lambda lanes: pl.BlockSpec((chunk, lanes), lambda w, t, core: (w * steps + t, 0))
-    specs, shapes = side_specs(windows, length // 2, width)
+    steps = half // chunk
+    side = lambda core: 1 - core[0] if base is None else core[0]
+    row = lambda lanes: pl.BlockSpec(
+        (chunk, lanes), lambda w, t, core: ((2 * w + side(core)) * steps + t, 0)
+    )
+    first = lambda core: 0 if base is None else windows * core[0]
+    arrays = [core, back_order, *actives, middle, *downs]
+    rows = windows * half
     return pl.pallas_call(
         leave_kernel,
         grid_spec=pltpu.PrefetchScalarGridSpec(
@@ -630,43 +640,18 @@
                 row(width),
                 whole(downs[0]),
                 whole(downs[1]),
+                *([] if base is None else [pl.BlockSpec(memory_space=pl.ANY)]),
             ],
-            out_specs=specs,
+            out_specs=pl.BlockSpec(
+                (1, chunk, width), lambda w, t, core: (first(core) + w, t, 0)
+            ),
         ),
-        out_shape=shapes,
+        out_shape=jax.ShapeDtypeStruct((windows if base is None else 2 * windows, half, width), low),
+        input_output_aliases={} if base is None else {len(arrays): 0},
         compiler_params=params(60, 2),
         cost_estimate=cost(rows * width * 2 * downs[0].shape[0], rows * downs[0].shape[0] * 6),
         name="block_output",
-    )(core, back_order, *actives, middle, *downs)
-
-
-def pack_kernel(width, *refs):
-    gains, taps, gain_two, gate_own, gate_other, up_own, up_other, mine_out, sent_out = refs
-    for out, gate, up in ((mine_out, gate_own, up_own), (sent_out, gate_other, up_other)):
-        out[...] = jnp.zeros_like(out)
-        row = 0
-        for part in (
-            gains[...],
-            taps[...],
-            gain_two[...],
-            jnp.sum(gate[...], axis=0, keepdims=True),
-            jnp.sum(up[...], axis=0, keepdims=True),
-        ):
-            for lane in range(0, part.shape[1], width):
-                out[row : row + part.shape[0], 0 : min(width, part.shape[1])] = part[:, lane : lane + width]
-                row += part.shape[0]
-
-
-def pack(width, gains, taps, *rest):
-    arrays = [gains, taps, *rest]
-    count = taps.shape[0] + 3 + -(-rest[-1].shape[1] // width)
-    out = jax.ShapeDtypeStruct((-(-count // 8) * 8, width), wide)
-    return pl.pallas_call(
-        functools.partial(pack_kernel, width),
-        out_shape=[out, out],
-        compiler_params=params(60, 0),
-        name="pack_short",
-    )(*arrays)
+    )(*arrays, *([] if base is None else [base]))
 
 
 def in_order(place, parts):
@@ -962,27 +947,32 @@
     def put_back(whole_rows, got):
         return lax.dynamic_update_slice_in_dim(whole_rows, got, (1 - core) * windows, 0)
 
-    grad_mine, grad_sent, gain_grad, taps_grad = beside(
+    grad_mine, grad_sent, short = beside(
         [feed_sum, mixer_sum],
         lambda lead: entry(
             core_at, inputs, got_inputs, orders, [lead, cand_own, gate_other, cand_other],
-            back_middle, mixers, gain, causal_filter,
+            back_middle, mixers, gain, causal_filter, gain_two_grad, bias_own, up_bias_own,
+            bias_other, up_bias_other,
         ),
         gate_own,
     )
-    short, sent = pack(
-        width, gain_grad, taps_grad, gain_two_grad, bias_own, bias_other, up_bias_own, up_bias_other
-    )
-
-    mixer_sum.rider = short + partner(sent)
-
-    def leave_all(lead, state_other, grad_sent):
+    mixer_sum.rider = short
+
+    def leave_first(lead, state_other, grad_sent):
         moved = [partner(array) for array in (state_other, grad_sent)]
-        return *leave(windows, core_at, orders[1], [lead, active_other], middle, downs), *moved
-
-    out_mine, out_sent, state_got, grad_got = beside(
-        [feed_sum, mixer_sum], leave_all, active_own, state_other[:, 0], grad_sent
-    )
+        return leave(windows, core_at, orders[1], [lead, active_other], middle, downs), *moved
+
+    out_sent, state_got, grad_got = beside(
+        [feed_sum, mixer_sum], leave_first, active_own, state_other[:, 0], grad_sent
+    )
+    common = causal_filter.shape[0] + 2
+    biases_rows = 1 + units // width
+
+    def swap(short):
+        own = short[: common + biases_rows]
+        other = jnp.concatenate([short[:common], short[common + biases_rows : common + 2 * biases_rows]])
+        filler = jnp.zeros((short.shape[0] - common - biases_rows, width), wide)
+        return jnp.concatenate([own + partner(other), filler])
 
     def exits(grad_mine, grad_got, state_own, state_got, out_sent):
         state_gradient = jnp.where(
@@ -990,22 +980,23 @@
             jnp.concatenate([state_own, state_got]),
             jnp.concatenate([state_got, state_own]),
         )
-        return put_back(grad_mine, grad_got), state_gradient, partner(out_sent)
+        out_got = put_back(jnp.zeros_like(grad_mine), partner(out_sent))
+        return put_back(grad_mine, grad_got), state_gradient, out_got
 
     last = len(feed_sum.todo) == 1
     if last:
         feed_sum.prepare()
         feed_sum.start()
-    input_gradient, state_gradient, out_got, *feed_got = beside(
+    input_gradient, state_gradient, out_base, mixer_sum.rider, *feed_got = beside(
         [mixer_sum],
-        lambda *leads: (*exits(*leads), *(feed_sum.got if last else ())),
-        grad_mine, grad_got, state_own[:, 0], state_got, out_sent,
+        lambda *leads: (*exits(*leads[:-1]), swap(leads[-1]), *(feed_sum.got if last else ())),
+        grad_mine, grad_got, state_own[:, 0], state_got, out_sent, mixer_sum.rider,
     )
     while len(mixer_sum.todo) > 1:
         beside([mixer_sum], lambda: ())
 
     mixer_sum.prepare()
-    (mixer_send, *feed_got) = hold(mixer_sum.sends[0], *feed_got)
+    (mixer_send, active_lead, *feed_got) = hold(mixer_sum.sends[0], active_own, *feed_got)
     mixer_sum.sends = [mixer_send]
     mixer_sum.start()
     if last:
@@ -1016,7 +1007,9 @@
         feed_sum.prepare()
         feed_sum.start()
     down_sum, up_sum = finish_feed(*feed_sum.last())
-    block_output = put_back(out_mine, out_got)
+    block_output = leave(
+        windows, core_at, orders[1], [active_lead, active_other], middle, downs, out_base
+    )
     mixer_sum.got = list(hold(*mixer_sum.got, down_sum, block_output)[: len(mixer_sum.got)])
     mixer_grad, read_grad, gain_sum, taps_sum, gain_two_sum, gate_bias_sum, up_bias_sum = finish_mixer(
         *mixer_sum.last(), width, causal_filter.shape[0], units

time: 206 us -> 202 us (0.981)
  waiting for transfers between devices: 23.2 us -> 18 us
    ppermute x22, waiting for transfers between devices: 20.1 us -> 15.6 us  [exchange(): return lax.ppermute(array, ('dp', 'tensor'), route)]
    pallas_call x1 -> x2, Pallas kernels: 11.2 us -> 14 us  [leave(): pl.pallas_call(leave_kernel, grid_spec=pltpu.PrefetchScalarGridSpec(num_s...]
    unnamed x67 -> x61, local copies, waits for them, and re-layouts: 5.13 us -> 4.43 us
  transfers between devices with their start and end apart: 37 -> 37, of which waited for: 11 -> 9; matrix products, arithmetic and copies ran while one was open for 3% -> 2% of each run, Pallas kernels for 49% -> 51%
where the time goes in v2:
time: 202 us
  Pallas kernels  125 us (62%)
  starting transfers between devices  36.1 us (18%)
  waiting for transfers between devices  18 us (9%)
  other arithmetic  12.9 us (6%)
  local copies, waits for them, and re-layouts  8.51 us (4%)
    ppermute x22, starting transfers between devices, exchange(): return lax.ppermute(array, ('dp', 'tensor'), route)  32.7 us
    pallas_call x2, Pallas kernels, feed(): pl.pallas_call(kernel, grid_spec=pltpu.PrefetchScalarGridSpec(num_scalar_...  32.7 us
    pallas_call x2, Pallas kernels, scan_back(): pl.pallas_call(functools.partial(scan_kernel, windows, chunk), grid=(coun...  24.3 us
    pallas_call x1, Pallas kernels, forward(): pl.pallas_call(forward_kernel, grid_spec=pltpu.PrefetchScalarGridSpec(num...  19.6 us
    ppermute x22, waiting for transfers between devices, exchange(): return lax.ppermute(array, ('dp', 'tensor'), route)  15.6 us
    pallas_call x1, Pallas kernels, entry(): pl.pallas_call(entry_kernel, grid_spec=pltpu.PrefetchScalarGridSpec(num_s...  15 us
    pallas_call x2, Pallas kernels, leave(): pl.pallas_call(leave_kernel, grid_spec=pltpu.PrefetchScalarGridSpec(num_s...  14 us
    pallas_call x1, Pallas kernels, norm_back(): pl.pallas_call(norm_kernel, grid=(rows // chunk,), in_specs=[row(width),...  11.8 us
  transfers between devices with their start and end apart: 37, of which 9 were waited for; matrix products, arithmetic and copies ran while one was open for 2% of the time, Pallas kernels for 51%

profile of v2, /device:TPU:0, one launch (start us, length us, event | category | flops | bytes accessed | tf_op | source)
XLA Modules:
  0.0 202.0 jit_solution(8720532345161508058)
XLA Ops:
  0.7 1.4 constant_dynamic-slice_fusion.1
  2.2 0.5 collective-permute-start
  2.7 0.2 copy.27
  3.1 0.5 collective-permute-start.4
  3.6 0.4 collective-permute-start.2
  4.0 1.0 constant_dynamic-slice_fusion
  5.1 2.2 %collective-permute-done.2 = f32[512]{0:T(512)S(1)} collective-permute-done((f32[512]{0:T(512)S(1)}, f32[512]{0:T(512)S(1)}, u32[]{:S(2)}, u32[]{:S(2)}) %collective-permute-start.2) | collective-permute-done | bytes 2080 | tf_op jit(solution)/shard_map/ppermute | solution.py:741
  7.2 0.4 collective-permute-start.5
  7.8 0.4 collective-permute-start.6
  8.4 0.8 copy-done.7
  9.2 1.0 copy-done.8
  10.2 19.6 %forward_mixer.1 = (bf16[2048,512]{1,0:T(8,128)(2,1)}, f32[2048,1024]{1,0:T(8,128)}, bf16[2048,1024]{1,0:T(8,128)(2,1)}, bf16[2048,1024]{1,0:T(8,128)(2,1)}, bf1...) custom-call(s32[1]{0:T(128)} %bitcast.core, ...), custom_call_target="tpu_custom_call" | custom-call | flops 6442450944 | bytes 25165824 | tf_op jit(solution)/shard_map/forward_mixer/pallas_call | solution.py:182
  29.9 0.5 copy-done.26
  30.4 0.4 copy-done.2
  30.9 17.5 %feed_forward.2 = (bf16[2048,1024]{1,0:T(8,128)(2,1)}, bf16[2048,1024]{1,0:T(8,128)(2,1)}, f32[8,1024]{1,0:T(8,128)}, bf16[1024,1024]{1,0:T(8,128)(2,1)}, bf16[2048,512]{1,0:T(8,128)(2,1)}) custom-call(s32[1]{0:T(128)} %bitcast.core, bf16[4,512,512]{2,1,0:T(8,128)(2,1)} %refs_0_.1, bf16[2,512,512]{2,1,0:T(8,128)(2,1)} %collective-permute-done.5.refs_1_, ...), custom_call_target="tpu_custom_call" | custom-call | flops 8589934592 | bytes 8388608 | tf_op jit(solution)/shard_map/feed_forward/pallas_call | solution.py:308
  48.6 15.1 %feed_forward.3 = (bf16[2048,1024]{1,0:T(8,128)(2,1)}, bf16[2048,1024]{1,0:T(8,128)(2,1)}, f32[8,1024]{1,0:T(8,128)}, f32[1024,1024]{1,0:T(8,128)}) custom-call(s32[1]{0:T(128)} %bitcast.core, bf16[2048,512]{1,0:T(8,128)(2,1)} %get-tuple-element.143.refs_0_.tangent, bf16[2048,512]{1,0:T(8,128)(2,1)} %get-tuple-element.140.refs_3_.refs_1_, ...), custom_call_target="tpu_custom_call" | custom-call | flops 8589934592 | bytes 8388608 | tf_op jit(solution)/shard_map/feed_forward/pallas_call | solution.py:308
  63.7 1.3 copy-done.5
  65.0 3.5 %convert_add_fusion = (f32[512,1024]{1,0:T(8,128)S(1)}, bf16[512,1024]{1,0:T(8,128)(2,1)S(1)}) fusion(f32[1024,1024]{1,0:T(8,128)} %get-tuple-element.147, s32[]{:T(128)S(6)} %select_n.160, bf16[1024,1024]{1,0:T(8,128)(2,1)} %copy-done.5, s32[]{:T(128)S(6)} %select_n.159), kind=kLoop, calls=%fused_computation | loop fusion | flops 2621440 | bytes 9437192 | tf_op jit(solution)/shard_map/add | solution.py:795
  68.5 2.8 %collective-permute-start.10 = (bf16[512,1024]{1,0:T(8,128)(2,1)S(1)}, bf16[512,1024]{1,0:T(8,128)(2,1)}, u32[]{:S(2)}, u32[]{:S(2)}) collective-permute-start(bf16[512,1024]{1,0:T(8,128)(2,1)S(1)} %get-tuple-element.155), channel_id=1, source_target_pairs={{0,2},{1,5},{2,0},{3,7},{4,6},{5,1},{6,4},{7,3},{8,10},{9,13},{10,... | collective-permute-start | bytes 3145736 | tf_op jit(solution)/shard_map/ppermute | solution.py:778
  71.3 11.8 %norm_back.1 = (f32[2048,512]{1,0:T(8,128)}, bf16[2048,512]{1,0:T(8,128)(2,1)}, f32[1,512]{1,0:T(1,128)}) custom-call(bf16[2048,512]{1,0:T(8,128)(2,1)} %get-tuple-element.143.refs_0_.tangent, bf16[2048,1024]{1,0:T(8,128)(2,1)} %get-tuple-element.149.back_own, bf16[2048,1024]{1,0:T(8,128)(2,1)} %get-tuple-element.150.back_other, ...), custom_call_target="tpu_custom_call" | custom-call | flops 4294967296 | bytes 25165824 | tf_op jit(solution)/shard_map/norm_back/pallas_call | solution.py:349
  83.1 1.1 collective-permute-done.10
  84.2 1.6 convert_add_fusion.1
  85.8 2.1 %collective-permute-start.11 = (bf16[256,1024]{1,0:T(8,128)(2,1)S(1)}, bf16[256,1024]{1,0:T(8,128)(2,1)S(1)}, u32[]{:S(2)}, u32[]{:S(2)}) collective-permute-start(bf16[256,1024]{1,0:T(8,128)(2,1)S(1)} %get-tuple-element.169), channel_id=1, source_target_pairs={{0,4},{1,3},{2,6},{3,1},{4,0},{5,7},{6,2},{7,5},{8,12},{9,11},{10,... | collective-permute-start | bytes 1572872 | tf_op jit(solution)/shard_map/ppermute | solution.py:778
  87.9 11.9 %scan_back.2 = (bf16[2048,512]{1,0:T(8,128)(2,1)}, bf16[2048,512]{1,0:T(8,128)(2,1)}, f32[2,1,512]{2,1,0:T(1,128)}, f32[8,512]{1,0:T(8,128)}, bf16[1536,512]{1,0:T(8,128)(2,1)}) custom-call(bf16[2048,512]{1,0:T(8,128)(2,1)} %get-tuple-element.173.mixed, bf16[2048,512]{1,0:T(8,128)(2,1)} %get-tuple-element.159.filtered, bf16[512,512]{1,0:T(8,128)(2,1)} %copy-done.12, ...), custom_call_target="tpu_custom_call" | custom-call | flops 4294967296 | bytes 14680064 | tf_op jit(solution)/shard_map/scan_back/pallas_call | solution.py:439
  100.0 1.6 collective-permute-start.12
  101.7 2.6 %collective-permute-start.13 = (bf16[64,1024]{1,0:T(8,128)(2,1)S(1)}, bf16[64,1024]{1,0:T(8,128)(2,1)S(1)}, u32[]{:S(2)}, u32[]{:S(2)}) collective-permute-start(bf16[64,1024]{1,0:T(8,128)(2,1)S(1)} %get-tuple-element.180), channel_id=1, source_target_pairs={{0,16},{1,17},{2,18},{3,19},{4,20},{5,21},{6,22},{7,23},{8,24},{9,... | collective-permute-start | bytes 393224 | tf_op jit(solution)/shard_map/ppermute | solution.py:778
  104.3 0.2 collective-permute-start.14
  104.5 12.4 %scan_back.3 = (bf16[2048,512]{1,0:T(8,128)(2,1)}, bf16[2048,512]{1,0:T(8,128)(2,1)}, f32[2,1,512]{2,1,0:T(1,128)}, f32[8,512]{1,0:T(8,128)}, f32[1536,512]{1,0:T(8,128)}) custom-call(bf16[2048,512]{1,0:T(8,128)(2,1)} %get-tuple-element.173.mixed, bf16[2048,512]{1,0:T(8,128)(2,1)} %get-tuple-element.159.filtered, bf16[512,512]{1,0:T(8,128)(2,1)} %read.1, ...), custom_call_target="tpu_custom_call" | custom-call | flops 4294967296 | bytes 14680064 | tf_op jit(solution)/shard_map/scan_back/pallas_call | solution.py:439
  117.1 3.3 %convert_add_fusion.2 = (f32[384,512]{1,0:T(8,128)S(1)}, bf16[384,512]{1,0:T(8,128)(2,1)S(1)}, bf16[384,512]{1,0:T(8,128)(2,1)}, bf16[384,512]{1,0:T(8,128)(2,1)}) fusion(f32[1536,512]{1,0:T(8,128)} %get-tuple-element.184, s32[]{:T(128)S(6)} %select_n.167, bf16[1536,512]{1,0:T(8,128)(2,1)S(1)} %collective-permute-done.15, s32[]{:T(128)S(6)} %select_n.172, ...), kind=kLoop, calls=%fused_computation.8 | loop fusion | flops 2162688 | bytes 6684688 | tf_op jit(solution)/shard_map/add | solution.py:795
  120.3 0.6 collective-permute-start.16
  121.0 3.4 %collective-permute-start.17 = (bf16[64,1024]{1,0:T(8,128)(2,1)S(1)}, bf16[64,1024]{1,0:T(8,128)(2,1)S(1)}, u32[]{:S(2)}, u32[]{:S(2)}) collective-permute-start(bf16[64,1024]{1,0:T(8,128)(2,1)S(1)} %add_convert_fusion.5), channel_id=1, source_target_pairs={{0,16},{1,17},{2,18},{3,19},{4,20},{5,21},{6,22},{7,23},{8,24},{9,... | collective-permute-start | bytes 393224 | tf_op jit(solution)/shard_map/ppermute | solution.py:778
  124.4 0.4 collective-permute-start.18
  124.7 1.5 collective-permute-start.19
  126.2 0.5 collective-permute-start.20
  126.7 0.4 collective-permute-done.16
  127.2 1.4 collective-permute-start.21
  128.6 15.0 %input_gradient.1 = (bf16[4,512,512]{2,1,0:T(8,128)(2,1)}, bf16[2,512,512]{2,1,0:T(8,128)(2,1)}, f32[16,512]{1,0:T(8,128)}) custom-call(s32[1]{0:T(128)} %bitcast.core, bf16[4,512,512]{2,1,0:T(8,128)(2,1)} %own.3, bf16[2,512,512]{2,1,0:T(8,128)(2,1)} %copy-done.7, bf16[512,512]{1,0:T(8,128)(2,1)} %get-tuple-element.139.refs_2_.order, ...), custom_call_target="tpu_custom_call" | custom-call | flops 4294967296 | bytes 12582912 | tf_op jit(solution)/shard_map/input_gradient/pallas_call | solution.py:577
  143.6 0.9 collective-permute-done.20
  144.5 0.8 convert_element_type.178
  145.9 0.8 collective-permute-start.24
  146.6 0.4 collective-permute-start.25
  147.0 3.7 %collective-permute-start.26 = (bf16[112,512]{1,0:T(8,128)(2,1)S(1)}, bf16[112,512]{1,0:T(8,128)(2,1)S(1)}, u32[]{:S(2)}, u32[]{:S(2)}) collective-permute-start(bf16[112,512]{1,0:T(8,128)(2,1)S(1)} %get-tuple-element.223), channel_id=1, source_target_pairs={{0,16},{1,17},{2,18},{3,19},{4,20},{5,21},{6,22},{7,23},{8,24},{9,... | collective-permute-start | bytes 344072 | tf_op jit(solution)/shard_map/ppermute | solution.py:778
  150.7 1.1 collective-permute-start.27
  151.9 7.0 %block_output.2 = bf16[2,512,512]{2,1,0:T(8,128)(2,1)} custom-call(s32[1]{0:T(128)} %bitcast.core, bf16[512,512]{1,0:T(8,128)(2,1)} %get-tuple-element.138.back_order, bf16[2048,1024]{1,0:T(8,128)(2,1)} %get-tuple-element.246.active_own, bf16[2048,1024]{1,0:T(8,128)(2,1)} %get-tuple-element.218.active_other, ...), custom_call_target="tpu_custom_call" | custom-call | flops 2147483648 | bytes 6291456 | tf_op jit(solution)/shard_map/block_output/pallas_call | solution.py:631
  158.8 0.8 collective-permute-done.26
  159.6 1.1 add_convert_fusion.9
  160.8 0.5 maximum_select_fusion.refs_0_
  161.3 1.4 collective-permute-start.30
  162.7 2.1 %collective-permute-start.31 = (bf16[96,512]{1,0:T(8,128)(2,1)S(1)}, bf16[96,512]{1,0:T(8,128)(2,1)S(1)}, u32[]{:S(2)}, u32[]{:S(2)}) collective-permute-start(bf16[96,512]{1,0:T(8,128)(2,1)S(1)} %add_convert_fusion.9), channel_id=1, source_target_pairs={{0,8},{1,9},{2,10},{3,11},{4,12},{5,13},{6,14},{7,15},{8,0},{9,1},... | collective-permute-start | bytes 294920 | tf_op jit(solution)/shard_map/ppermute | solution.py:778
  164.9 1.1 collective-permute-start.32
  165.9 0.3 collective-permute-start.29
  166.3 0.7 maximum_select_fusion.7
  167.2 1.4 collective-permute-start.33
  168.8 1.3 constant_dynamic-update-slice_fusion.1.refs_0_
  170.2 4.8 %collective-permute-done.32 = bf16[96,512]{1,0:T(8,128)(2,1)S(1)} collective-permute-done((bf16[96,512]{1,0:T(8,128)(2,1)S(1)}, bf16[96,512]{1,0:T(8,128)(2,1)S(1)}, u32[]{:S(2)}, u32[]{:S(2)}) %collective-permute-start.32) | collective-permute-done | bytes 98336 | tf_op jit(solution)/shard_map/ppermute | solution.py:778
  174.9 1.2 collective-permute-done.30.refs_1_
  176.4 1.4 collective-permute-start.34
  177.9 0.8 collective-permute-start.35
  178.7 1.3 collective-permute-start.36
  180.0 0.7 pad_add_fusion.place
  180.7 3.4 %finish_feed.1 = (f32[1024,512]{1,0:T(8,128)}, f32[512,1024]{1,0:T(8,128)}) custom-call(s32[1]{0:T(128)} %bitcast.9.place, bf16[512,1024]{1,0:T(8,128)(2,1)} %copy-done.4, bf16[512,1024]{1,0:T(8,128)(2,1)} %copy-done.9), custom_call_target="tpu_custom_call" | custom-call | tf_op jit(solution)/shard_map/finish_feed/pallas_call | solution.py:678
  184.1 7.0 %block_output.3 = bf16[4,512,512]{2,1,0:T(8,128)(2,1)} custom-call(s32[1]{0:T(128)} %bitcast.core, bf16[512,512]{1,0:T(8,128)(2,1)} %get-tuple-element.138.back_order, bf16[2048,1024]{1,0:T(8,128)(2,1)} %get-tuple-element.246.active_own, bf16[2048,1024]{1,0:T(8,128)(2,1)} %get-tuple-element.218.active_other, ...), custom_call_target="tpu_custom_call", output_to_operand_aliasing={{}: (7, {})} | custom-call | flops 2147483648 | bytes 6291456 | tf_op jit(solution)/shard_map/block_output/pallas_call | solution.py:631
  191.1 6.4 %collective-permute-done.35.refs_2_ = bf16[400,512]{1,0:T(8,128)(2,1)} collective-permute-done((bf16[400,512]{1,0:T(8,128)(2,1)S(1)}, bf16[400,512]{1,0:T(8,128)(2,1)}, u32[]{:S(2)}, u32[]{:S(2)}) %collective-permute-start.35) | collective-permute-done | bytes 409632 | tf_op jit(solution)/shard_map/ppermute | solution.py:778
  197.5 4.5 %finish_mixer.1 = (f32[512,2,512]{2,1,0:T(2,128)}, f32[512,512]{1,0:T(8,128)}, f32[1,512]{1,0:T(1,128)}, f32[4,512]{1,0:T(4,128)}, f32[1,512]{1,0:T(1,128)}, /*index=5*/f32[1,512]{1,0:T(1,128)}, f32[1,1024]{1,0:T(1,128)}) custom-call(s32[2]{0:T(128)} %pad_add_fusion.place, bf16[400,512]{1,0:T(8,128)(2,1)} %copy-done.6, bf16[400,512]{1,0:T(8,128)(2,1)} %copy-done.14, ...), custom_call_target="tpu_custom_call" | custom-call | tf_op jit(solution)/shard_map/finish_mixer/pallas_call | solution.py:718
  (111 shorter events, 2.6 us)
Async XLA Ops:
  0.6 2.0 %copy-start.10 = (bf16[512,2,512]{2,1,0:T(2,128)(2,1)S(1)}, bf16[512,2,512]{2,1,0:T(2,128)(2,1)}, u32[]{:S(2)}) copy-start(bf16[512,2,512]{2,1,0:T(2,128)(2,1)} %param.16) | copy-start | bytes 3145732
  0.7 2.4 %copy-start.11 = (bf16[512,512]{1,0:T(8,128)(2,1)S(1)}, bf16[512,512]{1,0:T(8,128)(2,1)}, u32[]{:S(2)}) copy-start(bf16[512,512]{1,0:T(8,128)(2,1)} %read.1) | copy-start | bytes 1572868
  0.7 2.9 %copy-start.23 = (f32[4,512]{1,0:T(4,128)S(1)}, f32[4,512]{1,0:T(4,128)}, u32[]{:S(2)}) copy-start(f32[4,512]{1,0:T(4,128)} %start_own.1) | copy-start | bytes 24580
  0.7 2.9 %copy-start.27 = (f32[512]{0:T(512)S(1)}, f32[512]{0:T(512)}, u32[]{:S(2)}) copy-start(f32[512]{0:T(512)} %param.17) | copy-start | bytes 6148
  0.7 3.3 %copy-start.13 = (bf16[4,512,512]{2,1,0:T(8,128)(2,1)S(1)}, bf16[4,512,512]{2,1,0:T(8,128)(2,1)}, u32[]{:S(2)}) copy-start(bf16[4,512,512]{2,1,0:T(8,128)(2,1)} %refs_0_.1) | copy-start | bytes 6291460
  2.2 6.0 %collective-permute-start = (bf16[2,512,512]{2,1,0:T(8,128)(2,1)S(1)}, bf16[2,512,512]{2,1,0:T(8,128)(2,1)S(1)}, u32[]{:S(2)}, u32[]{:S(2)}) collective-permute-start(bf16[2,512,512]{2,1,0:T(8,128)(2,1)S(1)} %constant_dynamic-slice_fusion.1), channel_id=1, source_target_pairs={{0,1},{1,0},{2,3},{3,2},{4,5},{5,4},{6,7},{7,6},{8,9},{9,8},{10,11... | collective-permute-start | bytes 3145736 | tf_op jit(solution)/shard_map/ppermute | solution.py:741
  2.7 4.9 %copy-start.1 = (bf16[1024,512]{1,0:T(8,128)(2,1)S(1)}, bf16[1024,512]{1,0:T(8,128)(2,1)}, u32[]{:S(2)}) copy-start(bf16[1024,512]{1,0:T(8,128)(2,1)} %down_own.3) | copy-start | bytes 3145732
  2.7 5.5 %copy-start.25 = (f32[1024]{0:T(1024)S(1)}, f32[1024]{0:T(1024)}, u32[]{:S(2)}) copy-start(f32[1024]{0:T(1024)} %param.21) | copy-start | bytes 12292
  2.9 7.2 %copy-start.3 = (bf16[64,8,2,512]{3,1,2,0:T(8,128)(2,1)}, bf16[64,8,2,512]{3,1,2,0:T(8,128)(2,1)S(1)}, u32[]{:S(2)}) copy-start(bf16[64,8,2,512]{3,1,2,0:T(8,128)(2,1)S(1)} %copy.27) | copy-start | bytes 3145732
  2.9 5.5 %collective-permute-start.1 = (bf16[512,1024]{1,0:T(8,128)(2,1)S(1)}, bf16[512,1024]{1,0:T(8,128)(2,1)S(1)}, u32[]{:S(2)}, u32[]{:S(2)}) collective-permute-start(bf16[512,1024]{1,0:T(8,128)(2,1)S(1)} %bitcast.22), channel_id=1, source_target_pairs={{0,1},{1,0},{2,3},{3,2},{4,5},{5,4},{6,7},{7,6},{8,9},{9,8},{10,11... | collective-permute-start | bytes 3145736 | tf_op jit(solution)/shard_map/ppermute | solution.py:741
  3.1 4.7 %collective-permute-start.4 = (bf16[512,512]{1,0:T(8,128)(2,1)S(1)}, bf16[512,512]{1,0:T(8,128)(2,1)S(1)}, u32[]{:S(2)}, u32[]{:S(2)}) collective-permute-start(bf16[512,512]{1,0:T(8,128)(2,1)S(1)} %copy-done.11), channel_id=1, source_target_pairs={{0,1},{1,0},{2,3},{3,2},{4,5},{5,4},{6,7},{7,6},{8,9},{9,8},{10,11... | collective-permute-start | bytes 1572872 | tf_op jit(solution)/shard_map/ppermute | solution.py:741
  3.5 4.1 %collective-permute-start.3 = (f32[4,512]{1,0:T(4,128)S(1)}, f32[4,512]{1,0:T(4,128)S(1)}, u32[]{:S(2)}, u32[]{:S(2)}) collective-permute-start(f32[4,512]{1,0:T(4,128)S(1)} %copy-done.23), channel_id=1, source_target_pairs={{0,1},{1,0},{2,3},{3,2},{4,5},{5,4},{6,7},{7,6},{8,9},{9,8},{10,11... | collective-permute-start | bytes 24584 | tf_op jit(solution)/shard_map/ppermute | solution.py:741
  3.6 3.6 %collective-permute-start.2 = (f32[512]{0:T(512)S(1)}, f32[512]{0:T(512)S(1)}, u32[]{:S(2)}, u32[]{:S(2)}) collective-permute-start(f32[512]{0:T(512)S(1)} %copy-done.27), channel_id=1, source_target_pairs={{0,1},{1,0},{2,3},{3,2},{4,5},{5,4},{6,7},{7,6},{8,9},{9,8},{10,11... | collective-permute-start | bytes 6152 | tf_op jit(solution)/shard_map/ppermute | solution.py:741
  7.2 2.9 %copy-start.28 = (f32[512]{0:T(512)}, f32[512]{0:T(512)S(1)}, u32[]{:S(2)}) copy-start(f32[512]{0:T(512)S(1)} %collective-permute-done.2) | copy-start | bytes 6148
  7.2 22.6 %collective-permute-start.5 = (bf16[2,512,512]{2,1,0:T(8,128)(2,1)}, bf16[2,512,512]{2,1,0:T(8,128)(2,1)}, u32[]{:S(2)}, u32[]{:S(2)}) collective-permute-start(bf16[2,512,512]{2,1,0:T(8,128)(2,1)} %constant_dynamic-slice_fusion), channel_id=1, source_target_pairs={{0,1},{1,0},{2,3},{3,2},{4,5},{5,4},{6,7},{7,6},{8,9},{9,8},{10,11... | collective-permute-start | bytes 3145736 | tf_op jit(solution)/shard_map/ppermute | solution.py:741
  7.6 2.6 %copy-start.24 = (f32[4,512]{1,0:T(4,128)}, f32[4,512]{1,0:T(4,128)S(1)}, u32[]{:S(2)}) copy-start(f32[4,512]{1,0:T(4,128)S(1)} %collective-permute-done.3.start_other) | copy-start | bytes 24580
  7.6 22.2 %collective-permute-start.8 = (bf16[1024,512]{1,0:T(8,128)(2,1)S(1)}, bf16[1024,512]{1,0:T(8,128)(2,1)S(1)}, u32[]{:S(2)}, u32[]{:S(2)}) collective-permute-start(bf16[1024,512]{1,0:T(8,128)(2,1)S(1)} %copy-done.1), channel_id=1, source_target_pairs={{0,1},{1,0},{2,3},{3,2},{4,5},{5,4},{6,7},{7,6},{8,9},{9,8},{10,11... | collective-permute-start | bytes 3145736 | tf_op jit(solution)/shard_map/ppermute | solution.py:741
  7.8 2.4 %copy-start.12 = (bf16[512,512]{1,0:T(8,128)(2,1)}, bf16[512,512]{1,0:T(8,128)(2,1)S(1)}, u32[]{:S(2)}) copy-start(bf16[512,512]{1,0:T(8,128)(2,1)S(1)} %collective-permute-done.4.read_other.read) | copy-start | bytes 1572868
  7.8 22.1 %collective-permute-start.6 = (bf16[512,1024]{1,0:T(8,128)(2,1)}, bf16[512,1024]{1,0:T(8,128)(2,1)}, u32[]{:S(2)}, u32[]{:S(2)}) collective-permute-start(bf16[512,1024]{1,0:T(8,128)(2,1)} %up_own.1), channel_id=1, source_target_pairs={{0,1},{1,0},{2,3},{3,2},{4,5},{5,4},{6,7},{7,6},{8,9},{9,8},{10,11... | collective-permute-start | bytes 3145736 | tf_op jit(solution)/shard_map/ppermute | solution.py:741
  8.2 21.6 %collective-permute-start.7 = (f32[1024]{0:T(1024)S(1)}, f32[1024]{0:T(1024)S(1)}, u32[]{:S(2)}, u32[]{:S(2)}) collective-permute-start(f32[1024]{0:T(1024)S(1)} %copy-done.25), channel_id=1, source_target_pairs={{0,1},{1,0},{2,3},{3,2},{4,5},{5,4},{6,7},{7,6},{8,9},{9,8},{10,11... | collective-permute-start | bytes 12296 | tf_op jit(solution)/shard_map/ppermute | solution.py:741
  9.2 1.0 copy-start.8
  29.9 1.0 copy-start.2
  48.4 15.3 %collective-permute-start.9 = (bf16[1024,1024]{1,0:T(8,128)(2,1)}, bf16[1024,1024]{1,0:T(8,128)(2,1)S(1)}, u32[]{:S(2)}, u32[]{:S(2)}) collective-permute-start(bf16[1024,1024]{1,0:T(8,128)(2,1)} %get-tuple-element.146), channel_id=1, source_target_pairs={{0,1},{1,0},{2,3},{3,2},{4,5},{5,4},{6,7},{7,6},{8,9},{9,8},{10,11... | collective-permute-start | bytes 6291464 | tf_op jit(solution)/shard_map/ppermute | solution.py:741
  63.7 1.3 copy-start.5
  68.5 15.7 %collective-permute-start.10 = (bf16[512,1024]{1,0:T(8,128)(2,1)S(1)}, bf16[512,1024]{1,0:T(8,128)(2,1)}, u32[]{:S(2)}, u32[]{:S(2)}) collective-permute-start(bf16[512,1024]{1,0:T(8,128)(2,1)S(1)} %get-tuple-element.155), channel_id=1, source_target_pairs={{0,2},{1,5},{2,0},{3,7},{4,6},{5,1},{6,4},{7,3},{8,10},{9,13},{10,... | collective-permute-start | bytes 3145736 | tf_op jit(solution)/shard_map/ppermute | solution.py:778
  85.8 14.0 %collective-permute-start.11 = (bf16[256,1024]{1,0:T(8,128)(2,1)S(1)}, bf16[256,1024]{1,0:T(8,128)(2,1)S(1)}, u32[]{:S(2)}, u32[]{:S(2)}) collective-permute-start(bf16[256,1024]{1,0:T(8,128)(2,1)S(1)} %get-tuple-element.169), channel_id=1, source_target_pairs={{0,4},{1,3},{2,6},{3,1},{4,0},{5,7},{6,2},{7,5},{8,12},{9,11},{10,... | collective-permute-start | bytes 1572872 | tf_op jit(solution)/shard_map/ppermute | solution.py:778
  99.8 17.3 %collective-permute-start.15 = (bf16[1536,512]{1,0:T(8,128)(2,1)}, bf16[1536,512]{1,0:T(8,128)(2,1)S(1)}, u32[]{:S(2)}, u32[]{:S(2)}) collective-permute-start(bf16[1536,512]{1,0:T(8,128)(2,1)} %get-tuple-element.183), channel_id=1, source_target_pairs={{0,1},{1,0},{2,3},{3,2},{4,5},{5,4},{6,7},{7,6},{8,9},{9,8},{10,11... | collective-permute-start | bytes 4718600 | tf_op jit(solution)/shard_map/ppermute | solution.py:741
  100.0 16.9 %collective-permute-start.12 = (bf16[64,1024]{1,0:T(8,128)(2,1)S(1)}, bf16[64,1024]{1,0:T(8,128)(2,1)S(1)}, u32[]{:S(2)}, u32[]{:S(2)}) collective-permute-start(bf16[64,1024]{1,0:T(8,128)(2,1)S(1)} %get-tuple-element.179), channel_id=1, source_target_pairs={{0,8},{1,9},{2,10},{3,11},{4,12},{5,13},{6,14},{7,15},{8,0},{9,1},... | collective-permute-start | bytes 393224 | tf_op jit(solution)/shard_map/ppermute | solution.py:778
  101.7 15.2 %collective-permute-start.13 = (bf16[64,1024]{1,0:T(8,128)(2,1)S(1)}, bf16[64,1024]{1,0:T(8,128)(2,1)S(1)}, u32[]{:S(2)}, u32[]{:S(2)}) collective-permute-start(bf16[64,1024]{1,0:T(8,128)(2,1)S(1)} %get-tuple-element.180), channel_id=1, source_target_pairs={{0,16},{1,17},{2,18},{3,19},{4,20},{5,21},{6,22},{7,23},{8,24},{9,... | collective-permute-start | bytes 393224 | tf_op jit(solution)/shard_map/ppermute | solution.py:778
  104.3 12.7 %collective-permute-start.14 = (bf16[64,1024]{1,0:T(8,128)(2,1)S(1)}, bf16[64,1024]{1,0:T(8,128)(2,1)S(1)}, u32[]{:S(2)}, u32[]{:S(2)}) collective-permute-start(bf16[64,1024]{1,0:T(8,128)(2,1)S(1)} %get-tuple-element.181), channel_id=1, source_target_pairs={{0,24},{1,25},{2,26},{3,27},{4,28},{5,29},{6,30},{7,31},{8,16},{9,... | collective-permute-start | bytes 393224 | tf_op jit(solution)/shard_map/ppermute | solution.py:778
  117.0 3.9 %copy-start.19 = (f32[2,1,512]{2,1,0:T(1,128)S(1)}, f32[2,1,512]{2,1,0:T(1,128)}, u32[]{:S(2)}) copy-start(f32[2,1,512]{2,1,0:T(1,128)} %get-tuple-element.211) | copy-start | bytes 12292
  120.3 6.8 %collective-permute-start.16 = (bf16[64,1024]{1,0:T(8,128)(2,1)S(1)}, bf16[64,1024]{1,0:T(8,128)(2,1)S(1)}, u32[]{:S(2)}, u32[]{:S(2)}) collective-permute-start(bf16[64,1024]{1,0:T(8,128)(2,1)S(1)} %add_convert_fusion.5), channel_id=1, source_target_pairs={{0,8},{1,9},{2,10},{3,11},{4,12},{5,13},{6,14},{7,15},{8,0},{9,1},... | collective-permute-start | bytes 393224 | tf_op jit(solution)/shard_map/ppermute | solution.py:778
  121.0 22.6 %collective-permute-start.17 = (bf16[64,1024]{1,0:T(8,128)(2,1)S(1)}, bf16[64,1024]{1,0:T(8,128)(2,1)S(1)}, u32[]{:S(2)}, u32[]{:S(2)}) collective-permute-start(bf16[64,1024]{1,0:T(8,128)(2,1)S(1)} %add_convert_fusion.5), channel_id=1, source_target_pairs={{0,16},{1,17},{2,18},{3,19},{4,20},{5,21},{6,22},{7,23},{8,24},{9,... | collective-permute-start | bytes 393224 | tf_op jit(solution)/shard_map/ppermute | solution.py:778
  124.4 19.2 %collective-permute-start.18 = (bf16[64,1024]{1,0:T(8,128)(2,1)S(1)}, bf16[64,1024]{1,0:T(8,128)(2,1)S(1)}, u32[]{:S(2)}, u32[]{:S(2)}) collective-permute-start(bf16[64,1024]{1,0:T(8,128)(2,1)S(1)} %add_convert_fusion.5), channel_id=1, source_target_pairs={{0,24},{1,25},{2,26},{3,27},{4,28},{5,29},{6,30},{7,31},{8,16},{9,... | collective-permute-start | bytes 393224 | tf_op jit(solution)/shard_map/ppermute | solution.py:778
  124.7 18.9 %collective-permute-start.19 = (bf16[384,512]{1,0:T(8,128)(2,1)}, bf16[384,512]{1,0:T(8,128)(2,1)S(1)}, u32[]{:S(2)}, u32[]{:S(2)}) collective-permute-start(bf16[384,512]{1,0:T(8,128)(2,1)} %get-tuple-element.204), channel_id=1, source_target_pairs={{0,2},{1,3},{2,0},{3,1},{4,6},{5,7},{6,4},{7,5},{8,10},{9,11},{10,... | collective-permute-start | bytes 1179656 | tf_op jit(solution)/shard_map/ppermute | solution.py:778
  126.2 18.3 %collective-permute-start.20 = (bf16[384,512]{1,0:T(8,128)(2,1)}, bf16[384,512]{1,0:T(8,128)(2,1)S(1)}, u32[]{:S(2)}, u32[]{:S(2)}) collective-permute-start(bf16[384,512]{1,0:T(8,128)(2,1)} %get-tuple-element.205), channel_id=1, source_target_pairs={{0,4},{1,5},{2,6},{3,7},{4,0},{5,1},{6,2},{7,3},{8,12},{9,13},{10,... | collective-permute-start | bytes 1179656 | tf_op jit(solution)/shard_map/ppermute | solution.py:778
  127.2 17.3 %collective-permute-start.21 = (bf16[384,512]{1,0:T(8,128)(2,1)S(1)}, bf16[384,512]{1,0:T(8,128)(2,1)S(1)}, u32[]{:S(2)}, u32[]{:S(2)}) collective-permute-start(bf16[384,512]{1,0:T(8,128)(2,1)S(1)} %get-tuple-element.206), channel_id=1, source_target_pairs={{0,6},{1,7},{2,4},{3,5},{4,2},{5,3},{6,0},{7,1},{8,14},{9,15},{10,... | collective-permute-start | bytes 1179656 | tf_op jit(solution)/shard_map/ppermute | solution.py:778
  143.6 2.2 %copy-start.15 = (bf16[384,512]{1,0:T(8,128)(2,1)}, bf16[384,512]{1,0:T(8,128)(2,1)S(1)}, u32[]{:S(2)}) copy-start(bf16[384,512]{1,0:T(8,128)(2,1)S(1)} %collective-permute-done.19) | copy-start | bytes 1179652
  144.5 1.3 copy-start.16
  144.5 1.3 copy-start.17
  145.3 1.4 copy-start.20
  145.8 13.8 %collective-permute-start.23 = (bf16[2,512,512]{2,1,0:T(8,128)(2,1)}, bf16[2,512,512]{2,1,0:T(8,128)(2,1)S(1)}, u32[]{:S(2)}, u32[]{:S(2)}) collective-permute-start(bf16[2,512,512]{2,1,0:T(8,128)(2,1)} %get-tuple-element.220), channel_id=1, source_target_pairs={{0,1},{1,0},{2,3},{3,2},{4,5},{5,4},{6,7},{7,6},{8,9},{9,8},{10,11... | collective-permute-start | bytes 3145736 | tf_op jit(solution)/shard_map/ppermute | solution.py:741
  145.9 13.7 %collective-permute-start.24 = (bf16[256,1024]{1,0:T(8,128)(2,1)S(1)}, bf16[256,1024]{1,0:T(8,128)(2,1)S(1)}, u32[]{:S(2)}, u32[]{:S(2)}) collective-permute-start(bf16[256,1024]{1,0:T(8,128)(2,1)S(1)} %maximum_select_fusion.1), channel_id=1, source_target_pairs={{0,4},{1,3},{2,6},{3,1},{4,0},{5,7},{6,2},{7,5},{8,12},{9,11},{10,... | collective-permute-start | bytes 1572872 | tf_op jit(solution)/shard_map/ppermute | solution.py:778
  146.6 4.1 %collective-permute-start.22 = (f32[2,512]{1,0:T(2,128)S(1)}, f32[2,512]{1,0:T(2,128)S(1)}, u32[]{:S(2)}, u32[]{:S(2)}) collective-permute-start(f32[2,512]{1,0:T(2,128)S(1)} %bitcast.27), channel_id=1, source_target_pairs={{0,1},{1,0},{2,3},{3,2},{4,5},{5,4},{6,7},{7,6},{8,9},{9,8},{10,11... | collective-permute-start | bytes 12296 | tf_op jit(solution)/shard_map/ppermute | solution.py:741
  146.6 12.2 %collective-permute-start.25 = (bf16[112,512]{1,0:T(8,128)(2,1)S(1)}, bf16[112,512]{1,0:T(8,128)(2,1)S(1)}, u32[]{:S(2)}, u32[]{:S(2)}) collective-permute-start(bf16[112,512]{1,0:T(8,128)(2,1)S(1)} %get-tuple-element.222), channel_id=1, source_target_pairs={{0,8},{1,9},{2,10},{3,11},{4,12},{5,13},{6,14},{7,15},{8,0},{9,1},... | collective-permute-start | bytes 344072 | tf_op jit(solution)/shard_map/ppermute | solution.py:778
  147.0 12.5 %collective-permute-start.26 = (bf16[112,512]{1,0:T(8,128)(2,1)S(1)}, bf16[112,512]{1,0:T(8,128)(2,1)S(1)}, u32[]{:S(2)}, u32[]{:S(2)}) collective-permute-start(bf16[112,512]{1,0:T(8,128)(2,1)S(1)} %get-tuple-element.223), channel_id=1, source_target_pairs={{0,16},{1,17},{2,18},{3,19},{4,20},{5,21},{6,22},{7,23},{8,24},{9,... | collective-permute-start | bytes 344072 | tf_op jit(solution)/shard_map/ppermute | solution.py:778
  150.7 8.9 %collective-permute-start.27 = (bf16[112,512]{1,0:T(8,128)(2,1)S(1)}, bf16[112,512]{1,0:T(8,128)(2,1)S(1)}, u32[]{:S(2)}, u32[]{:S(2)}) collective-permute-start(bf16[112,512]{1,0:T(8,128)(2,1)S(1)} %get-tuple-element.224), channel_id=1, source_target_pairs={{0,24},{1,25},{2,26},{3,27},{4,28},{5,29},{6,30},{7,31},{8,16},{9,... | collective-permute-start | bytes 344072 | tf_op jit(solution)/shard_map/ppermute | solution.py:778
  151.9 7.8 %copy-start.18 = (f32[16,512]{1,0:T(8,128)S(1)}, f32[16,512]{1,0:T(8,128)}, u32[]{:S(2)}) copy-start(f32[16,512]{1,0:T(8,128)} %get-tuple-element.216) | copy-start | bytes 98308
  160.7 7.9 %collective-permute-start.28 = (bf16[2,512,512]{2,1,0:T(8,128)(2,1)}, bf16[2,512,512]{2,1,0:T(8,128)(2,1)}, u32[]{:S(2)}, u32[]{:S(2)}) collective-permute-start(bf16[2,512,512]{2,1,0:T(8,128)(2,1)} %block_output.2), channel_id=1, source_target_pairs={{0,1},{1,0},{2,3},{3,2},{4,5},{5,4},{6,7},{7,6},{8,9},{9,8},{10,11... | collective-permute-start | bytes 3145736 | tf_op jit(solution)/shard_map/ppermute | solution.py:741
  160.8 5.4 %copy-start.21 = (bf16[4,512,512]{2,1,0:T(8,128)(2,1)S(1)}, bf16[4,512,512]{2,1,0:T(8,128)(2,1)}, u32[]{:S(2)}) copy-start(bf16[4,512,512]{2,1,0:T(8,128)(2,1)} %get-tuple-element.233) | copy-start | bytes 6291460
  161.3 7.5 %copy-start.4 = (bf16[512,1024]{1,0:T(8,128)(2,1)}, bf16[512,1024]{1,0:T(8,128)(2,1)S(1)}, u32[]{:S(2)}) copy-start(bf16[512,1024]{1,0:T(8,128)(2,1)S(1)} %maximum_select_fusion.refs_0_) | copy-start | bytes 3145732
  161.3 14.9 %collective-permute-start.30 = (bf16[512,1024]{1,0:T(8,128)(2,1)S(1)}, bf16[512,1024]{1,0:T(8,128)(2,1)S(1)}, u32[]{:S(2)}, u32[]{:S(2)}) collective-permute-start(bf16[512,1024]{1,0:T(8,128)(2,1)S(1)} %maximum_select_fusion.refs_0_), channel_id=1, source_target_pairs={{0,2},{1,5},{2,0},{3,7},{4,6},{5,1},{6,4},{7,3},{8,10},{9,13},{10,... | collective-permute-start | bytes 3145736 | tf_op jit(solution)/shard_map/ppermute | solution.py:778
  162.7 7.4 %collective-permute-start.31 = (bf16[96,512]{1,0:T(8,128)(2,1)S(1)}, bf16[96,512]{1,0:T(8,128)(2,1)S(1)}, u32[]{:S(2)}, u32[]{:S(2)}) collective-permute-start(bf16[96,512]{1,0:T(8,128)(2,1)S(1)} %add_convert_fusion.9), channel_id=1, source_target_pairs={{0,8},{1,9},{2,10},{3,11},{4,12},{5,13},{6,14},{7,15},{8,0},{9,1},... | collective-permute-start | bytes 294920 | tf_op jit(solution)/shard_map/ppermute | solution.py:778
  164.9 10.1 %collective-permute-start.32 = (bf16[96,512]{1,0:T(8,128)(2,1)S(1)}, bf16[96,512]{1,0:T(8,128)(2,1)S(1)}, u32[]{:S(2)}, u32[]{:S(2)}) collective-permute-start(bf16[96,512]{1,0:T(8,128)(2,1)S(1)} %add_convert_fusion.9), channel_id=1, source_target_pairs={{0,16},{1,17},{2,18},{3,19},{4,20},{5,21},{6,22},{7,23},{8,24},{9,... | collective-permute-start | bytes 294920 | tf_op jit(solution)/shard_map/ppermute | solution.py:778
  165.9 1.3 collective-permute-start.29
  166.3 3.8 %copy-start.22 = (bf16[4,512,512]{2,1,0:T(8,128)(2,1)}, bf16[4,512,512]{2,1,0:T(8,128)(2,1)S(1)}, u32[]{:S(2)}) copy-start(bf16[4,512,512]{2,1,0:T(8,128)(2,1)S(1)} %constant_dynamic-update-slice_fusion) | copy-start | bytes 6291460
  167.2 7.7 %collective-permute-start.33 = (bf16[96,512]{1,0:T(8,128)(2,1)S(1)}, bf16[96,512]{1,0:T(8,128)(2,1)S(1)}, u32[]{:S(2)}, u32[]{:S(2)}) collective-permute-start(bf16[96,512]{1,0:T(8,128)(2,1)S(1)} %add_convert_fusion.9), channel_id=1, source_target_pairs={{0,24},{1,25},{2,26},{3,27},{4,28},{5,29},{6,30},{7,31},{8,16},{9,... | collective-permute-start | bytes 294920 | tf_op jit(solution)/shard_map/ppermute | solution.py:778
  170.2 13.9 %copy-start = (bf16[4,512,512]{2,1,0:T(8,128)(2,1)}, bf16[4,512,512]{2,1,0:T(8,128)(2,1)S(1)}, u32[]{:S(2)}) copy-start(bf16[4,512,512]{2,1,0:T(8,128)(2,1)S(1)} %constant_dynamic-update-slice_fusion.1.refs_0_) | copy-start | bytes 6291460
  176.2 4.5 %copy-start.9 = (bf16[512,1024]{1,0:T(8,128)(2,1)}, bf16[512,1024]{1,0:T(8,128)(2,1)S(1)}, u32[]{:S(2)}) copy-start(bf16[512,1024]{1,0:T(8,128)(2,1)S(1)} %collective-permute-done.30.refs_1_) | copy-start | bytes 3145732
  176.4 14.7 %copy-start.6 = (bf16[400,512]{1,0:T(8,128)(2,1)}, bf16[400,512]{1,0:T(8,128)(2,1)S(1)}, u32[]{:S(2)}) copy-start(bf16[400,512]{1,0:T(8,128)(2,1)S(1)} %pad_maximum_fusion.refs_0_) | copy-start | bytes 1228804
  176.4 14.6 %collective-permute-start.34 = (bf16[400,512]{1,0:T(8,128)(2,1)S(1)}, bf16[400,512]{1,0:T(8,128)(2,1)S(1)}, u32[]{:S(2)}, u32[]{:S(2)}) collective-permute-start(bf16[400,512]{1,0:T(8,128)(2,1)S(1)} %pad_maximum_fusion.refs_0_), channel_id=1, source_target_pairs={{0,2},{1,3},{2,0},{3,1},{4,6},{5,7},{6,4},{7,5},{8,10},{9,11},{10,... | collective-permute-start | bytes 1228808 | tf_op jit(solution)/shard_map/ppermute | solution.py:778
  177.9 19.6 %collective-permute-start.35 = (bf16[400,512]{1,0:T(8,128)(2,1)S(1)}, bf16[400,512]{1,0:T(8,128)(2,1)}, u32[]{:S(2)}, u32[]{:S(2)}) collective-permute-start(bf16[400,512]{1,0:T(8,128)(2,1)S(1)} %pad_maximum_fusion.refs_0_), channel_id=1, source_target_pairs={{0,4},{1,5},{2,6},{3,7},{4,0},{5,1},{6,2},{7,3},{8,12},{9,13},{10,... | collective-permute-start | bytes 1228808 | tf_op jit(solution)/shard_map/ppermute | solution.py:778
  178.7 18.8 %collective-permute-start.36 = (bf16[400,512]{1,0:T(8,128)(2,1)S(1)}, bf16[400,512]{1,0:T(8,128)(2,1)}, u32[]{:S(2)}, u32[]{:S(2)}) collective-permute-start(bf16[400,512]{1,0:T(8,128)(2,1)S(1)} %pad_maximum_fusion.refs_0_), channel_id=1, source_target_pairs={{0,6},{1,7},{2,4},{3,5},{4,2},{5,3},{6,0},{7,1},{8,14},{9,15},{10,... | collective-permute-start | bytes 1228808 | tf_op jit(solution)/shard_map/ppermute | solution.py:778
  191.1 6.4 %copy-start.14 = (bf16[400,512]{1,0:T(8,128)(2,1)}, bf16[400,512]{1,0:T(8,128)(2,1)S(1)}, u32[]{:S(2)}) copy-start(bf16[400,512]{1,0:T(8,128)(2,1)S(1)} %collective-permute-done.34.refs_1_) | copy-start | bytes 1228804
  (2 other events, 1.6 us)

commit v3 on v2

--- a/solution.py
+++ b/solution.py
@@ -472,7 +472,7 @@
 def entry_kernel(
     core, own, got, order, back_order, gate_own, cand_own, gate_other, cand_other, middle_in, mixer_own,
     mixer_other, gain, taps, gain_two, bias_own, up_own, bias_other, up_other, mine_out, sent_out, short_out,
-    rim, head, sums,
+    rim, head, sums, packed,
 ):
     step = pl.program_id(1)
     steps = pl.num_programs(1)
@@ -525,13 +525,14 @@
         parts = [jnp.sum(totals * taps[...], axis=0, keepdims=True), totals * gain[...], gain_two[...]]
         for bias in (bias_own, up_own, bias_other, up_other):
             parts.append(jnp.sum(bias[...], axis=0, keepdims=True))
-        short_out[...] = jnp.zeros_like(short_out)
+        packed[...] = jnp.zeros_like(packed)
         row = 0
         for part in parts:
             for lane in range(0, part.shape[1], width):
                 some = min(width, part.shape[1])
-                short_out[row : row + part.shape[0], 0:some] = part[:, lane : lane + width]
+                packed[row : row + part.shape[0], 0:some] = part[:, lane : lane + width]
                 row += part.shape[0]
+        short_out[...] = packed[...].astype(low)
 
 
 def give(values, position, half_chunks, core, mine_out, sent_out):
@@ -600,9 +601,10 @@
                 pltpu.VMEM((chunk + 8 * (taps.shape[0] - 1), width), wide),
                 pltpu.VMEM((8 * (taps.shape[0] - 1), width), wide),
                 pltpu.VMEM((-(-taps.shape[0] // 8) * 8, width), wide),
+                pltpu.VMEM(short, wide),
             ],
         ),
-        out_shape=[*shapes, jax.ShapeDtypeStruct(short, wide)],
+        out_shape=[*shapes, jax.ShapeDtypeStruct(short, low)],
         compiler_params=params(60, 2),
         cost_estimate=cost(
             rows * width * 2 * mixers[0].shape[1], rows * mixers[0].shape[1] * 6
@@ -789,10 +791,12 @@
         count = 1 << len(bits)
         self.sends = [self.share(self.spot ^ mask, count).astype(low) for mask in range(1, count)]
 
+    def cuts(self, spot, count):
+        size = self.terms[0].shape[0] // count
+        return [lax.dynamic_slice_in_dim(term, spot * size, size) for term in self.terms]
+
     def share(self, spot, count):
-        size = self.terms[0].shape[0] // count
-        cuts = [lax.dynamic_slice_in_dim(term, spot * size, size) for term in self.terms]
-        return sum(cut.astype(wide) for cut in cuts)
+        return sum(cut.astype(wide) for cut in self.cuts(spot, count))
 
     def start(self):
         join, group = self.todo[0]
@@ -805,7 +809,11 @@
     def finish(self):
         join, group = self.todo.pop(0)
         if not join:
-            self.terms = [self.share(self.spot, 1 << len(group[0])), *self.got]
+            count = 1 << len(group[0])
+            if self.paired and len(self.terms) == 2:
+                self.terms = [*self.cuts(self.spot, count), *self.got]
+            else:
+                self.terms = [self.share(self.spot, count), *self.got]
             return
         parts = [self.piece] + self.got
         for bit in self.place(group):
@@ -851,14 +859,13 @@
     return parts[0]
 
 
-def beside(chains, work, *leads, loose=()):
+def beside(chains, work, *leads):
     chains = [chain for chain in chains if chain.todo]
-    begun = [*chains, *(chain for chain in loose if chain.todo)]
-    for chain in begun:
+    for chain in chains:
         chain.prepare()
-    held = hold(*leads, *(send for chain in begun for send in chain.sends))
+    held = hold(*leads, *(send for chain in chains for send in chain.sends))
     leads, sends = held[: len(leads)], list(held[len(leads) :])
-    for chain in begun:
+    for chain in chains:
         chain.sends, sends = sends[: len(chain.sends)], sends[len(chain.sends) :]
         chain.start()
     results = work(*leads)

time: 202 us -> 200 us (0.990)
    add x3 -> x2, other arithmetic: 8.35 us -> 5.72 us  [share(): return sum((cut.astype(wide) for cut in self.cuts(spot, count)))]
  transfers between devices with their start and end apart: 37 -> 37, of which waited for: 9 -> 9; matrix products, arithmetic and copies ran while one was open for 2% -> 2% of each run, Pallas kernels for 51% -> 52%
where the time goes in v3:
time: 200 us; the launch traced here: 199 us
  Pallas kernels  125 us (62%)
  starting transfers between devices  36 us (18%)
  waiting for transfers between devices  18.1 us (9%)
  other arithmetic  11.5 us (6%)
  local copies, waits for them, and re-layouts  7.55 us (4%)
    ppermute x22, starting transfers between devices, exchange(): return lax.ppermute(array, ('dp', 'tensor'), route)  32.7 us
    pallas_call x2, Pallas kernels, feed(): pl.pallas_call(kernel, grid_spec=pltpu.PrefetchScalarGridSpec(num_scalar_...  32.6 us
    pallas_call x2, Pallas kernels, scan_back(): pl.pallas_call(functools.partial(scan_kernel, windows, chunk), grid=(coun...  24.3 us
    pallas_call x1, Pallas kernels, forward(): pl.pallas_call(forward_kernel, grid_spec=pltpu.PrefetchScalarGridSpec(num...  19.6 us
    ppermute x22, waiting for transfers between devices, exchange(): return lax.ppermute(array, ('dp', 'tensor'), route)  15.6 us
    pallas_call x1, Pallas kernels, entry(): pl.pallas_call(entry_kernel, grid_spec=pltpu.PrefetchScalarGridSpec(num_s...  15 us
    pallas_call x2, Pallas kernels, leave(): pl.pallas_call(leave_kernel, grid_spec=pltpu.PrefetchScalarGridSpec(num_s...  14 us
    pallas_call x1, Pallas kernels, norm_back(): pl.pallas_call(norm_kernel, grid=(rows // chunk,), in_specs=[row(width),...  11.8 us
  transfers between devices with their start and end apart: 37, of which 9 were waited for; matrix products, arithmetic and copies ran while one was open for 2% of the time, Pallas kernels for 52%

profile of v3, /device:TPU:0, one launch (start us, length us, event | category | flops | bytes accessed | tf_op | source)
XLA Modules:
  0.0 199.5 jit_solution(9124148011544008737)
XLA Ops:
  0.7 1.4 constant_dynamic-slice_fusion.1
  2.2 0.5 collective-permute-start
  2.7 0.2 copy.27
  3.1 0.5 collective-permute-start.4
  3.6 0.4 collective-permute-start.2
  4.0 1.0 constant_dynamic-slice_fusion
  5.1 2.1 %collective-permute-done.2 = f32[512]{0:T(512)S(1)} collective-permute-done((f32[512]{0:T(512)S(1)}, f32[512]{0:T(512)S(1)}, u32[]{:S(2)}, u32[]{:S(2)}) %collective-permute-start.2) | collective-permute-done | bytes 2080 | tf_op jit(solution)/shard_map/ppermute | solution.py:743
  7.2 0.4 collective-permute-start.5
  7.8 0.4 collective-permute-start.6
  8.5 0.8 copy-done.7
  9.2 1.0 copy-done.8
  10.3 19.6 %forward_mixer.1 = (bf16[2048,512]{1,0:T(8,128)(2,1)}, f32[2048,1024]{1,0:T(8,128)}, bf16[2048,1024]{1,0:T(8,128)(2,1)}, bf16[2048,1024]{1,0:T(8,128)(2,1)}, bf1...) custom-call(s32[1]{0:T(128)} %bitcast.core, ...), custom_call_target="tpu_custom_call" | custom-call | flops 6442450944 | bytes 25165824 | tf_op jit(solution)/shard_map/forward_mixer/pallas_call | solution.py:182
  30.0 0.5 copy-done.26
  30.5 0.4 copy-done.2
  30.9 17.5 %feed_forward.2 = (bf16[2048,1024]{1,0:T(8,128)(2,1)}, bf16[2048,1024]{1,0:T(8,128)(2,1)}, f32[8,1024]{1,0:T(8,128)}, bf16[1024,1024]{1,0:T(8,128)(2,1)}, bf16[2048,512]{1,0:T(8,128)(2,1)}) custom-call(s32[1]{0:T(128)} %bitcast.core, bf16[4,512,512]{2,1,0:T(8,128)(2,1)} %refs_0_.1, bf16[2,512,512]{2,1,0:T(8,128)(2,1)} %collective-permute-done.5.refs_1_, ...), custom_call_target="tpu_custom_call" | custom-call | flops 8589934592 | bytes 8388608 | tf_op jit(solution)/shard_map/feed_forward/pallas_call | solution.py:308
  48.6 15.1 %feed_forward.3 = (bf16[2048,1024]{1,0:T(8,128)(2,1)}, bf16[2048,1024]{1,0:T(8,128)(2,1)}, f32[8,1024]{1,0:T(8,128)}, f32[1024,1024]{1,0:T(8,128)}) custom-call(s32[1]{0:T(128)} %bitcast.core, bf16[2048,512]{1,0:T(8,128)(2,1)} %get-tuple-element.143.refs_0_.tangent, bf16[2048,512]{1,0:T(8,128)(2,1)} %get-tuple-element.140.refs_3_.refs_1_, ...), custom_call_target="tpu_custom_call" | custom-call | flops 8589934592 | bytes 8388608 | tf_op jit(solution)/shard_map/feed_forward/pallas_call | solution.py:308
  63.7 1.9 add_convert_fusion
  65.7 2.8 %collective-permute-start.10 = (bf16[512,1024]{1,0:T(8,128)(2,1)S(1)}, bf16[512,1024]{1,0:T(8,128)(2,1)}, u32[]{:S(2)}, u32[]{:S(2)}) collective-permute-start(bf16[512,1024]{1,0:T(8,128)(2,1)S(1)} %add_convert_fusion), channel_id=1, source_target_pairs={{0,2},{1,5},{2,0},{3,7},{4,6},{5,1},{6,4},{7,3},{8,10},{9,13},{10,... | collective-permute-start | bytes 3145736 | tf_op jit(solution)/shard_map/ppermute | solution.py:780
  68.5 11.8 %norm_back.1 = (f32[2048,512]{1,0:T(8,128)}, bf16[2048,512]{1,0:T(8,128)(2,1)}, f32[1,512]{1,0:T(1,128)}) custom-call(bf16[2048,512]{1,0:T(8,128)(2,1)} %get-tuple-element.143.refs_0_.tangent, bf16[2048,1024]{1,0:T(8,128)(2,1)} %get-tuple-element.149.back_own, bf16[2048,1024]{1,0:T(8,128)(2,1)} %get-tuple-element.150.back_other, ...), custom_call_target="tpu_custom_call" | custom-call | flops 4294967296 | bytes 25165824 | tf_op jit(solution)/shard_map/norm_back/pallas_call | solution.py:349
  80.3 1.1 collective-permute-done.10
  81.4 2.5 %convert_add_fusion = (f32[256,1024]{1,0:T(8,128)S(1)}, bf16[256,1024]{1,0:T(8,128)(2,1)S(1)}) fusion(f32[1024,1024]{1,0:T(8,128)} %get-tuple-element.147, s32[]{:T(128)S(6)} %dynamic_slice.144, bf16[512,1024]{1,0:T(8,128)(2,1)} %collective-permute-done.10, s32[]{:T(128)S(6)} %select_n.173, bf16[1024,1024]{1,0:T(8,128)(2,1)S(1)} %collective-permute-done.9, ...), kind=kLoop, calls=%fused_computation.2 | loop fusion | flops 2359296 | bytes 5767184 | tf_op jit(solution)/shard_map/add | solution.py:799
  83.8 2.1 %collective-permute-start.11 = (bf16[256,1024]{1,0:T(8,128)(2,1)S(1)}, bf16[256,1024]{1,0:T(8,128)(2,1)S(1)}, u32[]{:S(2)}, u32[]{:S(2)}) collective-permute-start(bf16[256,1024]{1,0:T(8,128)(2,1)S(1)} %get-tuple-element.169), channel_id=1, source_target_pairs={{0,4},{1,3},{2,6},{3,1},{4,0},{5,7},{6,2},{7,5},{8,12},{9,11},{10,... | collective-permute-start | bytes 1572872 | tf_op jit(solution)/shard_map/ppermute | solution.py:780
  86.0 11.9 %scan_back.2 = (bf16[2048,512]{1,0:T(8,128)(2,1)}, bf16[2048,512]{1,0:T(8,128)(2,1)}, f32[2,1,512]{2,1,0:T(1,128)}, f32[8,512]{1,0:T(8,128)}, bf16[1536,512]{1,0:T(8,128)(2,1)}) custom-call(bf16[2048,512]{1,0:T(8,128)(2,1)} %get-tuple-element.173.mixed, bf16[2048,512]{1,0:T(8,128)(2,1)} %get-tuple-element.159.filtered, bf16[512,512]{1,0:T(8,128)(2,1)} %copy-done.12, ...), custom_call_target="tpu_custom_call" | custom-call | flops 4294967296 | bytes 14680064 | tf_op jit(solution)/shard_map/scan_back/pallas_call | solution.py:439
  98.1 1.6 collective-permute-start.12
  99.7 2.6 %collective-permute-start.13 = (bf16[64,1024]{1,0:T(8,128)(2,1)S(1)}, bf16[64,1024]{1,0:T(8,128)(2,1)S(1)}, u32[]{:S(2)}, u32[]{:S(2)}) collective-permute-start(bf16[64,1024]{1,0:T(8,128)(2,1)S(1)} %get-tuple-element.180), channel_id=1, source_target_pairs={{0,16},{1,17},{2,18},{3,19},{4,20},{5,21},{6,22},{7,23},{8,24},{9,... | collective-permute-start | bytes 393224 | tf_op jit(solution)/shard_map/ppermute | solution.py:780
  102.3 0.2 collective-permute-start.14
  102.5 12.4 %scan_back.3 = (bf16[2048,512]{1,0:T(8,128)(2,1)}, bf16[2048,512]{1,0:T(8,128)(2,1)}, f32[2,1,512]{2,1,0:T(1,128)}, f32[8,512]{1,0:T(8,128)}, f32[1536,512]{1,0:T(8,128)}) custom-call(bf16[2048,512]{1,0:T(8,128)(2,1)} %get-tuple-element.173.mixed, bf16[2048,512]{1,0:T(8,128)(2,1)} %get-tuple-element.159.filtered, bf16[512,512]{1,0:T(8,128)(2,1)} %read.1, ...), custom_call_target="tpu_custom_call" | custom-call | flops 4294967296 | bytes 14680064 | tf_op jit(solution)/shard_map/scan_back/pallas_call | solution.py:439
  115.1 3.3 %convert_add_fusion.1 = (f32[384,512]{1,0:T(8,128)S(1)}, bf16[384,512]{1,0:T(8,128)(2,1)S(1)}, bf16[384,512]{1,0:T(8,128)(2,1)}, bf16[384,512]{1,0:T(8,128)(2,1)}) fusion(f32[1536,512]{1,0:T(8,128)} %get-tuple-element.184, s32[]{:T(128)S(6)} %select_n.178, bf16[1536,512]{1,0:T(8,128)(2,1)S(1)} %collective-permute-done.15, s32[]{:T(128)S(6)} %select_n.183, ...), kind=kLoop, calls=%fused_computation.7 | loop fusion | flops 2162688 | bytes 6684688 | tf_op jit(solution)/shard_map/add | solution.py:799
  118.4 0.6 collective-permute-start.16
  119.0 3.4 %collective-permute-start.17 = (bf16[64,1024]{1,0:T(8,128)(2,1)S(1)}, bf16[64,1024]{1,0:T(8,128)(2,1)S(1)}, u32[]{:S(2)}, u32[]{:S(2)}) collective-permute-start(bf16[64,1024]{1,0:T(8,128)(2,1)S(1)} %add_convert_fusion.5), channel_id=1, source_target_pairs={{0,16},{1,17},{2,18},{3,19},{4,20},{5,21},{6,22},{7,23},{8,24},{9,... | collective-permute-start | bytes 393224 | tf_op jit(solution)/shard_map/ppermute | solution.py:780
  122.4 0.4 collective-permute-start.18
  122.8 1.5 collective-permute-start.19
  124.2 0.5 collective-permute-start.20
  124.8 0.5 collective-permute-done.16
  125.2 1.4 collective-permute-start.21
  126.6 15.0 %input_gradient.1 = (bf16[4,512,512]{2,1,0:T(8,128)(2,1)}, bf16[2,512,512]{2,1,0:T(8,128)(2,1)}, bf16[16,512]{1,0:T(8,128)(2,1)}) custom-call(s32[1]{0:T(128)} %bitcast.core, bf16[4,512,512]{2,1,0:T(8,128)(2,1)} %own.3, bf16[2,512,512]{2,1,0:T(8,128)(2,1)} %copy-done.7, bf16[512,512]{1,0:T(8,128)(2,1)} %get-tuple-element.139.refs_2_.order, ...), custom_call_target="tpu_custom_call" | custom-call | flops 4294967296 | bytes 12582912 | tf_op jit(solution)/shard_map/input_gradient/pallas_call | solution.py:578
  141.6 0.9 collective-permute-done.20
  143.0 0.2 copy-done.16
  143.4 0.8 collective-permute-start.24
  144.2 0.4 collective-permute-start.25
  144.6 3.7 %collective-permute-start.26 = (bf16[112,512]{1,0:T(8,128)(2,1)S(1)}, bf16[112,512]{1,0:T(8,128)(2,1)S(1)}, u32[]{:S(2)}, u32[]{:S(2)}) collective-permute-start(bf16[112,512]{1,0:T(8,128)(2,1)S(1)} %get-tuple-element.223), channel_id=1, source_target_pairs={{0,16},{1,17},{2,18},{3,19},{4,20},{5,21},{6,22},{7,23},{8,24},{9,... | collective-permute-start | bytes 344072 | tf_op jit(solution)/shard_map/ppermute | solution.py:780
  148.2 1.1 collective-permute-start.27
  149.4 7.0 %block_output.2 = bf16[2,512,512]{2,1,0:T(8,128)(2,1)} custom-call(s32[1]{0:T(128)} %bitcast.core, bf16[512,512]{1,0:T(8,128)(2,1)} %get-tuple-element.138.back_order, bf16[2048,1024]{1,0:T(8,128)(2,1)} %get-tuple-element.246.active_own, bf16[2048,1024]{1,0:T(8,128)(2,1)} %get-tuple-element.218.active_other, ...), custom_call_target="tpu_custom_call" | custom-call | flops 2147483648 | bytes 6291456 | tf_op jit(solution)/shard_map/block_output/pallas_call | solution.py:633
  156.3 0.8 collective-permute-done.26
  157.2 1.1 add_convert_fusion.9
  158.3 0.5 maximum_select_fusion.refs_0_
  158.8 1.4 collective-permute-start.30
  160.3 2.1 %collective-permute-start.31 = (bf16[96,512]{1,0:T(8,128)(2,1)S(1)}, bf16[96,512]{1,0:T(8,128)(2,1)S(1)}, u32[]{:S(2)}, u32[]{:S(2)}) collective-permute-start(bf16[96,512]{1,0:T(8,128)(2,1)S(1)} %add_convert_fusion.9), channel_id=1, source_target_pairs={{0,8},{1,9},{2,10},{3,11},{4,12},{5,13},{6,14},{7,15},{8,0},{9,1},... | collective-permute-start | bytes 294920 | tf_op jit(solution)/shard_map/ppermute | solution.py:780
  162.4 1.0 collective-permute-start.32
  163.5 0.2 collective-permute-start.29
  163.8 0.7 maximum_select_fusion.7
  164.5 0.3 collective-permute-done.29
  164.7 1.4 collective-permute-start.33
  166.3 1.3 constant_dynamic-update-slice_fusion.refs_0_
  167.7 4.7 %collective-permute-done.32 = bf16[96,512]{1,0:T(8,128)(2,1)S(1)} collective-permute-done((bf16[96,512]{1,0:T(8,128)(2,1)S(1)}, bf16[96,512]{1,0:T(8,128)(2,1)S(1)}, u32[]{:S(2)}, u32[]{:S(2)}) %collective-permute-start.32) | collective-permute-done | bytes 98336 | tf_op jit(solution)/shard_map/ppermute | solution.py:780
  172.4 1.3 collective-permute-done.30.refs_1_
  174.0 1.4 collective-permute-start.34
  175.4 0.9 collective-permute-start.35
  176.3 1.3 collective-permute-start.36
  177.5 0.7 pad_add_fusion.place
  178.2 3.4 %finish_feed.1 = (f32[1024,512]{1,0:T(8,128)}, f32[512,1024]{1,0:T(8,128)}) custom-call(s32[1]{0:T(128)} %bitcast.9.place, bf16[512,1024]{1,0:T(8,128)(2,1)} %copy-done.4, bf16[512,1024]{1,0:T(8,128)(2,1)} %copy-done.9), custom_call_target="tpu_custom_call" | custom-call | tf_op jit(solution)/shard_map/finish_feed/pallas_call | solution.py:680
  181.6 7.0 %block_output.3 = bf16[4,512,512]{2,1,0:T(8,128)(2,1)} custom-call(s32[1]{0:T(128)} %bitcast.core, bf16[512,512]{1,0:T(8,128)(2,1)} %get-tuple-element.138.back_order, bf16[2048,1024]{1,0:T(8,128)(2,1)} %get-tuple-element.246.active_own, bf16[2048,1024]{1,0:T(8,128)(2,1)} %get-tuple-element.218.active_other, ...), custom_call_target="tpu_custom_call", output_to_operand_aliasing={{}: (7, {})} | custom-call | flops 2147483648 | bytes 6291456 | tf_op jit(solution)/shard_map/block_output/pallas_call | solution.py:633
  188.6 6.3 %collective-permute-done.35.refs_2_ = bf16[400,512]{1,0:T(8,128)(2,1)} collective-permute-done((bf16[400,512]{1,0:T(8,128)(2,1)S(1)}, bf16[400,512]{1,0:T(8,128)(2,1)}, u32[]{:S(2)}, u32[]{:S(2)}) %collective-permute-start.35) | collective-permute-done | bytes 409632 | tf_op jit(solution)/shard_map/ppermute | solution.py:780
  195.0 4.5 %finish_mixer.1 = (f32[512,2,512]{2,1,0:T(2,128)}, f32[512,512]{1,0:T(8,128)}, f32[1,512]{1,0:T(1,128)}, f32[4,512]{1,0:T(4,128)}, f32[1,512]{1,0:T(1,128)}, /*index=5*/f32[1,512]{1,0:T(1,128)}, f32[1,1024]{1,0:T(1,128)}) custom-call(s32[2]{0:T(128)} %pad_add_fusion.place, bf16[400,512]{1,0:T(8,128)(2,1)} %copy-done.5, bf16[400,512]{1,0:T(8,128)(2,1)} %copy-done.14, ...), custom_call_target="tpu_custom_call" | custom-call | tf_op jit(solution)/shard_map/finish_mixer/pallas_call | solution.py:720
  (110 shorter events, 2.4 us)
Async XLA Ops:
  0.6 2.0 %copy-start.10 = (bf16[512,2,512]{2,1,0:T(2,128)(2,1)S(1)}, bf16[512,2,512]{2,1,0:T(2,128)(2,1)}, u32[]{:S(2)}) copy-start(bf16[512,2,512]{2,1,0:T(2,128)(2,1)} %param.16) | copy-start | bytes 3145732
  0.7 2.4 %copy-start.11 = (bf16[512,512]{1,0:T(8,128)(2,1)S(1)}, bf16[512,512]{1,0:T(8,128)(2,1)}, u32[]{:S(2)}) copy-start(bf16[512,512]{1,0:T(8,128)(2,1)} %read.1) | copy-start | bytes 1572868
  0.7 2.9 %copy-start.23 = (f32[4,512]{1,0:T(4,128)S(1)}, f32[4,512]{1,0:T(4,128)}, u32[]{:S(2)}) copy-start(f32[4,512]{1,0:T(4,128)} %start_own.1) | copy-start | bytes 24580
  0.7 2.9 %copy-start.27 = (f32[512]{0:T(512)S(1)}, f32[512]{0:T(512)}, u32[]{:S(2)}) copy-start(f32[512]{0:T(512)} %param.17) | copy-start | bytes 6148
  0.7 3.4 %copy-start.13 = (bf16[4,512,512]{2,1,0:T(8,128)(2,1)S(1)}, bf16[4,512,512]{2,1,0:T(8,128)(2,1)}, u32[]{:S(2)}) copy-start(bf16[4,512,512]{2,1,0:T(8,128)(2,1)} %refs_0_.1) | copy-start | bytes 6291460
  2.2 6.1 %collective-permute-start = (bf16[2,512,512]{2,1,0:T(8,128)(2,1)S(1)}, bf16[2,512,512]{2,1,0:T(8,128)(2,1)S(1)}, u32[]{:S(2)}, u32[]{:S(2)}) collective-permute-start(bf16[2,512,512]{2,1,0:T(8,128)(2,1)S(1)} %constant_dynamic-slice_fusion.1), channel_id=1, source_target_pairs={{0,1},{1,0},{2,3},{3,2},{4,5},{5,4},{6,7},{7,6},{8,9},{9,8},{10,11... | collective-permute-start | bytes 3145736 | tf_op jit(solution)/shard_map/ppermute | solution.py:743
  2.7 4.9 %copy-start.1 = (bf16[1024,512]{1,0:T(8,128)(2,1)S(1)}, bf16[1024,512]{1,0:T(8,128)(2,1)}, u32[]{:S(2)}) copy-start(bf16[1024,512]{1,0:T(8,128)(2,1)} %down_own.3) | copy-start | bytes 3145732
  2.7 5.1 %copy-start.6 = (bf16[512,1024]{1,0:T(8,128)(2,1)S(1)}, bf16[512,1024]{1,0:T(8,128)(2,1)}, u32[]{:S(2)}) copy-start(bf16[512,1024]{1,0:T(8,128)(2,1)} %up_own.1) | copy-start | bytes 3145732
  2.7 5.6 %copy-start.25 = (f32[1024]{0:T(1024)S(1)}, f32[1024]{0:T(1024)}, u32[]{:S(2)}) copy-start(f32[1024]{0:T(1024)} %param.21) | copy-start | bytes 12292
  2.9 4.9 %copy-start.3 = (bf16[64,8,2,512]{3,1,2,0:T(8,128)(2,1)}, bf16[64,8,2,512]{3,1,2,0:T(8,128)(2,1)S(1)}, u32[]{:S(2)}) copy-start(bf16[64,8,2,512]{3,1,2,0:T(8,128)(2,1)S(1)} %copy.27) | copy-start | bytes 3145732
  2.9 5.5 %collective-permute-start.1 = (bf16[512,1024]{1,0:T(8,128)(2,1)S(1)}, bf16[512,1024]{1,0:T(8,128)(2,1)S(1)}, u32[]{:S(2)}, u32[]{:S(2)}) collective-permute-start(bf16[512,1024]{1,0:T(8,128)(2,1)S(1)} %bitcast.22), channel_id=1, source_target_pairs={{0,1},{1,0},{2,3},{3,2},{4,5},{5,4},{6,7},{7,6},{8,9},{9,8},{10,11... | collective-permute-start | bytes 3145736 | tf_op jit(solution)/shard_map/ppermute | solution.py:743
  3.1 4.7 %collective-permute-start.4 = (bf16[512,512]{1,0:T(8,128)(2,1)S(1)}, bf16[512,512]{1,0:T(8,128)(2,1)S(1)}, u32[]{:S(2)}, u32[]{:S(2)}) collective-permute-start(bf16[512,512]{1,0:T(8,128)(2,1)S(1)} %copy-done.11), channel_id=1, source_target_pairs={{0,1},{1,0},{2,3},{3,2},{4,5},{5,4},{6,7},{7,6},{8,9},{9,8},{10,11... | collective-permute-start | bytes 1572872 | tf_op jit(solution)/shard_map/ppermute | solution.py:743
  3.5 4.1 %collective-permute-start.3 = (f32[4,512]{1,0:T(4,128)S(1)}, f32[4,512]{1,0:T(4,128)S(1)}, u32[]{:S(2)}, u32[]{:S(2)}) collective-permute-start(f32[4,512]{1,0:T(4,128)S(1)} %copy-done.23), channel_id=1, source_target_pairs={{0,1},{1,0},{2,3},{3,2},{4,5},{5,4},{6,7},{7,6},{8,9},{9,8},{10,11... | collective-permute-start | bytes 24584 | tf_op jit(solution)/shard_map/ppermute | solution.py:743
  3.6 3.6 %collective-permute-start.2 = (f32[512]{0:T(512)S(1)}, f32[512]{0:T(512)S(1)}, u32[]{:S(2)}, u32[]{:S(2)}) collective-permute-start(f32[512]{0:T(512)S(1)} %copy-done.27), channel_id=1, source_target_pairs={{0,1},{1,0},{2,3},{3,2},{4,5},{5,4},{6,7},{7,6},{8,9},{9,8},{10,11... | collective-permute-start | bytes 6152 | tf_op jit(solution)/shard_map/ppermute | solution.py:743
  7.2 3.0 %copy-start.28 = (f32[512]{0:T(512)}, f32[512]{0:T(512)S(1)}, u32[]{:S(2)}) copy-start(f32[512]{0:T(512)S(1)} %collective-permute-done.2) | copy-start | bytes 6148
  7.2 22.7 %collective-permute-start.5 = (bf16[2,512,512]{2,1,0:T(8,128)(2,1)}, bf16[2,512,512]{2,1,0:T(8,128)(2,1)}, u32[]{:S(2)}, u32[]{:S(2)}) collective-permute-start(bf16[2,512,512]{2,1,0:T(8,128)(2,1)} %constant_dynamic-slice_fusion), channel_id=1, source_target_pairs={{0,1},{1,0},{2,3},{3,2},{4,5},{5,4},{6,7},{7,6},{8,9},{9,8},{10,11... | collective-permute-start | bytes 3145736 | tf_op jit(solution)/shard_map/ppermute | solution.py:743
  7.6 2.7 %copy-start.24 = (f32[4,512]{1,0:T(4,128)}, f32[4,512]{1,0:T(4,128)S(1)}, u32[]{:S(2)}) copy-start(f32[4,512]{1,0:T(4,128)S(1)} %collective-permute-done.3.start_other) | copy-start | bytes 24580
  7.6 22.3 %collective-permute-start.8 = (bf16[1024,512]{1,0:T(8,128)(2,1)S(1)}, bf16[1024,512]{1,0:T(8,128)(2,1)S(1)}, u32[]{:S(2)}, u32[]{:S(2)}) collective-permute-start(bf16[1024,512]{1,0:T(8,128)(2,1)S(1)} %copy-done.1), channel_id=1, source_target_pairs={{0,1},{1,0},{2,3},{3,2},{4,5},{5,4},{6,7},{7,6},{8,9},{9,8},{10,11... | collective-permute-start | bytes 3145736 | tf_op jit(solution)/shard_map/ppermute | solution.py:743
  7.8 2.4 %copy-start.12 = (bf16[512,512]{1,0:T(8,128)(2,1)}, bf16[512,512]{1,0:T(8,128)(2,1)S(1)}, u32[]{:S(2)}) copy-start(bf16[512,512]{1,0:T(8,128)(2,1)S(1)} %collective-permute-done.4.read_other.read) | copy-start | bytes 1572868
  7.8 22.1 %collective-permute-start.6 = (bf16[512,1024]{1,0:T(8,128)(2,1)S(1)}, bf16[512,1024]{1,0:T(8,128)(2,1)}, u32[]{:S(2)}, u32[]{:S(2)}) collective-permute-start(bf16[512,1024]{1,0:T(8,128)(2,1)S(1)} %copy-done.6), channel_id=1, source_target_pairs={{0,1},{1,0},{2,3},{3,2},{4,5},{5,4},{6,7},{7,6},{8,9},{9,8},{10,11... | collective-permute-start | bytes 3145736 | tf_op jit(solution)/shard_map/ppermute | solution.py:743
  8.3 1.0 copy-start.7
  8.3 21.6 %collective-permute-start.7 = (f32[1024]{0:T(1024)S(1)}, f32[1024]{0:T(1024)S(1)}, u32[]{:S(2)}, u32[]{:S(2)}) collective-permute-start(f32[1024]{0:T(1024)S(1)} %copy-done.25), channel_id=1, source_target_pairs={{0,1},{1,0},{2,3},{3,2},{4,5},{5,4},{6,7},{7,6},{8,9},{9,8},{10,11... | collective-permute-start | bytes 12296 | tf_op jit(solution)/shard_map/ppermute | solution.py:743
  9.2 1.0 copy-start.8
  29.9 1.0 copy-start.2
  48.5 15.2 %collective-permute-start.9 = (bf16[1024,1024]{1,0:T(8,128)(2,1)}, bf16[1024,1024]{1,0:T(8,128)(2,1)S(1)}, u32[]{:S(2)}, u32[]{:S(2)}) collective-permute-start(bf16[1024,1024]{1,0:T(8,128)(2,1)} %get-tuple-element.146), channel_id=1, source_target_pairs={{0,1},{1,0},{2,3},{3,2},{4,5},{5,4},{6,7},{7,6},{8,9},{9,8},{10,11... | collective-permute-start | bytes 6291464 | tf_op jit(solution)/shard_map/ppermute | solution.py:743
  65.7 15.7 %collective-permute-start.10 = (bf16[512,1024]{1,0:T(8,128)(2,1)S(1)}, bf16[512,1024]{1,0:T(8,128)(2,1)}, u32[]{:S(2)}, u32[]{:S(2)}) collective-permute-start(bf16[512,1024]{1,0:T(8,128)(2,1)S(1)} %add_convert_fusion), channel_id=1, source_target_pairs={{0,2},{1,5},{2,0},{3,7},{4,6},{5,1},{6,4},{7,3},{8,10},{9,13},{10,... | collective-permute-start | bytes 3145736 | tf_op jit(solution)/shard_map/ppermute | solution.py:780
  83.8 14.0 %collective-permute-start.11 = (bf16[256,1024]{1,0:T(8,128)(2,1)S(1)}, bf16[256,1024]{1,0:T(8,128)(2,1)S(1)}, u32[]{:S(2)}, u32[]{:S(2)}) collective-permute-start(bf16[256,1024]{1,0:T(8,128)(2,1)S(1)} %get-tuple-element.169), channel_id=1, source_target_pairs={{0,4},{1,3},{2,6},{3,1},{4,0},{5,7},{6,2},{7,5},{8,12},{9,11},{10,... | collective-permute-start | bytes 1572872 | tf_op jit(solution)/shard_map/ppermute | solution.py:780
  97.8 17.3 %collective-permute-start.15 = (bf16[1536,512]{1,0:T(8,128)(2,1)}, bf16[1536,512]{1,0:T(8,128)(2,1)S(1)}, u32[]{:S(2)}, u32[]{:S(2)}) collective-permute-start(bf16[1536,512]{1,0:T(8,128)(2,1)} %get-tuple-element.183), channel_id=1, source_target_pairs={{0,1},{1,0},{2,3},{3,2},{4,5},{5,4},{6,7},{7,6},{8,9},{9,8},{10,11... | collective-permute-start | bytes 4718600 | tf_op jit(solution)/shard_map/ppermute | solution.py:743
  98.1 16.9 %collective-permute-start.12 = (bf16[64,1024]{1,0:T(8,128)(2,1)S(1)}, bf16[64,1024]{1,0:T(8,128)(2,1)S(1)}, u32[]{:S(2)}, u32[]{:S(2)}) collective-permute-start(bf16[64,1024]{1,0:T(8,128)(2,1)S(1)} %get-tuple-element.179), channel_id=1, source_target_pairs={{0,8},{1,9},{2,10},{3,11},{4,12},{5,13},{6,14},{7,15},{8,0},{9,1},... | collective-permute-start | bytes 393224 | tf_op jit(solution)/shard_map/ppermute | solution.py:780
  99.7 15.2 %collective-permute-start.13 = (bf16[64,1024]{1,0:T(8,128)(2,1)S(1)}, bf16[64,1024]{1,0:T(8,128)(2,1)S(1)}, u32[]{:S(2)}, u32[]{:S(2)}) collective-permute-start(bf16[64,1024]{1,0:T(8,128)(2,1)S(1)} %get-tuple-element.180), channel_id=1, source_target_pairs={{0,16},{1,17},{2,18},{3,19},{4,20},{5,21},{6,22},{7,23},{8,24},{9,... | collective-permute-start | bytes 393224 | tf_op jit(solution)/shard_map/ppermute | solution.py:780
  102.3 12.7 %collective-permute-start.14 = (bf16[64,1024]{1,0:T(8,128)(2,1)S(1)}, bf16[64,1024]{1,0:T(8,128)(2,1)S(1)}, u32[]{:S(2)}, u32[]{:S(2)}) collective-permute-start(bf16[64,1024]{1,0:T(8,128)(2,1)S(1)} %get-tuple-element.181), channel_id=1, source_target_pairs={{0,24},{1,25},{2,26},{3,27},{4,28},{5,29},{6,30},{7,31},{8,16},{9,... | collective-permute-start | bytes 393224 | tf_op jit(solution)/shard_map/ppermute | solution.py:780
  115.1 3.9 %copy-start.19 = (f32[2,1,512]{2,1,0:T(1,128)S(1)}, f32[2,1,512]{2,1,0:T(1,128)}, u32[]{:S(2)}) copy-start(f32[2,1,512]{2,1,0:T(1,128)} %get-tuple-element.211) | copy-start | bytes 12292
  118.4 6.8 %collective-permute-start.16 = (bf16[64,1024]{1,0:T(8,128)(2,1)S(1)}, bf16[64,1024]{1,0:T(8,128)(2,1)S(1)}, u32[]{:S(2)}, u32[]{:S(2)}) collective-permute-start(bf16[64,1024]{1,0:T(8,128)(2,1)S(1)} %add_convert_fusion.5), channel_id=1, source_target_pairs={{0,8},{1,9},{2,10},{3,11},{4,12},{5,13},{6,14},{7,15},{8,0},{9,1},... | collective-permute-start | bytes 393224 | tf_op jit(solution)/shard_map/ppermute | solution.py:780
  119.0 22.6 %collective-permute-start.17 = (bf16[64,1024]{1,0:T(8,128)(2,1)S(1)}, bf16[64,1024]{1,0:T(8,128)(2,1)S(1)}, u32[]{:S(2)}, u32[]{:S(2)}) collective-permute-start(bf16[64,1024]{1,0:T(8,128)(2,1)S(1)} %add_convert_fusion.5), channel_id=1, source_target_pairs={{0,16},{1,17},{2,18},{3,19},{4,20},{5,21},{6,22},{7,23},{8,24},{9,... | collective-permute-start | bytes 393224 | tf_op jit(solution)/shard_map/ppermute | solution.py:780
  122.4 19.2 %collective-permute-start.18 = (bf16[64,1024]{1,0:T(8,128)(2,1)S(1)}, bf16[64,1024]{1,0:T(8,128)(2,1)S(1)}, u32[]{:S(2)}, u32[]{:S(2)}) collective-permute-start(bf16[64,1024]{1,0:T(8,128)(2,1)S(1)} %add_convert_fusion.5), channel_id=1, source_target_pairs={{0,24},{1,25},{2,26},{3,27},{4,28},{5,29},{6,30},{7,31},{8,16},{9,... | collective-permute-start | bytes 393224 | tf_op jit(solution)/shard_map/ppermute | solution.py:780
  122.8 18.9 %collective-permute-start.19 = (bf16[384,512]{1,0:T(8,128)(2,1)}, bf16[384,512]{1,0:T(8,128)(2,1)S(1)}, u32[]{:S(2)}, u32[]{:S(2)}) collective-permute-start(bf16[384,512]{1,0:T(8,128)(2,1)} %get-tuple-element.204), channel_id=1, source_target_pairs={{0,2},{1,3},{2,0},{3,1},{4,6},{5,7},{6,4},{7,5},{8,10},{9,11},{10,... | collective-permute-start | bytes 1179656 | tf_op jit(solution)/shard_map/ppermute | solution.py:780
  124.2 18.3 %collective-permute-start.20 = (bf16[384,512]{1,0:T(8,128)(2,1)}, bf16[384,512]{1,0:T(8,128)(2,1)S(1)}, u32[]{:S(2)}, u32[]{:S(2)}) collective-permute-start(bf16[384,512]{1,0:T(8,128)(2,1)} %get-tuple-element.205), channel_id=1, source_target_pairs={{0,4},{1,5},{2,6},{3,7},{4,0},{5,1},{6,2},{7,3},{8,12},{9,13},{10,... | collective-permute-start | bytes 1179656 | tf_op jit(solution)/shard_map/ppermute | solution.py:780
  125.2 17.3 %collective-permute-start.21 = (bf16[384,512]{1,0:T(8,128)(2,1)S(1)}, bf16[384,512]{1,0:T(8,128)(2,1)S(1)}, u32[]{:S(2)}, u32[]{:S(2)}) collective-permute-start(bf16[384,512]{1,0:T(8,128)(2,1)S(1)} %get-tuple-element.206), channel_id=1, source_target_pairs={{0,6},{1,7},{2,4},{3,5},{4,2},{5,3},{6,0},{7,1},{8,14},{9,15},{10,... | collective-permute-start | bytes 1179656 | tf_op jit(solution)/shard_map/ppermute | solution.py:780
  141.6 1.4 copy-start.18
  141.6 1.4 copy-start.15
  142.5 0.9 copy-start.17
  142.5 1.7 copy-start.20
  143.4 13.8 %collective-permute-start.23 = (bf16[2,512,512]{2,1,0:T(8,128)(2,1)}, bf16[2,512,512]{2,1,0:T(8,128)(2,1)S(1)}, u32[]{:S(2)}, u32[]{:S(2)}) collective-permute-start(bf16[2,512,512]{2,1,0:T(8,128)(2,1)} %get-tuple-element.220), channel_id=1, source_target_pairs={{0,1},{1,0},{2,3},{3,2},{4,5},{5,4},{6,7},{7,6},{8,9},{9,8},{10,11... | collective-permute-start | bytes 3145736 | tf_op jit(solution)/shard_map/ppermute | solution.py:743
  143.4 13.7 %collective-permute-start.24 = (bf16[256,1024]{1,0:T(8,128)(2,1)S(1)}, bf16[256,1024]{1,0:T(8,128)(2,1)S(1)}, u32[]{:S(2)}, u32[]{:S(2)}) collective-permute-start(bf16[256,1024]{1,0:T(8,128)(2,1)S(1)} %maximum_select_fusion.1), channel_id=1, source_target_pairs={{0,4},{1,3},{2,6},{3,1},{4,0},{5,7},{6,2},{7,5},{8,12},{9,11},{10,... | collective-permute-start | bytes 1572872 | tf_op jit(solution)/shard_map/ppermute | solution.py:780
  144.2 4.1 %collective-permute-start.22 = (f32[2,512]{1,0:T(2,128)S(1)}, f32[2,512]{1,0:T(2,128)S(1)}, u32[]{:S(2)}, u32[]{:S(2)}) collective-permute-start(f32[2,512]{1,0:T(2,128)S(1)} %bitcast.27), channel_id=1, source_target_pairs={{0,1},{1,0},{2,3},{3,2},{4,5},{5,4},{6,7},{7,6},{8,9},{9,8},{10,11... | collective-permute-start | bytes 12296 | tf_op jit(solution)/shard_map/ppermute | solution.py:743
  144.2 12.1 %collective-permute-start.25 = (bf16[112,512]{1,0:T(8,128)(2,1)S(1)}, bf16[112,512]{1,0:T(8,128)(2,1)S(1)}, u32[]{:S(2)}, u32[]{:S(2)}) collective-permute-start(bf16[112,512]{1,0:T(8,128)(2,1)S(1)} %get-tuple-element.222), channel_id=1, source_target_pairs={{0,8},{1,9},{2,10},{3,11},{4,12},{5,13},{6,14},{7,15},{8,0},{9,1},... | collective-permute-start | bytes 344072 | tf_op jit(solution)/shard_map/ppermute | solution.py:780
  144.6 12.6 %collective-permute-start.26 = (bf16[112,512]{1,0:T(8,128)(2,1)S(1)}, bf16[112,512]{1,0:T(8,128)(2,1)S(1)}, u32[]{:S(2)}, u32[]{:S(2)}) collective-permute-start(bf16[112,512]{1,0:T(8,128)(2,1)S(1)} %get-tuple-element.223), channel_id=1, source_target_pairs={{0,16},{1,17},{2,18},{3,19},{4,20},{5,21},{6,22},{7,23},{8,24},{9,... | collective-permute-start | bytes 344072 | tf_op jit(solution)/shard_map/ppermute | solution.py:780
  148.2 8.9 %collective-permute-start.27 = (bf16[112,512]{1,0:T(8,128)(2,1)S(1)}, bf16[112,512]{1,0:T(8,128)(2,1)S(1)}, u32[]{:S(2)}, u32[]{:S(2)}) collective-permute-start(bf16[112,512]{1,0:T(8,128)(2,1)S(1)} %get-tuple-element.224), channel_id=1, source_target_pairs={{0,24},{1,25},{2,26},{3,27},{4,28},{5,29},{6,30},{7,31},{8,16},{9,... | collective-permute-start | bytes 344072 | tf_op jit(solution)/shard_map/ppermute | solution.py:780
  158.3 7.9 %collective-permute-start.28 = (bf16[2,512,512]{2,1,0:T(8,128)(2,1)}, bf16[2,512,512]{2,1,0:T(8,128)(2,1)}, u32[]{:S(2)}, u32[]{:S(2)}) collective-permute-start(bf16[2,512,512]{2,1,0:T(8,128)(2,1)} %block_output.2), channel_id=1, source_target_pairs={{0,1},{1,0},{2,3},{3,2},{4,5},{5,4},{6,7},{7,6},{8,9},{9,8},{10,11... | collective-permute-start | bytes 3145736 | tf_op jit(solution)/shard_map/ppermute | solution.py:743
  158.3 5.3 %copy-start.21 = (bf16[4,512,512]{2,1,0:T(8,128)(2,1)S(1)}, bf16[4,512,512]{2,1,0:T(8,128)(2,1)}, u32[]{:S(2)}) copy-start(bf16[4,512,512]{2,1,0:T(8,128)(2,1)} %get-tuple-element.233) | copy-start | bytes 6291460
  158.8 7.5 %copy-start.4 = (bf16[512,1024]{1,0:T(8,128)(2,1)}, bf16[512,1024]{1,0:T(8,128)(2,1)S(1)}, u32[]{:S(2)}) copy-start(bf16[512,1024]{1,0:T(8,128)(2,1)S(1)} %maximum_select_fusion.refs_0_) | copy-start | bytes 3145732
  158.8 14.9 %collective-permute-start.30 = (bf16[512,1024]{1,0:T(8,128)(2,1)S(1)}, bf16[512,1024]{1,0:T(8,128)(2,1)S(1)}, u32[]{:S(2)}, u32[]{:S(2)}) collective-permute-start(bf16[512,1024]{1,0:T(8,128)(2,1)S(1)} %maximum_select_fusion.refs_0_), channel_id=1, source_target_pairs={{0,2},{1,5},{2,0},{3,7},{4,6},{5,1},{6,4},{7,3},{8,10},{9,13},{10,... | collective-permute-start | bytes 3145736 | tf_op jit(solution)/shard_map/ppermute | solution.py:780
  160.3 7.4 %collective-permute-start.31 = (bf16[96,512]{1,0:T(8,128)(2,1)S(1)}, bf16[96,512]{1,0:T(8,128)(2,1)S(1)}, u32[]{:S(2)}, u32[]{:S(2)}) collective-permute-start(bf16[96,512]{1,0:T(8,128)(2,1)S(1)} %add_convert_fusion.9), channel_id=1, source_target_pairs={{0,8},{1,9},{2,10},{3,11},{4,12},{5,13},{6,14},{7,15},{8,0},{9,1},... | collective-permute-start | bytes 294920 | tf_op jit(solution)/shard_map/ppermute | solution.py:780
  162.4 10.0 %collective-permute-start.32 = (bf16[96,512]{1,0:T(8,128)(2,1)S(1)}, bf16[96,512]{1,0:T(8,128)(2,1)S(1)}, u32[]{:S(2)}, u32[]{:S(2)}) collective-permute-start(bf16[96,512]{1,0:T(8,128)(2,1)S(1)} %add_convert_fusion.9), channel_id=1, source_target_pairs={{0,16},{1,17},{2,18},{3,19},{4,20},{5,21},{6,22},{7,23},{8,24},{9,... | collective-permute-start | bytes 294920 | tf_op jit(solution)/shard_map/ppermute | solution.py:780
  163.5 1.3 collective-permute-start.29
  163.8 3.9 %copy-start.22 = (bf16[4,512,512]{2,1,0:T(8,128)(2,1)}, bf16[4,512,512]{2,1,0:T(8,128)(2,1)S(1)}, u32[]{:S(2)}) copy-start(bf16[4,512,512]{2,1,0:T(8,128)(2,1)S(1)} %constant_dynamic-update-slice_fusion.1) | copy-start | bytes 6291460
  164.7 7.7 %collective-permute-start.33 = (bf16[96,512]{1,0:T(8,128)(2,1)S(1)}, bf16[96,512]{1,0:T(8,128)(2,1)S(1)}, u32[]{:S(2)}, u32[]{:S(2)}) collective-permute-start(bf16[96,512]{1,0:T(8,128)(2,1)S(1)} %add_convert_fusion.9), channel_id=1, source_target_pairs={{0,24},{1,25},{2,26},{3,27},{4,28},{5,29},{6,30},{7,31},{8,16},{9,... | collective-permute-start | bytes 294920 | tf_op jit(solution)/shard_map/ppermute | solution.py:780
  167.7 13.9 %copy-start = (bf16[4,512,512]{2,1,0:T(8,128)(2,1)}, bf16[4,512,512]{2,1,0:T(8,128)(2,1)S(1)}, u32[]{:S(2)}) copy-start(bf16[4,512,512]{2,1,0:T(8,128)(2,1)S(1)} %constant_dynamic-update-slice_fusion.refs_0_) | copy-start | bytes 6291460
  173.7 4.5 %copy-start.9 = (bf16[512,1024]{1,0:T(8,128)(2,1)}, bf16[512,1024]{1,0:T(8,128)(2,1)S(1)}, u32[]{:S(2)}) copy-start(bf16[512,1024]{1,0:T(8,128)(2,1)S(1)} %collective-permute-done.30.refs_1_) | copy-start | bytes 3145732
  174.0 14.7 %copy-start.5 = (bf16[400,512]{1,0:T(8,128)(2,1)}, bf16[400,512]{1,0:T(8,128)(2,1)S(1)}, u32[]{:S(2)}) copy-start(bf16[400,512]{1,0:T(8,128)(2,1)S(1)} %pad_maximum_fusion.refs_0_) | copy-start | bytes 1228804
  174.0 14.6 %collective-permute-start.34 = (bf16[400,512]{1,0:T(8,128)(2,1)S(1)}, bf16[400,512]{1,0:T(8,128)(2,1)S(1)}, u32[]{:S(2)}, u32[]{:S(2)}) collective-permute-start(bf16[400,512]{1,0:T(8,128)(2,1)S(1)} %pad_maximum_fusion.refs_0_), channel_id=1, source_target_pairs={{0,2},{1,3},{2,0},{3,1},{4,6},{5,7},{6,4},{7,5},{8,10},{9,11},{10,... | collective-permute-start | bytes 1228808 | tf_op jit(solution)/shard_map/ppermute | solution.py:780
  175.4 19.6 %collective-permute-start.35 = (bf16[400,512]{1,0:T(8,128)(2,1)S(1)}, bf16[400,512]{1,0:T(8,128)(2,1)}, u32[]{:S(2)}, u32[]{:S(2)}) collective-permute-start(bf16[400,512]{1,0:T(8,128)(2,1)S(1)} %pad_maximum_fusion.refs_0_), channel_id=1, source_target_pairs={{0,4},{1,5},{2,6},{3,7},{4,0},{5,1},{6,2},{7,3},{8,12},{9,13},{10,... | collective-permute-start | bytes 1228808 | tf_op jit(solution)/shard_map/ppermute | solution.py:780
  176.3 18.7 %collective-permute-start.36 = (bf16[400,512]{1,0:T(8,128)(2,1)S(1)}, bf16[400,512]{1,0:T(8,128)(2,1)}, u32[]{:S(2)}, u32[]{:S(2)}) collective-permute-start(bf16[400,512]{1,0:T(8,128)(2,1)S(1)} %pad_maximum_fusion.refs_0_), channel_id=1, source_target_pairs={{0,6},{1,7},{2,4},{3,5},{4,2},{5,3},{6,0},{7,1},{8,14},{9,15},{10,... | collective-permute-start | bytes 1228808 | tf_op jit(solution)/shard_map/ppermute | solution.py:780
  188.6 6.4 %copy-start.14 = (bf16[400,512]{1,0:T(8,128)(2,1)}, bf16[400,512]{1,0:T(8,128)(2,1)S(1)}, u32[]{:S(2)}) copy-start(bf16[400,512]{1,0:T(8,128)(2,1)S(1)} %collective-permute-done.34.refs_1_) | copy-start | bytes 1228804
  (2 other events, 1.3 us)

commit v4 on v3

--- a/solution.py
+++ b/solution.py
@@ -326,9 +326,17 @@
 
     rows = tangent.shape[0]
     part = math.gcd(rows, 256)
+
+    def lead(begin):
+        at = slice(begin, begin + part)
+        return mm_nt(back_own[at, :], up_own[...]) + mm_nt(back_other[at, :], up_other[...])
+
+    ahead = lead(0)
     for begin in range(0, rows, part):
         at = slice(begin, begin + part)
-        back = mm_nt(back_own[at, :], up_own[...]) + mm_nt(back_other[at, :], up_other[...])
+        back = ahead
+        if begin + part < rows:
+            ahead = lead(begin + part)
         middle = middle_in[at, :]
         scale = lax.rsqrt(jnp.mean(middle * middle, axis=-1, keepdims=True) + epsilon)
         gain_out[...] += jnp.sum(back * (middle * scale), axis=0, keepdims=True)
@@ -703,36 +711,47 @@
     cut = 3 * width // len(shares)
     total = jnp.concatenate(in_order(place, [share[:cut, :].astype(wide) for share in shares]))
     short = sum_alike([share[cut:, :] for share in shares])
+    lanes = short.shape[1]
     row = 0
-    for out in (gain_out, taps_out, gain_two_out, gate_out, up_out):
-        for lane in range(0, out.shape[1], width):
-            some = min(width, out.shape[1])
-            out[:, lane : lane + some] = short[row : row + out.shape[0], :some]
-            row += out.shape[0]
+    for out in (gain_out, taps_out, gain_two_out, gate_out):
+        out[...] = short[row : row + out.shape[0], :]
+        row += out.shape[0]
+    for lane in range(0, up_out.shape[1], width):
+        at = pl.multiple_of(lane + pl.program_id(0) * lanes, lanes)
+        up_out[:, pl.ds(at, lanes)] = short[row : row + 1, :]
+        row += 1
     mixer_out[:, 0, :] = total[:width]
     mixer_out[:, 1, :] = total[width : 2 * width]
     read_out[...] = total[2 * width :].T
 
 
 def finish_mixer(place, shares, width, taps, units):
-    channels = shares[0].shape[1]
-    short = [(1, width), (taps, width), (1, width), (1, channels), (1, units)]
+    rows, channels = shares[0].shape
+    block = min(channels, 256)
+    lanes = lambda count: pl.BlockSpec((count, block), lambda j, place: (0, j))
     return pl.pallas_call(
         finish_mixer_kernel,
         grid_spec=pltpu.PrefetchScalarGridSpec(
             num_scalar_prefetch=1,
-            grid=(1,),
-            in_specs=[whole(share) for share in shares],
+            grid=(channels // block,),
+            in_specs=[lanes(rows) for _ in shares],
             out_specs=[
-                pl.BlockSpec((width, 2, channels), lambda j, place: (0, 0, 0)),
-                pl.BlockSpec((channels, width), lambda j, place: (0, 0)),
-                *[pl.BlockSpec(shape, lambda j, place: (0, 0)) for shape in short],
+                pl.BlockSpec((width, 2, block), lambda j, place: (0, 0, j)),
+                pl.BlockSpec((block, width), lambda j, place: (j, 0)),
+                lanes(1),
+                lanes(taps),
+                lanes(1),
+                lanes(1),
+                pl.BlockSpec((1, units), lambda j, place: (0, 0)),
             ],
         ),
         out_shape=[
             jax.ShapeDtypeStruct((width, 2, channels), wide),
             jax.ShapeDtypeStruct((channels, width), wide),
-            *[jax.ShapeDtypeStruct(shape, wide) for shape in short],
+            *[
+                jax.ShapeDtypeStruct(shape, wide)
+                for shape in ((1, width), (taps, width), (1, width), (1, channels), (1, units))
+            ],
         ],
         compiler_params=params(60, 1),
         name="finish_mixer",

time: 200 us -> 200 us (level)
  no operation moved by 1% of the time
where the time goes in v4:
time: 200 us; the launch traced here: 199 us
  Pallas kernels  125 us (62%)
  starting transfers between devices  36 us (18%)
  waiting for transfers between devices  18.1 us (9%)
  other arithmetic  11.5 us (6%)
  local copies, waits for them, and re-layouts  7.55 us (4%)
    ppermute x22, starting transfers between devices, exchange(): return lax.ppermute(array, ('dp', 'tensor'), route)  32.7 us
    pallas_call x2, Pallas kernels, feed(): pl.pallas_call(kernel, grid_spec=pltpu.PrefetchScalarGridSpec(num_scalar_...  32.6 us
    pallas_call x2, Pallas kernels, scan_back(): pl.pallas_call(functools.partial(scan_kernel, windows, chunk), grid=(coun...  24.3 us
    pallas_call x1, Pallas kernels, forward(): pl.pallas_call(forward_kernel, grid_spec=pltpu.PrefetchScalarGridSpec(num...  19.6 us
    ppermute x22, waiting for transfers between devices, exchange(): return lax.ppermute(array, ('dp', 'tensor'), route)  15.7 us
    pallas_call x1, Pallas kernels, entry(): pl.pallas_call(entry_kernel, grid_spec=pltpu.PrefetchScalarGridSpec(num_s...  15 us
    pallas_call x2, Pallas kernels, leave(): pl.pallas_call(leave_kernel, grid_spec=pltpu.PrefetchScalarGridSpec(num_s...  14 us
    pallas_call x1, Pallas kernels, norm_back(): pl.pallas_call(norm_kernel, grid=(rows // chunk,), in_specs=[row(width),...  11.7 us
  transfers between devices with their start and end apart: 37, of which 9 were waited for; matrix products, arithmetic and copies ran while one was open for 2% of the time, Pallas kernels for 52%

profile of v4, /device:TPU:0, one launch (start us, length us, event | category | flops | bytes accessed | tf_op | source)
XLA Modules:
  0.0 199.3 jit_solution(9817803113583873304)
XLA Ops:
  0.7 1.4 constant_dynamic-slice_fusion.1
  2.2 0.5 collective-permute-start
  2.7 0.2 copy.27
  3.1 0.5 collective-permute-start.4
  3.6 0.4 collective-permute-start.2
  4.0 1.0 constant_dynamic-slice_fusion
  5.1 2.1 %collective-permute-done.2 = f32[512]{0:T(512)S(1)} collective-permute-done((f32[512]{0:T(512)S(1)}, f32[512]{0:T(512)S(1)}, u32[]{:S(2)}, u32[]{:S(2)}) %collective-permute-start.2) | collective-permute-done | bytes 2080 | tf_op jit(solution)/shard_map/ppermute | solution.py:762
  7.2 0.4 collective-permute-start.5
  7.8 0.4 collective-permute-start.6
  8.5 0.8 copy-done.7
  9.2 1.0 copy-done.8
  10.3 19.6 %forward_mixer.1 = (bf16[2048,512]{1,0:T(8,128)(2,1)}, f32[2048,1024]{1,0:T(8,128)}, bf16[2048,1024]{1,0:T(8,128)(2,1)}, bf16[2048,1024]{1,0:T(8,128)(2,1)}, bf1...) custom-call(s32[1]{0:T(128)} %bitcast.core, ...), custom_call_target="tpu_custom_call" | custom-call | flops 6442450944 | bytes 25165824 | tf_op jit(solution)/shard_map/forward_mixer/pallas_call | solution.py:182
  30.0 0.5 copy-done.26
  30.5 0.4 copy-done.2
  30.9 17.5 %feed_forward.2 = (bf16[2048,1024]{1,0:T(8,128)(2,1)}, bf16[2048,1024]{1,0:T(8,128)(2,1)}, f32[8,1024]{1,0:T(8,128)}, bf16[1024,1024]{1,0:T(8,128)(2,1)}, bf16[2048,512]{1,0:T(8,128)(2,1)}) custom-call(s32[1]{0:T(128)} %bitcast.core, bf16[4,512,512]{2,1,0:T(8,128)(2,1)} %refs_0_.1, bf16[2,512,512]{2,1,0:T(8,128)(2,1)} %collective-permute-done.5.refs_1_, ...), custom_call_target="tpu_custom_call" | custom-call | flops 8589934592 | bytes 8388608 | tf_op jit(solution)/shard_map/feed_forward/pallas_call | solution.py:308
  48.6 15.1 %feed_forward.3 = (bf16[2048,1024]{1,0:T(8,128)(2,1)}, bf16[2048,1024]{1,0:T(8,128)(2,1)}, f32[8,1024]{1,0:T(8,128)}, f32[1024,1024]{1,0:T(8,128)}) custom-call(s32[1]{0:T(128)} %bitcast.core, bf16[2048,512]{1,0:T(8,128)(2,1)} %get-tuple-element.143.refs_0_.tangent, bf16[2048,512]{1,0:T(8,128)(2,1)} %get-tuple-element.140.refs_3_.refs_1_, ...), custom_call_target="tpu_custom_call" | custom-call | flops 8589934592 | bytes 8388608 | tf_op jit(solution)/shard_map/feed_forward/pallas_call | solution.py:308
  63.7 1.9 add_convert_fusion
  65.7 2.8 %collective-permute-start.10 = (bf16[512,1024]{1,0:T(8,128)(2,1)S(1)}, bf16[512,1024]{1,0:T(8,128)(2,1)}, u32[]{:S(2)}, u32[]{:S(2)}) collective-permute-start(bf16[512,1024]{1,0:T(8,128)(2,1)S(1)} %add_convert_fusion), channel_id=1, source_target_pairs={{0,2},{1,5},{2,0},{3,7},{4,6},{5,1},{6,4},{7,3},{8,10},{9,13},{10,... | collective-permute-start | bytes 3145736 | tf_op jit(solution)/shard_map/ppermute | solution.py:799
  68.5 11.7 %norm_back.1 = (f32[2048,512]{1,0:T(8,128)}, bf16[2048,512]{1,0:T(8,128)(2,1)}, f32[1,512]{1,0:T(1,128)}) custom-call(bf16[2048,512]{1,0:T(8,128)(2,1)} %get-tuple-element.143.refs_0_.tangent, bf16[2048,1024]{1,0:T(8,128)(2,1)} %get-tuple-element.149.back_own, bf16[2048,1024]{1,0:T(8,128)(2,1)} %get-tuple-element.150.back_other, ...), custom_call_target="tpu_custom_call" | custom-call | flops 4294967296 | bytes 25165824 | tf_op jit(solution)/shard_map/norm_back/pallas_call | solution.py:357
  80.2 1.2 collective-permute-done.10
  81.4 2.5 %convert_add_fusion = (f32[256,1024]{1,0:T(8,128)S(1)}, bf16[256,1024]{1,0:T(8,128)(2,1)S(1)}) fusion(f32[1024,1024]{1,0:T(8,128)} %get-tuple-element.147, s32[]{:T(128)S(6)} %dynamic_slice.144, bf16[512,1024]{1,0:T(8,128)(2,1)} %collective-permute-done.10, s32[]{:T(128)S(6)} %select_n.173, bf16[1024,1024]{1,0:T(8,128)(2,1)S(1)} %collective-permute-done.9, ...), kind=kLoop, calls=%fused_computation.2 | loop fusion | flops 2359296 | bytes 5767184 | tf_op jit(solution)/shard_map/add | solution.py:818
  83.8 2.1 %collective-permute-start.11 = (bf16[256,1024]{1,0:T(8,128)(2,1)S(1)}, bf16[256,1024]{1,0:T(8,128)(2,1)S(1)}, u32[]{:S(2)}, u32[]{:S(2)}) collective-permute-start(bf16[256,1024]{1,0:T(8,128)(2,1)S(1)} %get-tuple-element.169), channel_id=1, source_target_pairs={{0,4},{1,3},{2,6},{3,1},{4,0},{5,7},{6,2},{7,5},{8,12},{9,11},{10,... | collective-permute-start | bytes 1572872 | tf_op jit(solution)/shard_map/ppermute | solution.py:799
  86.0 11.9 %scan_back.2 = (bf16[2048,512]{1,0:T(8,128)(2,1)}, bf16[2048,512]{1,0:T(8,128)(2,1)}, f32[2,1,512]{2,1,0:T(1,128)}, f32[8,512]{1,0:T(8,128)}, bf16[1536,512]{1,0:T(8,128)(2,1)}) custom-call(bf16[2048,512]{1,0:T(8,128)(2,1)} %get-tuple-element.173.mixed, bf16[2048,512]{1,0:T(8,128)(2,1)} %get-tuple-element.159.filtered, bf16[512,512]{1,0:T(8,128)(2,1)} %copy-done.12, ...), custom_call_target="tpu_custom_call" | custom-call | flops 4294967296 | bytes 14680064 | tf_op jit(solution)/shard_map/scan_back/pallas_call | solution.py:447
  98.1 1.6 collective-permute-start.12
  99.7 2.6 %collective-permute-start.13 = (bf16[64,1024]{1,0:T(8,128)(2,1)S(1)}, bf16[64,1024]{1,0:T(8,128)(2,1)S(1)}, u32[]{:S(2)}, u32[]{:S(2)}) collective-permute-start(bf16[64,1024]{1,0:T(8,128)(2,1)S(1)} %get-tuple-element.180), channel_id=1, source_target_pairs={{0,16},{1,17},{2,18},{3,19},{4,20},{5,21},{6,22},{7,23},{8,24},{9,... | collective-permute-start | bytes 393224 | tf_op jit(solution)/shard_map/ppermute | solution.py:799
  102.3 0.2 collective-permute-start.14
  102.5 12.4 %scan_back.3 = (bf16[2048,512]{1,0:T(8,128)(2,1)}, bf16[2048,512]{1,0:T(8,128)(2,1)}, f32[2,1,512]{2,1,0:T(1,128)}, f32[8,512]{1,0:T(8,128)}, f32[1536,512]{1,0:T(8,128)}) custom-call(bf16[2048,512]{1,0:T(8,128)(2,1)} %get-tuple-element.173.mixed, bf16[2048,512]{1,0:T(8,128)(2,1)} %get-tuple-element.159.filtered, bf16[512,512]{1,0:T(8,128)(2,1)} %read.1, ...), custom_call_target="tpu_custom_call" | custom-call | flops 4294967296 | bytes 14680064 | tf_op jit(solution)/shard_map/scan_back/pallas_call | solution.py:447
  115.1 3.3 %convert_add_fusion.1 = (f32[384,512]{1,0:T(8,128)S(1)}, bf16[384,512]{1,0:T(8,128)(2,1)S(1)}, bf16[384,512]{1,0:T(8,128)(2,1)}, bf16[384,512]{1,0:T(8,128)(2,1)}) fusion(f32[1536,512]{1,0:T(8,128)} %get-tuple-element.184, s32[]{:T(128)S(6)} %select_n.178, bf16[1536,512]{1,0:T(8,128)(2,1)S(1)} %collective-permute-done.15, s32[]{:T(128)S(6)} %select_n.183, ...), kind=kLoop, calls=%fused_computation.7 | loop fusion | flops 2162688 | bytes 6684688 | tf_op jit(solution)/shard_map/add | solution.py:818
  118.4 0.6 collective-permute-start.16
  119.0 3.4 %collective-permute-start.17 = (bf16[64,1024]{1,0:T(8,128)(2,1)S(1)}, bf16[64,1024]{1,0:T(8,128)(2,1)S(1)}, u32[]{:S(2)}, u32[]{:S(2)}) collective-permute-start(bf16[64,1024]{1,0:T(8,128)(2,1)S(1)} %add_convert_fusion.5), channel_id=1, source_target_pairs={{0,16},{1,17},{2,18},{3,19},{4,20},{5,21},{6,22},{7,23},{8,24},{9,... | collective-permute-start | bytes 393224 | tf_op jit(solution)/shard_map/ppermute | solution.py:799
  122.4 0.4 collective-permute-start.18
  122.8 1.5 collective-permute-start.19
  124.2 0.5 collective-permute-start.20
  124.8 0.5 collective-permute-done.16
  125.2 1.4 collective-permute-start.21
  126.6 15.0 %input_gradient.1 = (bf16[4,512,512]{2,1,0:T(8,128)(2,1)}, bf16[2,512,512]{2,1,0:T(8,128)(2,1)}, bf16[16,512]{1,0:T(8,128)(2,1)}) custom-call(s32[1]{0:T(128)} %bitcast.core, bf16[4,512,512]{2,1,0:T(8,128)(2,1)} %own.3, bf16[2,512,512]{2,1,0:T(8,128)(2,1)} %copy-done.7, bf16[512,512]{1,0:T(8,128)(2,1)} %get-tuple-element.139.refs_2_.order, ...), custom_call_target="tpu_custom_call" | custom-call | flops 4294967296 | bytes 12582912 | tf_op jit(solution)/shard_map/input_gradient/pallas_call | solution.py:586
  141.6 0.9 collective-permute-done.20
  143.0 0.2 copy-done.16
  143.4 0.8 collective-permute-start.24
  144.2 0.4 collective-permute-start.25
  144.6 3.7 %collective-permute-start.26 = (bf16[112,512]{1,0:T(8,128)(2,1)S(1)}, bf16[112,512]{1,0:T(8,128)(2,1)S(1)}, u32[]{:S(2)}, u32[]{:S(2)}) collective-permute-start(bf16[112,512]{1,0:T(8,128)(2,1)S(1)} %get-tuple-element.223), channel_id=1, source_target_pairs={{0,16},{1,17},{2,18},{3,19},{4,20},{5,21},{6,22},{7,23},{8,24},{9,... | collective-permute-start | bytes 344072 | tf_op jit(solution)/shard_map/ppermute | solution.py:799
  148.2 1.1 collective-permute-start.27
  149.4 7.0 %block_output.2 = bf16[2,512,512]{2,1,0:T(8,128)(2,1)} custom-call(s32[1]{0:T(128)} %bitcast.core, bf16[512,512]{1,0:T(8,128)(2,1)} %get-tuple-element.138.back_order, bf16[2048,1024]{1,0:T(8,128)(2,1)} %get-tuple-element.246.active_own, bf16[2048,1024]{1,0:T(8,128)(2,1)} %get-tuple-element.218.active_other, ...), custom_call_target="tpu_custom_call" | custom-call | flops 2147483648 | bytes 6291456 | tf_op jit(solution)/shard_map/block_output/pallas_call | solution.py:641
  156.3 0.8 collective-permute-done.26
  157.2 1.1 add_convert_fusion.9
  158.3 0.5 maximum_select_fusion.refs_0_
  158.8 1.4 collective-permute-start.30
  160.3 2.1 %collective-permute-start.31 = (bf16[96,512]{1,0:T(8,128)(2,1)S(1)}, bf16[96,512]{1,0:T(8,128)(2,1)S(1)}, u32[]{:S(2)}, u32[]{:S(2)}) collective-permute-start(bf16[96,512]{1,0:T(8,128)(2,1)S(1)} %add_convert_fusion.9), channel_id=1, source_target_pairs={{0,8},{1,9},{2,10},{3,11},{4,12},{5,13},{6,14},{7,15},{8,0},{9,1},... | collective-permute-start | bytes 294920 | tf_op jit(solution)/shard_map/ppermute | solution.py:799
  162.4 1.0 collective-permute-start.32
  163.5 0.2 collective-permute-start.29
  163.8 0.7 maximum_select_fusion.7
  164.5 0.3 collective-permute-done.29
  164.7 1.4 collective-permute-start.33
  166.3 1.3 constant_dynamic-update-slice_fusion.refs_0_
  167.7 4.7 %collective-permute-done.32 = bf16[96,512]{1,0:T(8,128)(2,1)S(1)} collective-permute-done((bf16[96,512]{1,0:T(8,128)(2,1)S(1)}, bf16[96,512]{1,0:T(8,128)(2,1)S(1)}, u32[]{:S(2)}, u32[]{:S(2)}) %collective-permute-start.32) | collective-permute-done | bytes 98336 | tf_op jit(solution)/shard_map/ppermute | solution.py:799
  172.4 1.3 collective-permute-done.30.refs_1_
  174.0 1.4 collective-permute-start.34
  175.4 0.9 collective-permute-start.35
  176.3 1.3 collective-permute-start.36
  177.5 0.7 pad_add_fusion.place
  178.2 3.4 %finish_feed.1 = (f32[1024,512]{1,0:T(8,128)}, f32[512,1024]{1,0:T(8,128)}) custom-call(s32[1]{0:T(128)} %bitcast.9.place, bf16[512,1024]{1,0:T(8,128)(2,1)} %copy-done.4, bf16[512,1024]{1,0:T(8,128)(2,1)} %copy-done.9), custom_call_target="tpu_custom_call" | custom-call | tf_op jit(solution)/shard_map/finish_feed/pallas_call | solution.py:688
  181.6 7.0 %block_output.3 = bf16[4,512,512]{2,1,0:T(8,128)(2,1)} custom-call(s32[1]{0:T(128)} %bitcast.core, bf16[512,512]{1,0:T(8,128)(2,1)} %get-tuple-element.138.back_order, bf16[2048,1024]{1,0:T(8,128)(2,1)} %get-tuple-element.246.active_own, bf16[2048,1024]{1,0:T(8,128)(2,1)} %get-tuple-element.218.active_other, ...), custom_call_target="tpu_custom_call", output_to_operand_aliasing={{}: (7, {})} | custom-call | flops 2147483648 | bytes 6291456 | tf_op jit(solution)/shard_map/block_output/pallas_call | solution.py:641
  188.6 6.3 %collective-permute-done.35.refs_2_ = bf16[400,512]{1,0:T(8,128)(2,1)} collective-permute-done((bf16[400,512]{1,0:T(8,128)(2,1)S(1)}, bf16[400,512]{1,0:T(8,128)(2,1)}, u32[]{:S(2)}, u32[]{:S(2)}) %collective-permute-start.35) | collective-permute-done | bytes 409632 | tf_op jit(solution)/shard_map/ppermute | solution.py:799
  195.0 4.1 %finish_mixer.1 = (f32[512,2,512]{2,1,0:T(2,128)}, f32[512,512]{1,0:T(8,128)}, f32[1,512]{1,0:T(1,128)}, f32[4,512]{1,0:T(4,128)}, f32[1,512]{1,0:T(1,128)}, /*index=5*/f32[1,512]{1,0:T(1,128)}, f32[1,1024]{1,0:T(1,128)}) custom-call(s32[2]{0:T(128)} %pad_add_fusion.place, bf16[400,512]{1,0:T(8,128)(2,1)} %copy-done.5, bf16[400,512]{1,0:T(8,128)(2,1)} %copy-done.14, ...), custom_call_target="tpu_custom_call" | custom-call | tf_op jit(solution)/shard_map/finish_mixer/pallas_call | solution.py:732
  (110 shorter events, 2.4 us)
Async XLA Ops:
  0.6 2.0 %copy-start.10 = (bf16[512,2,512]{2,1,0:T(2,128)(2,1)S(1)}, bf16[512,2,512]{2,1,0:T(2,128)(2,1)}, u32[]{:S(2)}) copy-start(bf16[512,2,512]{2,1,0:T(2,128)(2,1)} %param.16) | copy-start | bytes 3145732
  0.7 2.4 %copy-start.11 = (bf16[512,512]{1,0:T(8,128)(2,1)S(1)}, bf16[512,512]{1,0:T(8,128)(2,1)}, u32[]{:S(2)}) copy-start(bf16[512,512]{1,0:T(8,128)(2,1)} %read.1) | copy-start | bytes 1572868
  0.7 2.9 %copy-start.23 = (f32[4,512]{1,0:T(4,128)S(1)}, f32[4,512]{1,0:T(4,128)}, u32[]{:S(2)}) copy-start(f32[4,512]{1,0:T(4,128)} %start_own.1) | copy-start | bytes 24580
  0.7 2.9 %copy-start.27 = (f32[512]{0:T(512)S(1)}, f32[512]{0:T(512)}, u32[]{:S(2)}) copy-start(f32[512]{0:T(512)} %param.17) | copy-start | bytes 6148
  0.7 3.4 %copy-start.13 = (bf16[4,512,512]{2,1,0:T(8,128)(2,1)S(1)}, bf16[4,512,512]{2,1,0:T(8,128)(2,1)}, u32[]{:S(2)}) copy-start(bf16[4,512,512]{2,1,0:T(8,128)(2,1)} %refs_0_.1) | copy-start | bytes 6291460
  2.2 6.1 %collective-permute-start = (bf16[2,512,512]{2,1,0:T(8,128)(2,1)S(1)}, bf16[2,512,512]{2,1,0:T(8,128)(2,1)S(1)}, u32[]{:S(2)}, u32[]{:S(2)}) collective-permute-start(bf16[2,512,512]{2,1,0:T(8,128)(2,1)S(1)} %constant_dynamic-slice_fusion.1), channel_id=1, source_target_pairs={{0,1},{1,0},{2,3},{3,2},{4,5},{5,4},{6,7},{7,6},{8,9},{9,8},{10,11... | collective-permute-start | bytes 3145736 | tf_op jit(solution)/shard_map/ppermute | solution.py:762
  2.7 4.9 %copy-start.1 = (bf16[1024,512]{1,0:T(8,128)(2,1)S(1)}, bf16[1024,512]{1,0:T(8,128)(2,1)}, u32[]{:S(2)}) copy-start(bf16[1024,512]{1,0:T(8,128)(2,1)} %down_own.3) | copy-start | bytes 3145732
  2.7 5.1 %copy-start.6 = (bf16[512,1024]{1,0:T(8,128)(2,1)S(1)}, bf16[512,1024]{1,0:T(8,128)(2,1)}, u32[]{:S(2)}) copy-start(bf16[512,1024]{1,0:T(8,128)(2,1)} %up_own.1) | copy-start | bytes 3145732
  2.7 5.6 %copy-start.25 = (f32[1024]{0:T(1024)S(1)}, f32[1024]{0:T(1024)}, u32[]{:S(2)}) copy-start(f32[1024]{0:T(1024)} %param.21) | copy-start | bytes 12292
  2.9 4.9 %copy-start.3 = (bf16[64,8,2,512]{3,1,2,0:T(8,128)(2,1)}, bf16[64,8,2,512]{3,1,2,0:T(8,128)(2,1)S(1)}, u32[]{:S(2)}) copy-start(bf16[64,8,2,512]{3,1,2,0:T(8,128)(2,1)S(1)} %copy.27) | copy-start | bytes 3145732
  2.9 5.5 %collective-permute-start.1 = (bf16[512,1024]{1,0:T(8,128)(2,1)S(1)}, bf16[512,1024]{1,0:T(8,128)(2,1)S(1)}, u32[]{:S(2)}, u32[]{:S(2)}) collective-permute-start(bf16[512,1024]{1,0:T(8,128)(2,1)S(1)} %bitcast.22), channel_id=1, source_target_pairs={{0,1},{1,0},{2,3},{3,2},{4,5},{5,4},{6,7},{7,6},{8,9},{9,8},{10,11... | collective-permute-start | bytes 3145736 | tf_op jit(solution)/shard_map/ppermute | solution.py:762
  3.1 4.7 %collective-permute-start.4 = (bf16[512,512]{1,0:T(8,128)(2,1)S(1)}, bf16[512,512]{1,0:T(8,128)(2,1)S(1)}, u32[]{:S(2)}, u32[]{:S(2)}) collective-permute-start(bf16[512,512]{1,0:T(8,128)(2,1)S(1)} %copy-done.11), channel_id=1, source_target_pairs={{0,1},{1,0},{2,3},{3,2},{4,5},{5,4},{6,7},{7,6},{8,9},{9,8},{10,11... | collective-permute-start | bytes 1572872 | tf_op jit(solution)/shard_map/ppermute | solution.py:762
  3.5 4.1 %collective-permute-start.3 = (f32[4,512]{1,0:T(4,128)S(1)}, f32[4,512]{1,0:T(4,128)S(1)}, u32[]{:S(2)}, u32[]{:S(2)}) collective-permute-start(f32[4,512]{1,0:T(4,128)S(1)} %copy-done.23), channel_id=1, source_target_pairs={{0,1},{1,0},{2,3},{3,2},{4,5},{5,4},{6,7},{7,6},{8,9},{9,8},{10,11... | collective-permute-start | bytes 24584 | tf_op jit(solution)/shard_map/ppermute | solution.py:762
  3.6 3.6 %collective-permute-start.2 = (f32[512]{0:T(512)S(1)}, f32[512]{0:T(512)S(1)}, u32[]{:S(2)}, u32[]{:S(2)}) collective-permute-start(f32[512]{0:T(512)S(1)} %copy-done.27), channel_id=1, source_target_pairs={{0,1},{1,0},{2,3},{3,2},{4,5},{5,4},{6,7},{7,6},{8,9},{9,8},{10,11... | collective-permute-start | bytes 6152 | tf_op jit(solution)/shard_map/ppermute | solution.py:762
  7.2 3.0 %copy-start.28 = (f32[512]{0:T(512)}, f32[512]{0:T(512)S(1)}, u32[]{:S(2)}) copy-start(f32[512]{0:T(512)S(1)} %collective-permute-done.2) | copy-start | bytes 6148
  7.2 22.7 %collective-permute-start.5 = (bf16[2,512,512]{2,1,0:T(8,128)(2,1)}, bf16[2,512,512]{2,1,0:T(8,128)(2,1)}, u32[]{:S(2)}, u32[]{:S(2)}) collective-permute-start(bf16[2,512,512]{2,1,0:T(8,128)(2,1)} %constant_dynamic-slice_fusion), channel_id=1, source_target_pairs={{0,1},{1,0},{2,3},{3,2},{4,5},{5,4},{6,7},{7,6},{8,9},{9,8},{10,11... | collective-permute-start | bytes 3145736 | tf_op jit(solution)/shard_map/ppermute | solution.py:762
  7.6 2.7 %copy-start.24 = (f32[4,512]{1,0:T(4,128)}, f32[4,512]{1,0:T(4,128)S(1)}, u32[]{:S(2)}) copy-start(f32[4,512]{1,0:T(4,128)S(1)} %collective-permute-done.3.start_other) | copy-start | bytes 24580
  7.6 22.3 %collective-permute-start.8 = (bf16[1024,512]{1,0:T(8,128)(2,1)S(1)}, bf16[1024,512]{1,0:T(8,128)(2,1)S(1)}, u32[]{:S(2)}, u32[]{:S(2)}) collective-permute-start(bf16[1024,512]{1,0:T(8,128)(2,1)S(1)} %copy-done.1), channel_id=1, source_target_pairs={{0,1},{1,0},{2,3},{3,2},{4,5},{5,4},{6,7},{7,6},{8,9},{9,8},{10,11... | collective-permute-start | bytes 3145736 | tf_op jit(solution)/shard_map/ppermute | solution.py:762
  7.8 2.4 %copy-start.12 = (bf16[512,512]{1,0:T(8,128)(2,1)}, bf16[512,512]{1,0:T(8,128)(2,1)S(1)}, u32[]{:S(2)}) copy-start(bf16[512,512]{1,0:T(8,128)(2,1)S(1)} %collective-permute-done.4.read_other.read) | copy-start | bytes 1572868
  7.8 22.1 %collective-permute-start.6 = (bf16[512,1024]{1,0:T(8,128)(2,1)S(1)}, bf16[512,1024]{1,0:T(8,128)(2,1)}, u32[]{:S(2)}, u32[]{:S(2)}) collective-permute-start(bf16[512,1024]{1,0:T(8,128)(2,1)S(1)} %copy-done.6), channel_id=1, source_target_pairs={{0,1},{1,0},{2,3},{3,2},{4,5},{5,4},{6,7},{7,6},{8,9},{9,8},{10,11... | collective-permute-start | bytes 3145736 | tf_op jit(solution)/shard_map/ppermute | solution.py:762
  8.3 1.0 copy-start.7
  8.3 21.6 %collective-permute-start.7 = (f32[1024]{0:T(1024)S(1)}, f32[1024]{0:T(1024)S(1)}, u32[]{:S(2)}, u32[]{:S(2)}) collective-permute-start(f32[1024]{0:T(1024)S(1)} %copy-done.25), channel_id=1, source_target_pairs={{0,1},{1,0},{2,3},{3,2},{4,5},{5,4},{6,7},{7,6},{8,9},{9,8},{10,11... | collective-permute-start | bytes 12296 | tf_op jit(solution)/shard_map/ppermute | solution.py:762
  9.2 1.0 copy-start.8
  29.9 1.0 copy-start.2
  48.5 15.2 %collective-permute-start.9 = (bf16[1024,1024]{1,0:T(8,128)(2,1)}, bf16[1024,1024]{1,0:T(8,128)(2,1)S(1)}, u32[]{:S(2)}, u32[]{:S(2)}) collective-permute-start(bf16[1024,1024]{1,0:T(8,128)(2,1)} %get-tuple-element.146), channel_id=1, source_target_pairs={{0,1},{1,0},{2,3},{3,2},{4,5},{5,4},{6,7},{7,6},{8,9},{9,8},{10,11... | collective-permute-start | bytes 6291464 | tf_op jit(solution)/shard_map/ppermute | solution.py:762
  65.7 15.7 %collective-permute-start.10 = (bf16[512,1024]{1,0:T(8,128)(2,1)S(1)}, bf16[512,1024]{1,0:T(8,128)(2,1)}, u32[]{:S(2)}, u32[]{:S(2)}) collective-permute-start(bf16[512,1024]{1,0:T(8,128)(2,1)S(1)} %add_convert_fusion), channel_id=1, source_target_pairs={{0,2},{1,5},{2,0},{3,7},{4,6},{5,1},{6,4},{7,3},{8,10},{9,13},{10,... | collective-permute-start | bytes 3145736 | tf_op jit(solution)/shard_map/ppermute | solution.py:799
  83.8 14.0 %collective-permute-start.11 = (bf16[256,1024]{1,0:T(8,128)(2,1)S(1)}, bf16[256,1024]{1,0:T(8,128)(2,1)S(1)}, u32[]{:S(2)}, u32[]{:S(2)}) collective-permute-start(bf16[256,1024]{1,0:T(8,128)(2,1)S(1)} %get-tuple-element.169), channel_id=1, source_target_pairs={{0,4},{1,3},{2,6},{3,1},{4,0},{5,7},{6,2},{7,5},{8,12},{9,11},{10,... | collective-permute-start | bytes 1572872 | tf_op jit(solution)/shard_map/ppermute | solution.py:799
  97.8 17.3 %collective-permute-start.15 = (bf16[1536,512]{1,0:T(8,128)(2,1)}, bf16[1536,512]{1,0:T(8,128)(2,1)S(1)}, u32[]{:S(2)}, u32[]{:S(2)}) collective-permute-start(bf16[1536,512]{1,0:T(8,128)(2,1)} %get-tuple-element.183), channel_id=1, source_target_pairs={{0,1},{1,0},{2,3},{3,2},{4,5},{5,4},{6,7},{7,6},{8,9},{9,8},{10,11... | collective-permute-start | bytes 4718600 | tf_op jit(solution)/shard_map/ppermute | solution.py:762
  98.1 16.9 %collective-permute-start.12 = (bf16[64,1024]{1,0:T(8,128)(2,1)S(1)}, bf16[64,1024]{1,0:T(8,128)(2,1)S(1)}, u32[]{:S(2)}, u32[]{:S(2)}) collective-permute-start(bf16[64,1024]{1,0:T(8,128)(2,1)S(1)} %get-tuple-element.179), channel_id=1, source_target_pairs={{0,8},{1,9},{2,10},{3,11},{4,12},{5,13},{6,14},{7,15},{8,0},{9,1},... | collective-permute-start | bytes 393224 | tf_op jit(solution)/shard_map/ppermute | solution.py:799
  99.7 15.2 %collective-permute-start.13 = (bf16[64,1024]{1,0:T(8,128)(2,1)S(1)}, bf16[64,1024]{1,0:T(8,128)(2,1)S(1)}, u32[]{:S(2)}, u32[]{:S(2)}) collective-permute-start(bf16[64,1024]{1,0:T(8,128)(2,1)S(1)} %get-tuple-element.180), channel_id=1, source_target_pairs={{0,16},{1,17},{2,18},{3,19},{4,20},{5,21},{6,22},{7,23},{8,24},{9,... | collective-permute-start | bytes 393224 | tf_op jit(solution)/shard_map/ppermute | solution.py:799
  102.3 12.7 %collective-permute-start.14 = (bf16[64,1024]{1,0:T(8,128)(2,1)S(1)}, bf16[64,1024]{1,0:T(8,128)(2,1)S(1)}, u32[]{:S(2)}, u32[]{:S(2)}) collective-permute-start(bf16[64,1024]{1,0:T(8,128)(2,1)S(1)} %get-tuple-element.181), channel_id=1, source_target_pairs={{0,24},{1,25},{2,26},{3,27},{4,28},{5,29},{6,30},{7,31},{8,16},{9,... | collective-permute-start | bytes 393224 | tf_op jit(solution)/shard_map/ppermute | solution.py:799
  115.1 3.9 %copy-start.19 = (f32[2,1,512]{2,1,0:T(1,128)S(1)}, f32[2,1,512]{2,1,0:T(1,128)}, u32[]{:S(2)}) copy-start(f32[2,1,512]{2,1,0:T(1,128)} %get-tuple-element.211) | copy-start | bytes 12292
  118.4 6.8 %collective-permute-start.16 = (bf16[64,1024]{1,0:T(8,128)(2,1)S(1)}, bf16[64,1024]{1,0:T(8,128)(2,1)S(1)}, u32[]{:S(2)}, u32[]{:S(2)}) collective-permute-start(bf16[64,1024]{1,0:T(8,128)(2,1)S(1)} %add_convert_fusion.5), channel_id=1, source_target_pairs={{0,8},{1,9},{2,10},{3,11},{4,12},{5,13},{6,14},{7,15},{8,0},{9,1},... | collective-permute-start | bytes 393224 | tf_op jit(solution)/shard_map/ppermute | solution.py:799
  119.0 22.6 %collective-permute-start.17 = (bf16[64,1024]{1,0:T(8,128)(2,1)S(1)}, bf16[64,1024]{1,0:T(8,128)(2,1)S(1)}, u32[]{:S(2)}, u32[]{:S(2)}) collective-permute-start(bf16[64,1024]{1,0:T(8,128)(2,1)S(1)} %add_convert_fusion.5), channel_id=1, source_target_pairs={{0,16},{1,17},{2,18},{3,19},{4,20},{5,21},{6,22},{7,23},{8,24},{9,... | collective-permute-start | bytes 393224 | tf_op jit(solution)/shard_map/ppermute | solution.py:799
  122.4 19.2 %collective-permute-start.18 = (bf16[64,1024]{1,0:T(8,128)(2,1)S(1)}, bf16[64,1024]{1,0:T(8,128)(2,1)S(1)}, u32[]{:S(2)}, u32[]{:S(2)}) collective-permute-start(bf16[64,1024]{1,0:T(8,128)(2,1)S(1)} %add_convert_fusion.5), channel_id=1, source_target_pairs={{0,24},{1,25},{2,26},{3,27},{4,28},{5,29},{6,30},{7,31},{8,16},{9,... | collective-permute-start | bytes 393224 | tf_op jit(solution)/shard_map/ppermute | solution.py:799
  122.8 18.9 %collective-permute-start.19 = (bf16[384,512]{1,0:T(8,128)(2,1)}, bf16[384,512]{1,0:T(8,128)(2,1)S(1)}, u32[]{:S(2)}, u32[]{:S(2)}) collective-permute-start(bf16[384,512]{1,0:T(8,128)(2,1)} %get-tuple-element.204), channel_id=1, source_target_pairs={{0,2},{1,3},{2,0},{3,1},{4,6},{5,7},{6,4},{7,5},{8,10},{9,11},{10,... | collective-permute-start | bytes 1179656 | tf_op jit(solution)/shard_map/ppermute | solution.py:799
  124.2 18.3 %collective-permute-start.20 = (bf16[384,512]{1,0:T(8,128)(2,1)}, bf16[384,512]{1,0:T(8,128)(2,1)S(1)}, u32[]{:S(2)}, u32[]{:S(2)}) collective-permute-start(bf16[384,512]{1,0:T(8,128)(2,1)} %get-tuple-element.205), channel_id=1, source_target_pairs={{0,4},{1,5},{2,6},{3,7},{4,0},{5,1},{6,2},{7,3},{8,12},{9,13},{10,... | collective-permute-start | bytes 1179656 | tf_op jit(solution)/shard_map/ppermute | solution.py:799
  125.2 17.3 %collective-permute-start.21 = (bf16[384,512]{1,0:T(8,128)(2,1)S(1)}, bf16[384,512]{1,0:T(8,128)(2,1)S(1)}, u32[]{:S(2)}, u32[]{:S(2)}) collective-permute-start(bf16[384,512]{1,0:T(8,128)(2,1)S(1)} %get-tuple-element.206), channel_id=1, source_target_pairs={{0,6},{1,7},{2,4},{3,5},{4,2},{5,3},{6,0},{7,1},{8,14},{9,15},{10,... | collective-permute-start | bytes 1179656 | tf_op jit(solution)/shard_map/ppermute | solution.py:799
  141.6 1.4 copy-start.18
  141.6 1.4 copy-start.15
  142.5 0.9 copy-start.17
  142.5 1.7 copy-start.20
  143.4 13.8 %collective-permute-start.23 = (bf16[2,512,512]{2,1,0:T(8,128)(2,1)}, bf16[2,512,512]{2,1,0:T(8,128)(2,1)S(1)}, u32[]{:S(2)}, u32[]{:S(2)}) collective-permute-start(bf16[2,512,512]{2,1,0:T(8,128)(2,1)} %get-tuple-element.220), channel_id=1, source_target_pairs={{0,1},{1,0},{2,3},{3,2},{4,5},{5,4},{6,7},{7,6},{8,9},{9,8},{10,11... | collective-permute-start | bytes 3145736 | tf_op jit(solution)/shard_map/ppermute | solution.py:762
  143.4 13.7 %collective-permute-start.24 = (bf16[256,1024]{1,0:T(8,128)(2,1)S(1)}, bf16[256,1024]{1,0:T(8,128)(2,1)S(1)}, u32[]{:S(2)}, u32[]{:S(2)}) collective-permute-start(bf16[256,1024]{1,0:T(8,128)(2,1)S(1)} %maximum_select_fusion.1), channel_id=1, source_target_pairs={{0,4},{1,3},{2,6},{3,1},{4,0},{5,7},{6,2},{7,5},{8,12},{9,11},{10,... | collective-permute-start | bytes 1572872 | tf_op jit(solution)/shard_map/ppermute | solution.py:799
  144.2 4.1 %collective-permute-start.22 = (f32[2,512]{1,0:T(2,128)S(1)}, f32[2,512]{1,0:T(2,128)S(1)}, u32[]{:S(2)}, u32[]{:S(2)}) collective-permute-start(f32[2,512]{1,0:T(2,128)S(1)} %bitcast.27), channel_id=1, source_target_pairs={{0,1},{1,0},{2,3},{3,2},{4,5},{5,4},{6,7},{7,6},{8,9},{9,8},{10,11... | collective-permute-start | bytes 12296 | tf_op jit(solution)/shard_map/ppermute | solution.py:762
  144.2 12.1 %collective-permute-start.25 = (bf16[112,512]{1,0:T(8,128)(2,1)S(1)}, bf16[112,512]{1,0:T(8,128)(2,1)S(1)}, u32[]{:S(2)}, u32[]{:S(2)}) collective-permute-start(bf16[112,512]{1,0:T(8,128)(2,1)S(1)} %get-tuple-element.222), channel_id=1, source_target_pairs={{0,8},{1,9},{2,10},{3,11},{4,12},{5,13},{6,14},{7,15},{8,0},{9,1},... | collective-permute-start | bytes 344072 | tf_op jit(solution)/shard_map/ppermute | solution.py:799
  144.6 12.6 %collective-permute-start.26 = (bf16[112,512]{1,0:T(8,128)(2,1)S(1)}, bf16[112,512]{1,0:T(8,128)(2,1)S(1)}, u32[]{:S(2)}, u32[]{:S(2)}) collective-permute-start(bf16[112,512]{1,0:T(8,128)(2,1)S(1)} %get-tuple-element.223), channel_id=1, source_target_pairs={{0,16},{1,17},{2,18},{3,19},{4,20},{5,21},{6,22},{7,23},{8,24},{9,... | collective-permute-start | bytes 344072 | tf_op jit(solution)/shard_map/ppermute | solution.py:799
  148.2 8.9 %collective-permute-start.27 = (bf16[112,512]{1,0:T(8,128)(2,1)S(1)}, bf16[112,512]{1,0:T(8,128)(2,1)S(1)}, u32[]{:S(2)}, u32[]{:S(2)}) collective-permute-start(bf16[112,512]{1,0:T(8,128)(2,1)S(1)} %get-tuple-element.224), channel_id=1, source_target_pairs={{0,24},{1,25},{2,26},{3,27},{4,28},{5,29},{6,30},{7,31},{8,16},{9,... | collective-permute-start | bytes 344072 | tf_op jit(solution)/shard_map/ppermute | solution.py:799
  158.3 7.9 %collective-permute-start.28 = (bf16[2,512,512]{2,1,0:T(8,128)(2,1)}, bf16[2,512,512]{2,1,0:T(8,128)(2,1)}, u32[]{:S(2)}, u32[]{:S(2)}) collective-permute-start(bf16[2,512,512]{2,1,0:T(8,128)(2,1)} %block_output.2), channel_id=1, source_target_pairs={{0,1},{1,0},{2,3},{3,2},{4,5},{5,4},{6,7},{7,6},{8,9},{9,8},{10,11... | collective-permute-start | bytes 3145736 | tf_op jit(solution)/shard_map/ppermute | solution.py:762
  158.3 5.3 %copy-start.21 = (bf16[4,512,512]{2,1,0:T(8,128)(2,1)S(1)}, bf16[4,512,512]{2,1,0:T(8,128)(2,1)}, u32[]{:S(2)}) copy-start(bf16[4,512,512]{2,1,0:T(8,128)(2,1)} %get-tuple-element.233) | copy-start | bytes 6291460
  158.8 7.5 %copy-start.4 = (bf16[512,1024]{1,0:T(8,128)(2,1)}, bf16[512,1024]{1,0:T(8,128)(2,1)S(1)}, u32[]{:S(2)}) copy-start(bf16[512,1024]{1,0:T(8,128)(2,1)S(1)} %maximum_select_fusion.refs_0_) | copy-start | bytes 3145732
  158.8 14.9 %collective-permute-start.30 = (bf16[512,1024]{1,0:T(8,128)(2,1)S(1)}, bf16[512,1024]{1,0:T(8,128)(2,1)S(1)}, u32[]{:S(2)}, u32[]{:S(2)}) collective-permute-start(bf16[512,1024]{1,0:T(8,128)(2,1)S(1)} %maximum_select_fusion.refs_0_), channel_id=1, source_target_pairs={{0,2},{1,5},{2,0},{3,7},{4,6},{5,1},{6,4},{7,3},{8,10},{9,13},{10,... | collective-permute-start | bytes 3145736 | tf_op jit(solution)/shard_map/ppermute | solution.py:799
  160.3 7.4 %collective-permute-start.31 = (bf16[96,512]{1,0:T(8,128)(2,1)S(1)}, bf16[96,512]{1,0:T(8,128)(2,1)S(1)}, u32[]{:S(2)}, u32[]{:S(2)}) collective-permute-start(bf16[96,512]{1,0:T(8,128)(2,1)S(1)} %add_convert_fusion.9), channel_id=1, source_target_pairs={{0,8},{1,9},{2,10},{3,11},{4,12},{5,13},{6,14},{7,15},{8,0},{9,1},... | collective-permute-start | bytes 294920 | tf_op jit(solution)/shard_map/ppermute | solution.py:799
  162.4 10.0 %collective-permute-start.32 = (bf16[96,512]{1,0:T(8,128)(2,1)S(1)}, bf16[96,512]{1,0:T(8,128)(2,1)S(1)}, u32[]{:S(2)}, u32[]{:S(2)}) collective-permute-start(bf16[96,512]{1,0:T(8,128)(2,1)S(1)} %add_convert_fusion.9), channel_id=1, source_target_pairs={{0,16},{1,17},{2,18},{3,19},{4,20},{5,21},{6,22},{7,23},{8,24},{9,... | collective-permute-start | bytes 294920 | tf_op jit(solution)/shard_map/ppermute | solution.py:799
  163.5 1.3 collective-permute-start.29
  163.8 3.9 %copy-start.22 = (bf16[4,512,512]{2,1,0:T(8,128)(2,1)}, bf16[4,512,512]{2,1,0:T(8,128)(2,1)S(1)}, u32[]{:S(2)}) copy-start(bf16[4,512,512]{2,1,0:T(8,128)(2,1)S(1)} %constant_dynamic-update-slice_fusion.1) | copy-start | bytes 6291460
  164.7 7.7 %collective-permute-start.33 = (bf16[96,512]{1,0:T(8,128)(2,1)S(1)}, bf16[96,512]{1,0:T(8,128)(2,1)S(1)}, u32[]{:S(2)}, u32[]{:S(2)}) collective-permute-start(bf16[96,512]{1,0:T(8,128)(2,1)S(1)} %add_convert_fusion.9), channel_id=1, source_target_pairs={{0,24},{1,25},{2,26},{3,27},{4,28},{5,29},{6,30},{7,31},{8,16},{9,... | collective-permute-start | bytes 294920 | tf_op jit(solution)/shard_map/ppermute | solution.py:799
  167.7 13.9 %copy-start = (bf16[4,512,512]{2,1,0:T(8,128)(2,1)}, bf16[4,512,512]{2,1,0:T(8,128)(2,1)S(1)}, u32[]{:S(2)}) copy-start(bf16[4,512,512]{2,1,0:T(8,128)(2,1)S(1)} %constant_dynamic-update-slice_fusion.refs_0_) | copy-start | bytes 6291460
  173.7 4.5 %copy-start.9 = (bf16[512,1024]{1,0:T(8,128)(2,1)}, bf16[512,1024]{1,0:T(8,128)(2,1)S(1)}, u32[]{:S(2)}) copy-start(bf16[512,1024]{1,0:T(8,128)(2,1)S(1)} %collective-permute-done.30.refs_1_) | copy-start | bytes 3145732
  174.0 14.7 %copy-start.5 = (bf16[400,512]{1,0:T(8,128)(2,1)}, bf16[400,512]{1,0:T(8,128)(2,1)S(1)}, u32[]{:S(2)}) copy-start(bf16[400,512]{1,0:T(8,128)(2,1)S(1)} %pad_maximum_fusion.refs_0_) | copy-start | bytes 1228804
  174.0 14.6 %collective-permute-start.34 = (bf16[400,512]{1,0:T(8,128)(2,1)S(1)}, bf16[400,512]{1,0:T(8,128)(2,1)S(1)}, u32[]{:S(2)}, u32[]{:S(2)}) collective-permute-start(bf16[400,512]{1,0:T(8,128)(2,1)S(1)} %pad_maximum_fusion.refs_0_), channel_id=1, source_target_pairs={{0,2},{1,3},{2,0},{3,1},{4,6},{5,7},{6,4},{7,5},{8,10},{9,11},{10,... | collective-permute-start | bytes 1228808 | tf_op jit(solution)/shard_map/ppermute | solution.py:799
  175.4 19.6 %collective-permute-start.35 = (bf16[400,512]{1,0:T(8,128)(2,1)S(1)}, bf16[400,512]{1,0:T(8,128)(2,1)}, u32[]{:S(2)}, u32[]{:S(2)}) collective-permute-start(bf16[400,512]{1,0:T(8,128)(2,1)S(1)} %pad_maximum_fusion.refs_0_), channel_id=1, source_target_pairs={{0,4},{1,5},{2,6},{3,7},{4,0},{5,1},{6,2},{7,3},{8,12},{9,13},{10,... | collective-permute-start | bytes 1228808 | tf_op jit(solution)/shard_map/ppermute | solution.py:799
  176.3 18.7 %collective-permute-start.36 = (bf16[400,512]{1,0:T(8,128)(2,1)S(1)}, bf16[400,512]{1,0:T(8,128)(2,1)}, u32[]{:S(2)}, u32[]{:S(2)}) collective-permute-start(bf16[400,512]{1,0:T(8,128)(2,1)S(1)} %pad_maximum_fusion.refs_0_), channel_id=1, source_target_pairs={{0,6},{1,7},{2,4},{3,5},{4,2},{5,3},{6,0},{7,1},{8,14},{9,15},{10,... | collective-permute-start | bytes 1228808 | tf_op jit(solution)/shard_map/ppermute | solution.py:799
  188.6 6.4 %copy-start.14 = (bf16[400,512]{1,0:T(8,128)(2,1)}, bf16[400,512]{1,0:T(8,128)(2,1)S(1)}, u32[]{:S(2)}) copy-start(bf16[400,512]{1,0:T(8,128)(2,1)S(1)} %collective-permute-done.34.refs_1_) | copy-start | bytes 1228804
  (2 other events, 1.3 us)
